TPU v7x, 256 devices: a whole 4x4x8 slice. The times are simulated.
256 devices in a mesh: blk: 64 (over z, x, y_hi), hid: 4 (over y_lo, core).
Axes of the slice: x: 4, y: 4 (y_hi: 2, y_lo: 2; y = y_hi * 2 + y_lo), z: 8, core: 2. Of those that a mesh axis runs over, the one named last changes fastest.
Arguments:
- inputs: bfloat16 [4096, 8192], P(None, 'blk'), may hold values from -6 to 6
- targets: bfloat16 [4096, 8192], P(None, 'blk'), may hold values from -6 to 6
- row_order: int32 [4096], replicated, may hold values from 0 to 4095, each once
- mix_order: int32 [128], replicated, may hold values from 0 to 127, each once
- first_factor: bfloat16 [64, 128, 128], P('blk'), may hold values from -0.5 to 0.5
- up_factor: bfloat16 [64, 448, 128], P('blk', 'hid'), may hold values from -0.5 to 0.5
- down_factor: bfloat16 [64, 448, 128], P('blk', 'hid'), may hold values from -0.25 to 0.25
- last_factor: bfloat16 [64, 128, 128], P('blk'), may hold values from -0.5 to 0.5
Outputs:
- grad_first: float32 [64, 128, 128], P('blk')
- grad_up: float32 [64, 448, 128], P('blk', 'hid')
- grad_down: float32 [64, 448, 128], P('blk', 'hid')
- grad_last: float32 [64, 128, 128], P('blk')
Inputs may be any that keep to these rules, and one draw needn't show every extreme that they name: `row_order`: a permutation of the 4096 stored rows. `mix_order`: a permutation of the 128 features of a group.
All inputs are finite; a program needn't handle non-finite values.
Results may differ from a plain program's by a relative error of at most 0.018.
Values may be sent and summed in bfloat16 or wider, within the bound.
No kernel may reach another device: no remote copies, remote signals or barrier semaphores. Data moves between devices by JAX's collectives and lax.ppermute only.
A program may use at most 64 MiB of HBM per device.

v0:
```python
import math

import jax
import jax.numpy as jnp
from jax import lax
from jax.sharding import PartitionSpec as P

BS = 128
NB = 64
G = 2


def gelu_parts(preact):
    cdf = 0.5 * (1.0 + jax.scipy.special.erf(preact * (1.0 / math.sqrt(2.0))))
    dens = jnp.exp(-0.5 * preact * preact) * (1.0 / math.sqrt(2.0 * math.pi))
    return (preact * cdf, cdf + preact * dens)


def local(inputs, targets, row_order, mix_order, first_factor, up_factor, down_factor, last_factor):
    token_count = inputs.shape[0]
    blocks_here = first_factor.shape[0]
    loss_scale = 1.0 / math.sqrt(token_count)
    blocked = inputs.reshape(token_count, blocks_here, BS)
    feature_ids = lax.broadcasted_iota(jnp.int32, (BS, BS), 0)
    one_hot = (mix_order[None, :] == feature_ids).astype(jnp.float32)
    up_mixed = jnp.einsum(
        "mhi,ji->mhj", up_factor.astype(jnp.float32), one_hot, precision=lax.Precision.HIGHEST
    ).astype(jnp.bfloat16)
    first_out = jnp.einsum(
        "tkb,kbc->tkc", blocked, first_factor, preferred_element_type=jnp.float32
    ).astype(jnp.bfloat16)
    outgoing = first_out.reshape(token_count, blocks_here, NB, G).transpose(0, 2, 1, 3)
    piece = lax.all_to_all(outgoing, "blk", split_axis=1, concat_axis=2, tiled=True)
    grouped = piece.reshape(piece.shape[0], blocks_here, BS)
    preact = jnp.einsum("tmj,mhj->tmh", grouped, up_mixed, preferred_element_type=jnp.float32)
    hidden = gelu_parts(preact)[0].astype(jnp.bfloat16)
    partial_value = jnp.einsum(
        "tmh,mhc->tmc", hidden, down_factor, preferred_element_type=jnp.float32
    )
    partial_value, grouped, preact = (partial_value, grouped, preact)
    shared = lax.psum(partial_value.astype(jnp.bfloat16), "hid")
    arriving = lax.all_to_all(
        shared.reshape(token_count, blocks_here, NB, G),
        "blk",
        split_axis=2,
        concat_axis=1,
        tiled=True,
    )
    returned = arriving.transpose(0, 2, 1, 3).reshape(token_count, blocks_here, BS)
    student = jnp.einsum("tkb,kbc->tkc", returned, last_factor, preferred_element_type=jnp.float32)
    teacher = jnp.take(targets, row_order, axis=0).reshape(token_count, blocks_here, BS)
    err_grad = ((student - teacher.astype(jnp.float32)) * loss_scale).astype(jnp.bfloat16)
    grad_last = jnp.einsum("tkb,tkc->kbc", returned, err_grad, preferred_element_type=jnp.float32)
    grad_returned = jnp.einsum(
        "tkc,kbc->tkb", err_grad, last_factor, preferred_element_type=jnp.float32
    ).astype(jnp.bfloat16)
    grad_arrived = lax.all_to_all(
        grad_returned.reshape(token_count, blocks_here, NB, G),
        "blk",
        split_axis=2,
        concat_axis=1,
        tiled=True,
    )
    grad_summed = grad_arrived.transpose(0, 2, 1, 3).reshape(token_count, blocks_here, BS)
    hidden_full, slope = gelu_parts(preact)
    hidden = hidden_full.astype(jnp.bfloat16)
    grad_down = jnp.einsum("tmh,tmc->mhc", hidden, grad_summed, preferred_element_type=jnp.float32)
    grad_hidden = jnp.einsum(
        "tmc,mhc->tmh", grad_summed, down_factor, preferred_element_type=jnp.float32
    )
    grad_preact = (grad_hidden * slope).astype(jnp.bfloat16)
    grad_plain = jnp.einsum(
        "tmh,tmj->mhj", grad_preact, grouped, preferred_element_type=jnp.float32
    )
    grad_up = jnp.einsum("mhj,ji->mhi", grad_plain, one_hot, precision=lax.Precision.HIGHEST)
    grad_partial = jnp.einsum(
        "tmh,mhj->tmj", grad_preact, up_mixed, preferred_element_type=jnp.float32
    )
    grad_shared = lax.psum(grad_partial.astype(jnp.bfloat16), "hid")
    grad_landed = lax.all_to_all(
        grad_shared.reshape(token_count, blocks_here, NB, G),
        "blk",
        split_axis=2,
        concat_axis=1,
        tiled=True,
    )
    grad_first_out = grad_landed.transpose(0, 2, 1, 3).reshape(token_count, blocks_here, BS)
    grad_first = jnp.einsum(
        "tkb,tkc->kbc", blocked, grad_first_out, preferred_element_type=jnp.float32
    )
    return (grad_first, grad_up, grad_down, grad_last)


def solution(mesh):
    placed = (
        P(None, "blk"),
        P(None, "blk"),
        P(),
        P(),
        P("blk", None, None),
        P("blk", "hid", None),
        P("blk", "hid", None),
        P("blk", None, None),
    )
    return jax.shard_map(
        local,
        mesh=mesh,
        in_specs=placed,
        out_specs=(
            P("blk", None, None),
            P("blk", "hid", None),
            P("blk", "hid", None),
            P("blk", None, None),
        ),
        check_vma=False,
    )
```

profile of v0, /device:TPU:1, one launch (start us, length us, event | category | flops | bytes accessed | tf_op | source)
XLA Modules:
  0.0 293.5 jit_solution(10014217720580849058)
XLA Ops:
  9.6 1.5 transpose_reshape.3
  11.1 15.1 %all-to-all-start = ((bf16[4096,64,1,2]{0,3,2,1:T(2,128)(2,1)}), bf16[4096,64,1,2]{0,3,2,1:T(2,128)(2,1)S(1)}, u32[]{:S(2)}, u32[]{:S(2)}) async-start(bf16[4096,64,1,2]{0,3,2,1:T(2,128)(2,1)} %bitcast.4), calls=%async_computation | async-start | bytes 2097152 | tf_op jit(solution)/shard_map/all_to_all | solution.py:33
  26.5 27.2 %all-to-all-done = bf16[4096,64,1,2]{0,3,2,1:T(2,128)(2,1)S(1)} async-done(((bf16[4096,64,1,2]{0,3,2,1:T(2,128)(2,1)}), bf16[4096,64,1,2]{0,3,2,1:T(2,128)(2,1)S(1)}, u32[]{:S(2)}, u32[]{:S(2)}) %all-to-all-start) | async-done | bytes 1048608 | tf_op jit(solution)/shard_map/all_to_all | solution.py:33
  56.5 1.5 fusion.6
  58.0 2.5 reshape.151
  60.5 44.7 %all-reduce.3.cloned.1.call-done = bf16[4096,1,64,2]{0,3,1,2:T(2,128)(2,1)} async-done(((bf16[4096,1,64,2]{0,3,1,2:T(2,128)(2,1)}), bf16[4096,1,64,2]{0,3,1,2:T(2,128)(2,1)}) %all-reduce.3.cloned.1.call-update) | async-done | bytes 1048592 | tf_op jit(solution)/shard_map/psum | solution.py:41
  105.2 12.6 %all-to-all-start.1 = ((bf16[4096,1,64,2]{0,3,1,2:T(2,128)(2,1)}), bf16[4096,1,64,2]{0,3,1,2:T(2,128)(2,1)}, u32[]{:S(2)}, u32[]{:S(2)}) async-start(bf16[4096,1,64,2]{0,3,1,2:T(2,128)(2,1)} %all-reduce.3.cloned.1.call-done), calls=%async_computation.1 | async-start | bytes 2097152 | tf_op jit(solution)/shard_map/all_to_all | solution.py:42
  117.8 14.9 %gather_fusion = bf16[4096,128]{1,0:T(8,128)(2,1)} fusion(bf16[4096,128]{1,0:T(8,128)(2,1)S(1)} %copy-done.1, s32[4096]{0:T(1024)S(1)} %fusion.24), kind=kCustom, calls=%fused_computation | custom fusion | bytes 2113536 | tf_op jit(solution)/shard_map/jit(_take)/gather | solution.py:51
  132.7 12.6 %all-to-all-done.1 = bf16[4096,1,64,2]{0,3,1,2:T(2,128)(2,1)} async-done(((bf16[4096,1,64,2]{0,3,1,2:T(2,128)(2,1)}), bf16[4096,1,64,2]{0,3,1,2:T(2,128)(2,1)}, u32[]{:S(2)}, u32[]{:S(2)}) %all-to-all-start.1) | async-done | bytes 1048608 | tf_op jit(solution)/shard_map/all_to_all | solution.py:42
  145.3 1.5 reshape.152
  146.8 2.1 fusion.9
  149.9 1.4 fusion.7
  151.3 2.5 reshape.155
  153.8 35.1 %all_to_all.16 = bf16[4096,1,64,2]{0,3,1,2:T(2,128)(2,1)} all-to-all(bf16[4096,1,64,2]{0,3,1,2:T(2,128)(2,1)} %bitcast.126), channel_id=1, replica_groups=mesh['blk'=64,'hid'=4] {'blk'}, dimensions={2} | all-to-all | bytes 2097152 | tf_op jit(solution)/shard_map/all_to_all | solution.py:57
  188.9 2.2 reshape.156
  191.1 2.7 fusion.10
  194.8 1.4 fusion.8
  196.2 2.5 reshape.158
  198.8 45.1 %all-reduce.5.cloned.1.call-done = bf16[4096,1,64,2]{0,3,1,2:T(2,128)(2,1)} async-done(((bf16[4096,1,64,2]{0,3,1,2:T(2,128)(2,1)}), bf16[4096,1,64,2]{0,3,1,2:T(2,128)(2,1)}) %all-reduce.5.cloned.1.call-update) | async-done | bytes 1048592 | tf_op jit(solution)/shard_map/psum | solution.py:79
  243.8 12.6 %all-to-all-start.3 = ((bf16[4096,1,64,2]{0,3,1,2:T(2,128)(2,1)}), bf16[4096,1,64,2]{0,3,1,2:T(2,128)(2,1)}, u32[]{:S(2)}, u32[]{:S(2)}) async-start(bf16[4096,1,64,2]{0,3,1,2:T(2,128)(2,1)} %all-reduce.5.cloned.1.call-done), calls=%async_computation.3 | async-start | bytes 2097152 | tf_op jit(solution)/shard_map/all_to_all | solution.py:80
  256.4 2.4 convolution_bitcast_fusion.3
  258.8 1.6 fusion.25
  262.3 21.6 %all-to-all-done.3 = bf16[4096,1,64,2]{0,3,1,2:T(2,128)(2,1)} async-done(((bf16[4096,1,64,2]{0,3,1,2:T(2,128)(2,1)}), bf16[4096,1,64,2]{0,3,1,2:T(2,128)(2,1)}, u32[]{:S(2)}, u32[]{:S(2)}) %all-to-all-start.3) | async-done | bytes 1048608 | tf_op jit(solution)/shard_map/all_to_all | solution.py:80
  284.0 1.5 reshape.159
  (41 shorter events, 10.5 us)
Async XLA Ops:
  7.2 1.2 copy-start
  9.6 16.7 %copy-start.11 = (bf16[1,112,128]{2,1,0:T(8,128)(2,1)S(1)}, bf16[1,112,128]{2,1,0:T(8,128)(2,1)}, u32[]{:S(2)}) copy-start(bf16[1,112,128]{2,1,0:T(8,128)(2,1)} %param.13) | copy-start | bytes 86020
  9.6 16.7 %copy-start.12 = (s32[128]{0:T(128)S(1)}, s32[128]{0:T(128)}, u32[]{:S(2)}) copy-start(s32[128]{0:T(128)} %param.11) | copy-start | bytes 1540
  11.1 42.5 %all-to-all-start = ((bf16[4096,64,1,2]{0,3,2,1:T(2,128)(2,1)}), bf16[4096,64,1,2]{0,3,2,1:T(2,128)(2,1)S(1)}, u32[]{:S(2)}, u32[]{:S(2)}) async-start(bf16[4096,64,1,2]{0,3,2,1:T(2,128)(2,1)} %bitcast.4), calls=%async_computation | async-start | bytes 2097152 | tf_op jit(solution)/shard_map/all_to_all | solution.py:33
  26.3 78.9 %all-reduce.3.cloned.1.call-start = ((), (), s32[]{:S(2)}) async-start(), calls=%async_computation.4 | async-start | bytes 2097152 | tf_op jit(solution)/shard_map/psum | solution.py:41
  54.5 1.3 copy-start.4
  55.7 0.7 copy-start.10
  56.5 1.5 copy-start.2
  60.5 57.3 %copy-start.8 = (s32[4096]{0:T(1024)S(1)}, s32[4096]{0:T(1024)}, u32[]{:S(2)}) copy-start(s32[4096]{0:T(1024)} %param.10) | copy-start | bytes 49156
  60.5 57.3 %copy-start.1 = (bf16[4096,128]{1,0:T(8,128)(2,1)S(1)}, bf16[4096,128]{1,0:T(8,128)(2,1)}, u32[]{:S(2)}) copy-start(bf16[4096,128]{1,0:T(8,128)(2,1)} %param.9) | copy-start | bytes 3145732
  105.2 40.2 %all-to-all-start.1 = ((bf16[4096,1,64,2]{0,3,1,2:T(2,128)(2,1)}), bf16[4096,1,64,2]{0,3,1,2:T(2,128)(2,1)}, u32[]{:S(2)}, u32[]{:S(2)}) async-start(bf16[4096,1,64,2]{0,3,1,2:T(2,128)(2,1)} %all-reduce.3.cloned.1.call-done), calls=%async_computation.1 | async-start | bytes 2097152 | tf_op jit(solution)/shard_map/all_to_all | solution.py:42
  117.7 126.1 %all-reduce.5.cloned.1.call-start = ((), (), s32[]{:S(2)}) async-start(), calls=%async_computation.5 | async-start | bytes 2097152 | tf_op jit(solution)/shard_map/psum | solution.py:79
  132.7 14.1 %copy-start.9 = (bf16[1,128,128]{2,1,0:T(8,128)(2,1)S(1)}, bf16[1,128,128]{2,1,0:T(8,128)(2,1)}, u32[]{:S(2)}) copy-start(bf16[1,128,128]{2,1,0:T(8,128)(2,1)} %param.15) | copy-start | bytes 98308
  148.9 1.0 copy-start.5
  193.8 0.9 copy-start.7
  243.8 40.2 %all-to-all-start.3 = ((bf16[4096,1,64,2]{0,3,1,2:T(2,128)(2,1)}), bf16[4096,1,64,2]{0,3,1,2:T(2,128)(2,1)}, u32[]{:S(2)}, u32[]{:S(2)}) async-start(bf16[4096,1,64,2]{0,3,1,2:T(2,128)(2,1)} %all-reduce.5.cloned.1.call-done), calls=%async_computation.3 | async-start | bytes 2097152 | tf_op jit(solution)/shard_map/all_to_all | solution.py:80
  256.4 4.9 %copy-start.3 = (bf16[4096,112]{0,1:T(8,128)(2,1)S(1)}, bf16[4096,112]{0,1:T(8,128)(2,1)}, u32[]{:S(2)}) copy-start(bf16[4096,112]{0,1:T(8,128)(2,1)} %copy-done.2) | copy-start | bytes 2752516
  256.4 4.9 %copy-start.6 = (bf16[4096,128]{0,1:T(8,128)(2,1)S(1)}, bf16[4096,128]{0,1:T(8,128)(2,1)}, u32[]{:S(2)}) copy-start(bf16[4096,128]{0,1:T(8,128)(2,1)} %reshape.156) | copy-start | bytes 3145732
Sparse Core Ops, SparseCore 0:
  60.6 44.4 all-reduce.2
  198.9 44.9 all-reduce.4
where the time goes:
time: 296 us; the launch traced here: 293 us
  waiting for transfers between devices  151 us (51%)
  starting transfers between devices  40.3 us (14%)
  local copies, waits for them, and re-layouts  35.1 us (12%)
  blocking collectives  35.1 us (12%)
  matrix products  17.2 us (6%)
  between operations  14.3 us (5%)
    psum x1, waiting for transfers between devices, local(): grad_shared = lax.psum(grad_partial.astype(jnp.bfloat16), 'hid')  45.1 us
    psum x1, waiting for transfers between devices, local(): shared = lax.psum(partial_value.astype(jnp.bfloat16), 'hid')  44.7 us
    all_to_all x1, blocking collectives, local(): lax.all_to_all(grad_returned.reshape(token_count, blocks_here, NB, G), 'b...  35.1 us
    all_to_all x1, waiting for transfers between devices, local(): lax.all_to_all(outgoing, 'blk', split_axis=1, concat_axis=2, tiled=True)  27.2 us
    all_to_all x1, waiting for transfers between devices, local(): lax.all_to_all(grad_shared.reshape(token_count, blocks_here, NB, G), 'blk...  21.6 us
    all_to_all x1, starting transfers between devices, local(): lax.all_to_all(outgoing, 'blk', split_axis=1, concat_axis=2, tiled=True)  15.1 us
    gather x1, local copies, waits for them, and re-layouts, local(): jnp.take(targets, row_order, axis=0).reshape(token_count, blocks_here, BS)  14.9 us
    all_to_all x1, waiting for transfers between devices, local(): lax.all_to_all(shared.reshape(token_count, blocks_here, NB, G), 'blk', sp...  12.6 us
  transfers between devices with their start and end apart: 5, of which 5 were waited for; matrix products, arithmetic and copies ran while one was open for 7% of the time, Pallas kernels for 0%

commit v1 on v0

v1 whole, which is shorter than its diff:
```python
import math

import jax
import jax.numpy as jnp
from jax import lax
from jax.sharding import PartitionSpec as P

BS = 128
NB = 64
G = 2
N_HID = 4


def gelu_parts(preact):
    cdf = 0.5 * (1.0 + jax.scipy.special.erf(preact * (1.0 / math.sqrt(2.0))))
    dens = jnp.exp(-0.5 * preact * preact) * (1.0 / math.sqrt(2.0 * math.pi))
    return (preact * cdf, cdf + preact * dens)


def token_groups():
    return [
        [b * N_HID + (q ^ (2 * (b % 2))) for b in range(NB)] for q in range(N_HID)
    ]


def from_partner(value, m):
    return lax.ppermute(value, "hid", [(i, i ^ m) for i in range(N_HID)])


def exchange(rows):
    pieces = rows.reshape(NB, 16, rows.shape[0] * rows.shape[1] // (NB * 16))
    pieces = lax.all_to_all(
        pieces, ("blk", "hid"), 0, 0, tiled=True, axis_index_groups=token_groups()
    )
    return pieces.reshape(rows.shape)


def dot(a, b, dims):
    return lax.dot_general(a, b, (dims, ((), ())), preferred_element_type=jnp.float32)


def sum_over_hid(part):
    got = [from_partner(part, m) for m in (1, 2, 3)]
    return (part + got[0]) + (got[1] + got[2])


def local(inputs, targets, row_order, mix_order, first_factor, up_factor, down_factor, last_factor):
    tokens = inputs.shape[0]
    count = tokens // N_HID
    loss_scale = 1.0 / math.sqrt(tokens)
    quarter = lax.axis_index("hid") ^ (2 * (lax.axis_index("blk") % 2))
    start = quarter * count
    x = lax.dynamic_slice_in_dim(inputs, start, count, 0)
    rows = lax.dynamic_slice_in_dim(row_order, start, count, 0)
    first = first_factor[0]
    last = last_factor[0]
    weights = jnp.stack([up_factor[0], down_factor[0]])
    gathered = [weights] + [from_partner(weights, m) for m in (1, 2, 3)]

    first_out = dot(first, x, ((0,), (1,))).astype(jnp.bfloat16)
    grouped = exchange(first_out)

    up = jnp.concatenate([g[0] for g in gathered])
    down = jnp.concatenate([g[1] for g in gathered])
    feature_ids = lax.broadcasted_iota(jnp.int32, (BS, BS), 0)
    one_hot = mix_order[None, :] == feature_ids
    up_mixed = dot(up, one_hot.astype(jnp.bfloat16), ((1,), (1,))).astype(jnp.bfloat16)
    teacher = jnp.take(targets, rows, axis=0)

    preact = dot(up_mixed, grouped, ((1,), (0,)))
    hidden_full, slope = gelu_parts(preact)
    hidden = hidden_full.astype(jnp.bfloat16)
    summed = dot(down, hidden, ((0,), (0,))).astype(jnp.bfloat16)
    returned = exchange(summed)

    student = dot(returned, last, ((0,), (0,)))
    err_grad = ((student - teacher.astype(jnp.float32)) * loss_scale).astype(jnp.bfloat16)
    grad_returned = dot(last, err_grad, ((1,), (1,))).astype(jnp.bfloat16)
    grad_summed = exchange(grad_returned)
    grad_last = dot(returned, err_grad, ((1,), (0,)))

    grad_hidden = dot(down, grad_summed, ((1,), (0,)))
    grad_preact = (grad_hidden * slope).astype(jnp.bfloat16)
    grad_grouped = dot(up_mixed, grad_preact, ((0,), (0,))).astype(jnp.bfloat16)
    grad_first_out = exchange(grad_grouped)

    grad_up = dot(grad_preact, grouped, ((1,), (1,)))
    grad_down = dot(hidden, grad_summed, ((1,), (1,)))
    both = jnp.stack([grad_up.reshape(N_HID, -1, BS), grad_down.reshape(N_HID, -1, BS)], 1)
    got = [both[0]] + [from_partner(both[m], m) for m in (1, 2, 3)]
    both = (got[0] + got[1]) + (got[2] + got[3])
    grad_up = jnp.dot(both[0], one_hot.astype(jnp.float32), precision=lax.Precision.HIGHEST)
    grad_down = both[1]
    grad_last = sum_over_hid(grad_last)

    grad_first = sum_over_hid(dot(x, grad_first_out, ((0,), (1,))))
    return (grad_first[None], grad_up[None], grad_down[None], grad_last[None])


def solution(mesh):
    placed = (
        P(None, "blk"),
        P(None, "blk"),
        P(),
        P(),
        P("blk", None, None),
        P("blk", "hid", None),
        P("blk", "hid", None),
        P("blk", None, None),
    )
    return jax.shard_map(
        local,
        mesh=mesh,
        in_specs=placed,
        out_specs=(
            P("blk", None, None),
            P("blk", "hid", None),
            P("blk", "hid", None),
            P("blk", None, None),
        ),
        check_vma=False,
    )
```

time: 296 us -> 109 us (0.37)
  waiting for transfers between devices: 151 us -> 29.7 us
  blocking collectives: 35.1 us -> 0 us
  local copies, waits for them, and re-layouts: 35.1 us -> 14.1 us
  between operations: 14.3 us -> 0.91 us
  starting transfers between devices: 40.3 us -> 46.8 us
  matrix products: 17.2 us -> 13 us
  other arithmetic: 0.35 us -> 3.65 us
    psum x2 -> x0, waiting for transfers between devices: 89.7 us -> none  [the longest x1 45.1 us: local(): grad_shared = lax.psum(grad_partial.astype(jnp.bfloat16), 'hid')]
    all_to_all x3 -> x4, waiting for transfers between devices: 61.4 us -> 23.8 us  [exchange(): lax.all_to_all(pieces, ('blk', 'hid'), 0, 0, tiled=True, axis_index_group...]
    all_to_all x1 -> x0, blocking collectives: 35.1 us -> none  [local(): lax.all_to_all(grad_returned.reshape(token_count, blocks_here, NB, G), 'b...]
    ppermute x0 -> x12, starting transfers between devices: none -> 15.7 us  [from_partner(): return lax.ppermute(value, 'hid', [(i, i ^ m) for i in range(N_HID)])]
    gather x1, local copies, waits for them, and re-layouts: 14.9 us -> 4.29 us  [local(): teacher = jnp.take(targets, rows, axis=0)]
    all_to_all x3 -> x4, starting transfers between devices: 40.2 us -> 31.1 us  [exchange(): lax.all_to_all(pieces, ('blk', 'hid'), 0, 0, tiled=True, axis_index_group...]
    another operation x5 -> x1, local copies, waits for them, and re-layouts: 7.08 us -> 0.76 us  [local(): weights = jnp.stack([up_factor[0], down_factor[0]])]
    ppermute x0 -> x12, waiting for transfers between devices: none -> 5.85 us  [from_partner(): return lax.ppermute(value, 'hid', [(i, i ^ m) for i in range(N_HID)])]
  transfers between devices with their start and end apart: 5 -> 16, of which waited for: 5 -> 5; matrix products, arithmetic and copies ran while one was open for 7% -> 19% of each run, Pallas kernels for 0% -> 0%
where the time goes in v1:
time: 109 us; the launch traced here: 108 us
  starting transfers between devices  46.8 us (43%)
  waiting for transfers between devices  29.7 us (27%)
  local copies, waits for them, and re-layouts  14.1 us (13%)
  matrix products  13 us (12%)
  other arithmetic  3.65 us (3%)
    all_to_all x4, starting transfers between devices, exchange(): lax.all_to_all(pieces, ('blk', 'hid'), 0, 0, tiled=True, axis_index_group...  31.1 us
    all_to_all x4, waiting for transfers between devices, exchange(): lax.all_to_all(pieces, ('blk', 'hid'), 0, 0, tiled=True, axis_index_group...  23.8 us
    ppermute x12, starting transfers between devices, from_partner(): return lax.ppermute(value, 'hid', [(i, i ^ m) for i in range(N_HID)])  15.7 us
    dot_general x12, matrix products, dot(): lax.dot_general(a, b, (dims, ((), ())), preferred_element_type=jnp.float32)  12.2 us
    ppermute x12, waiting for transfers between devices, from_partner(): return lax.ppermute(value, 'hid', [(i, i ^ m) for i in range(N_HID)])  5.85 us
    gather x1, local copies, waits for them, and re-layouts, local(): teacher = jnp.take(targets, rows, axis=0)  4.29 us
    reshape x4, local copies, waits for them, and re-layouts, exchange(): pieces = rows.reshape(NB, 16, rows.shape[0] * rows.shape[1] // (NB * 16))  3.28 us
    broadcast_in_dim x2, other arithmetic, local(): return (grad_first[None], grad_up[None], grad_down[None], grad_last[None])  2.19 us
  transfers between devices with their start and end apart: 16, of which 5 were waited for; matrix products, arithmetic and copies ran while one was open for 19% of the time, Pallas kernels for 0%

profile of v1, /device:TPU:1, one launch (start us, length us, event | category | flops | bytes accessed | tf_op | source)
XLA Modules:
  0.0 108.1 jit_solution(3828105265702227831)
XLA Ops:
  2.3 2.7 %collective-permute-start.2 = (bf16[2,112,128]{2,1,0:T(8,128)(2,1)S(1)}, bf16[2,112,128]{2,1,0:T(8,128)(2,1)S(1)}, u32[]{:S(2)}, u32[]{:S(2)}) collective-permute-start(bf16[2,112,128]{2,1,0:T(8,128)(2,1)S(1)} %constant_dynamic-update-slice_fusion), channel_id=1, source_target_pairs={{0,3},{1,2},{2,1},{3,0},{4,7},{5,6},{6,5},{7,4},{8,11},{9,10},{10,... | collective-permute-start | bytes 172040 | tf_op jit(solution)/shard_map/ppermute | solution.py:27
  4.9 1.9 %collective-permute-start.1 = (bf16[2,112,128]{2,1,0:T(8,128)(2,1)S(1)}, bf16[2,112,128]{2,1,0:T(8,128)(2,1)S(1)}, u32[]{:S(2)}, u32[]{:S(2)}) collective-permute-start(bf16[2,112,128]{2,1,0:T(8,128)(2,1)S(1)} %constant_dynamic-update-slice_fusion), channel_id=1, source_target_pairs={{0,2},{1,3},{2,0},{3,1},{4,6},{5,7},{6,4},{7,5},{8,10},{9,11},{10,... | collective-permute-start | bytes 172040 | tf_op jit(solution)/shard_map/ppermute | solution.py:27
  8.8 12.5 %all-to-all-start = ((bf16[64,16,128]{2,1,0:T(8,128)(2,1)}), bf16[64,16,128]{2,1,0:T(8,128)(2,1)S(1)}, u32[]{:S(2)}, u32[]{:S(2)}) async-start(bf16[64,16,128]{2,1,0:T(8,128)(2,1)} %reshape.50), calls=%async_computation | async-start | bytes 524288 | tf_op jit(solution)/shard_map/all_to_all | solution.py:32
  23.4 10.2 %all-to-all-done = bf16[64,16,128]{2,1,0:T(8,128)(2,1)S(1)} async-done(((bf16[64,16,128]{2,1,0:T(8,128)(2,1)}), bf16[64,16,128]{2,1,0:T(8,128)(2,1)S(1)}, u32[]{:S(2)}, u32[]{:S(2)}) %all-to-all-start) | async-done | bytes 262176 | tf_op jit(solution)/shard_map/all_to_all | solution.py:32
  33.7 1.7 %multiply_convert_fusion = (bf16[448,1024]{1,0:T(8,128)(2,1)S(1)}, f32[448,1024]{1,0:T(8,128)}) fusion(bf16[448,128]{1,0:T(8,128)(2,1)S(1)} %convolution_convert_fusion.4, bf16[128,1024]{1,0:T(8,128)(2,1)S(1)} %reshape.51), kind=kOutput, calls=%fused_computation.8 | convolution fusion | flops 119734272 | bytes 3129344 | tf_op jit(solution)/shard_map/dot_general | solution.py:39
  35.4 1.2 %convolution_convert_fusion.3 = bf16[128,1024]{1,0:T(8,128)(2,1)S(1)} fusion(bf16[448,1024]{1,0:T(8,128)(2,1)S(1)} %get-tuple-element.13, bf16[112,128]{1,0:T(8,128)(2,1)} %get-tuple-element.11, bf16[112,128]{1,0:T(8,128)(2,1)} %get-tuple-element.9, bf16[112,128]{1,0:T(8,128)(2,1)} %get-tuple-element.7, bf16[112,128]{1,0:T(8,128)(2,1)} %bitcast.76), kind=kOutput, calls=%fused_computation.16 | convolution fusion | flops 118030336 | bytes 1294336 | tf_op jit(solution)/shard_map/dot_general | solution.py:39
  37.4 6.3 %all-to-all-start.1 = ((bf16[64,16,128]{2,1,0:T(8,128)(2,1)}), bf16[64,16,128]{2,1,0:T(8,128)(2,1)S(1)}, u32[]{:S(2)}, u32[]{:S(2)}) async-start(bf16[64,16,128]{2,1,0:T(8,128)(2,1)} %reshape.52), calls=%async_computation.1 | async-start | bytes 524288 | tf_op jit(solution)/shard_map/all_to_all | solution.py:32
  44.4 4.3 %gather_fusion = bf16[1024,128]{1,0:T(8,128)(2,1)} fusion(bf16[4096,128]{1,0:T(8,128)(2,1)S(1)} %copy-done.1, s32[1024]{0:T(1024)S(1)} %fusion.34), kind=kCustom, calls=%fused_computation | custom fusion | bytes 528384 | tf_op jit(solution)/shard_map/jit(_take)/gather | solution.py:68
  49.4 6.1 %all-to-all-done.1 = bf16[64,16,128]{2,1,0:T(8,128)(2,1)S(1)} async-done(((bf16[64,16,128]{2,1,0:T(8,128)(2,1)}), bf16[64,16,128]{2,1,0:T(8,128)(2,1)S(1)}, u32[]{:S(2)}, u32[]{:S(2)}) %all-to-all-start.1) | async-done | bytes 262176 | tf_op jit(solution)/shard_map/all_to_all | solution.py:32
  55.6 1.3 %fusion.7 = bf16[1024,128]{1,0:T(8,128)(2,1)S(1)} fusion(bf16[128,1024]{1,0:T(8,128)(2,1)S(1)} %reshape.53, bf16[1024,128]{1,0:T(8,128)(2,1)} %gather_fusion, pred[1024]{0:T(1024)(128)(4,1)S(1)} %compare_and_fusion, bf16[1,128,128]{2,1,0:T(8,128)(2,1)} %param.15), kind=kOutput, calls=%fused_computation.12 | convolution fusion | flops 34209792 | bytes 820224 | tf_op jit(solution)/shard_map/dot_general | solution.py:39
  57.0 1.0 fusion.9
  58.9 6.4 %all-to-all-start.2 = ((bf16[64,16,128]{2,1,0:T(8,128)(2,1)}), bf16[64,16,128]{2,1,0:T(8,128)(2,1)S(1)}, u32[]{:S(2)}, u32[]{:S(2)}) async-start(bf16[64,16,128]{2,1,0:T(8,128)(2,1)} %reshape.54), calls=%async_computation.2 | async-start | bytes 524288 | tf_op jit(solution)/shard_map/all_to_all | solution.py:32
  66.5 3.2 %collective-permute-start.10 = (f32[128,128]{1,0:T(8,128)S(1)}, f32[128,128]{1,0:T(8,128)}, u32[]{:S(2)}, u32[]{:S(2)}) collective-permute-start(f32[128,128]{1,0:T(8,128)S(1)} %fusion.40), channel_id=1, source_target_pairs={{0,2},{1,3},{2,0},{3,1},{4,6},{5,7},{6,4},{7,5},{8,10},{9,11},{10,... | collective-permute-start | bytes 196616 | tf_op jit(solution)/shard_map/ppermute | solution.py:27
  69.7 7.5 %all-to-all-done.2 = bf16[64,16,128]{2,1,0:T(8,128)(2,1)S(1)} async-done(((bf16[64,16,128]{2,1,0:T(8,128)(2,1)}), bf16[64,16,128]{2,1,0:T(8,128)(2,1)S(1)}, u32[]{:S(2)}, u32[]{:S(2)}) %all-to-all-start.2) | async-done | bytes 262176 | tf_op jit(solution)/shard_map/all_to_all | solution.py:32
  77.3 2.4 %fusion.5 = bf16[448,1024]{1,0:T(8,128)(2,1)S(1)} fusion(f32[448,1024]{1,0:T(8,128)} %get-tuple-element.14, bf16[128,1024]{1,0:T(8,128)(2,1)S(1)} %reshape.55, bf16[112,128]{1,0:T(8,128)(2,1)S(1)} %copy-done.5, bf16[112,128]{1,0:T(8,128)(2,1)} %get-tuple-element.9, bf16[112,128]{1,0:T(8,128)(2,1)} %get-tuple-element.7, bf16[112,128]{1,0:T(8,128)(2,1)S(1)} %bitcast.77), kind=kOutput, calls=%fused_computation.7 | convolution fusion | flops 122486784 | bytes 3129344 | tf_op jit(solution)/shard_map/dot_general | solution.py:39
  80.9 5.9 %all-to-all-start.3 = ((bf16[64,16,128]{2,1,0:T(8,128)(2,1)}), bf16[64,16,128]{2,1,0:T(8,128)(2,1)S(1)}, u32[]{:S(2)}, u32[]{:S(2)}) async-start(bf16[64,16,128]{2,1,0:T(8,128)(2,1)} %reshape.56), calls=%async_computation.3 | async-start | bytes 524288 | tf_op jit(solution)/shard_map/all_to_all | solution.py:32
  87.6 1.3 %convolution_bitcast_fusion = f32[4,1,112,128]{3,2,0,1:T(8,128)S(1)} fusion(bf16[4,112,1024]{2,1,0:T(8,128)(2,1)S(1)} %bitcast.74, bf16[128,1024,1]{1,0,2:T(8,128)(2,1)} %reshape.70), kind=kOutput, calls=%fused_computation.19 | convolution fusion | flops 117440512 | bytes 1409024 | tf_op jit(solution)/shard_map/dot_general | solution.py:39
  89.0 1.4 %convolution_bitcast_fusion.1 = f32[4,1,112,128]{3,2,0,1:T(8,128)S(1)} fusion(bf16[4,112,1024]{2,1,0:T(8,128)(2,1)S(1)} %bitcast.75, bf16[128,1024,1]{1,0,2:T(8,128)(2,1)} %reshape.69), kind=kOutput, calls=%fused_computation.20 | convolution fusion | flops 117440512 | bytes 1409024 | tf_op jit(solution)/shard_map/dot_general | solution.py:39
  90.5 2.6 %collective-permute-start.6 = (f32[2,112,128]{2,1,0:T(8,128)S(1)}, f32[2,112,128]{2,1,0:T(8,128)S(1)}, u32[]{:S(2)}, u32[]{:S(2)}) collective-permute-start(f32[2,112,128]{2,1,0:T(8,128)S(1)} %get-tuple-element.5), channel_id=1, source_target_pairs={{0,1},{1,0},{2,3},{3,2},{4,5},{5,4},{6,7},{7,6},{8,9},{9,8},{10,11... | collective-permute-start | bytes 344072 | tf_op jit(solution)/shard_map/ppermute | solution.py:27
  93.1 1.3 %collective-permute-start.7 = (f32[2,112,128]{2,1,0:T(8,128)S(1)}, f32[2,112,128]{2,1,0:T(8,128)S(1)}, u32[]{:S(2)}, u32[]{:S(2)}) collective-permute-start(f32[2,112,128]{2,1,0:T(8,128)S(1)} %get-tuple-element.6), channel_id=1, source_target_pairs={{0,2},{1,3},{2,0},{3,1},{4,6},{5,7},{6,4},{7,5},{8,10},{9,11},{10,... | collective-permute-start | bytes 344072 | tf_op jit(solution)/shard_map/ppermute | solution.py:27
  94.4 1.5 %add_bitcast_fusion = f32[1,128,128]{2,1,0:T(8,128)} fusion(f32[128,128]{1,0:T(8,128)} %collective-permute-done.10, f32[128,128]{1,0:T(8,128)} %collective-permute-done.11, f32[128,128]{1,0:T(8,128)S(1)} %fusion.40, f32[128,128]{1,0:T(8,128)} %collective-permute-done.9), kind=kLoop, calls=%fused_computation.50 | loop fusion | flops 49152 | bytes 327680 | tf_op jit(solution)/shard_map/broadcast_in_dim | solution.py:97
  95.9 3.4 %collective-permute-done.7 = f32[2,112,128]{2,1,0:T(8,128)S(1)} collective-permute-done((f32[2,112,128]{2,1,0:T(8,128)S(1)}, f32[2,112,128]{2,1,0:T(8,128)S(1)}, u32[]{:S(2)}, u32[]{:S(2)}) %collective-permute-start.7) | collective-permute-done | bytes 114720 | tf_op jit(solution)/shard_map/ppermute | solution.py:27
  101.0 3.2 %collective-permute-start.4 = (f32[128,128]{1,0:T(8,128)S(1)}, f32[128,128]{1,0:T(8,128)S(1)}, u32[]{:S(2)}, u32[]{:S(2)}) collective-permute-start(f32[128,128]{1,0:T(8,128)S(1)} %fusion.10), channel_id=1, source_target_pairs={{0,2},{1,3},{2,0},{3,1},{4,6},{5,7},{6,4},{7,5},{8,10},{9,11},{10,... | collective-permute-start | bytes 196616 | tf_op jit(solution)/shard_map/ppermute | solution.py:27
  105.0 2.5 %collective-permute-done.4 = f32[128,128]{1,0:T(8,128)S(1)} collective-permute-done((f32[128,128]{1,0:T(8,128)S(1)}, f32[128,128]{1,0:T(8,128)S(1)}, u32[]{:S(2)}, u32[]{:S(2)}) %collective-permute-start.4) | collective-permute-done | bytes 65568 | tf_op jit(solution)/shard_map/ppermute | solution.py:27
  (62 shorter events, 15.5 us)
Async XLA Ops:
  0.6 6.2 %copy-start = (bf16[4096,128]{1,0:T(8,128)(2,1)S(1)}, bf16[4096,128]{1,0:T(8,128)(2,1)}, u32[]{:S(2)}) copy-start(bf16[4096,128]{1,0:T(8,128)(2,1)} %param.8) | copy-start | bytes 3145732
  0.6 22.5 %copy-start.6 = (bf16[1,112,128]{2,1,0:T(8,128)(2,1)S(1)}, bf16[1,112,128]{2,1,0:T(8,128)(2,1)}, u32[]{:S(2)}) copy-start(bf16[1,112,128]{2,1,0:T(8,128)(2,1)} %param.13) | copy-start | bytes 86020
  0.7 22.5 %copy-start.7 = (s32[128]{0:T(128)S(1)}, s32[128]{0:T(128)}, u32[]{:S(2)}) copy-start(s32[128]{0:T(128)} %param.11) | copy-start | bytes 1540
  2.3 19.0 %collective-permute-start.2 = (bf16[2,112,128]{2,1,0:T(8,128)(2,1)S(1)}, bf16[2,112,128]{2,1,0:T(8,128)(2,1)S(1)}, u32[]{:S(2)}, u32[]{:S(2)}) collective-permute-start(bf16[2,112,128]{2,1,0:T(8,128)(2,1)S(1)} %constant_dynamic-update-slice_fusion), channel_id=1, source_target_pairs={{0,3},{1,2},{2,1},{3,0},{4,7},{5,6},{6,5},{7,4},{8,11},{9,10},{10,... | collective-permute-start | bytes 172040 | tf_op jit(solution)/shard_map/ppermute | solution.py:27
  4.9 17.0 %collective-permute-start.1 = (bf16[2,112,128]{2,1,0:T(8,128)(2,1)S(1)}, bf16[2,112,128]{2,1,0:T(8,128)(2,1)S(1)}, u32[]{:S(2)}, u32[]{:S(2)}) collective-permute-start(bf16[2,112,128]{2,1,0:T(8,128)(2,1)S(1)} %constant_dynamic-update-slice_fusion), channel_id=1, source_target_pairs={{0,2},{1,3},{2,0},{3,1},{4,6},{5,7},{6,4},{7,5},{8,10},{9,11},{10,... | collective-permute-start | bytes 172040 | tf_op jit(solution)/shard_map/ppermute | solution.py:27
  6.9 15.7 %collective-permute-start = (bf16[2,112,128]{2,1,0:T(8,128)(2,1)S(1)}, bf16[2,112,128]{2,1,0:T(8,128)(2,1)S(1)}, u32[]{:S(2)}, u32[]{:S(2)}) collective-permute-start(bf16[2,112,128]{2,1,0:T(8,128)(2,1)S(1)} %constant_dynamic-update-slice_fusion), channel_id=1, source_target_pairs={{0,1},{1,0},{2,3},{3,2},{4,5},{5,4},{6,7},{7,6},{8,9},{9,8},{10,11... | collective-permute-start | bytes 172040 | tf_op jit(solution)/shard_map/ppermute | solution.py:27
  8.8 24.8 %all-to-all-start = ((bf16[64,16,128]{2,1,0:T(8,128)(2,1)}), bf16[64,16,128]{2,1,0:T(8,128)(2,1)S(1)}, u32[]{:S(2)}, u32[]{:S(2)}) async-start(bf16[64,16,128]{2,1,0:T(8,128)(2,1)} %reshape.50), calls=%async_computation | async-start | bytes 524288 | tf_op jit(solution)/shard_map/all_to_all | solution.py:32
  23.3 10.4 %copy-start.2 = (bf16[448,128]{1,0:T(8,128)(2,1)}, bf16[448,128]{1,0:T(8,128)(2,1)S(1)}, u32[]{:S(2)}) copy-start(bf16[448,128]{1,0:T(8,128)(2,1)S(1)} %convolution_convert_fusion.4) | copy-start | bytes 344068
  35.4 9.0 %copy-start.1 = (bf16[4096,128]{1,0:T(8,128)(2,1)S(1)}, bf16[4096,128]{1,0:T(8,128)(2,1)}, u32[]{:S(2)}) copy-start(bf16[4096,128]{1,0:T(8,128)(2,1)} %param.9) | copy-start | bytes 3145732
  37.4 18.1 %all-to-all-start.1 = ((bf16[64,16,128]{2,1,0:T(8,128)(2,1)}), bf16[64,16,128]{2,1,0:T(8,128)(2,1)S(1)}, u32[]{:S(2)}, u32[]{:S(2)}) async-start(bf16[64,16,128]{2,1,0:T(8,128)(2,1)} %reshape.52), calls=%async_computation.1 | async-start | bytes 524288 | tf_op jit(solution)/shard_map/all_to_all | solution.py:32
  56.9 20.4 %copy-start.4 = (bf16[1,112,128]{2,1,0:T(8,128)(2,1)S(1)}, bf16[1,112,128]{2,1,0:T(8,128)(2,1)}, u32[]{:S(2)}) copy-start(bf16[1,112,128]{2,1,0:T(8,128)(2,1)} %param.14) | copy-start | bytes 86020
  56.9 20.4 %copy-start.5 = (bf16[112,128]{1,0:T(8,128)(2,1)S(1)}, bf16[112,128]{1,0:T(8,128)(2,1)}, u32[]{:S(2)}) copy-start(bf16[112,128]{1,0:T(8,128)(2,1)} %get-tuple-element.11) | copy-start | bytes 86020
  58.9 18.2 %all-to-all-start.2 = ((bf16[64,16,128]{2,1,0:T(8,128)(2,1)}), bf16[64,16,128]{2,1,0:T(8,128)(2,1)S(1)}, u32[]{:S(2)}, u32[]{:S(2)}) async-start(bf16[64,16,128]{2,1,0:T(8,128)(2,1)} %reshape.54), calls=%async_computation.2 | async-start | bytes 524288 | tf_op jit(solution)/shard_map/all_to_all | solution.py:32
  66.4 26.7 %collective-permute-start.11 = (f32[128,128]{1,0:T(8,128)S(1)}, f32[128,128]{1,0:T(8,128)}, u32[]{:S(2)}, u32[]{:S(2)}) collective-permute-start(f32[128,128]{1,0:T(8,128)S(1)} %fusion.40), channel_id=1, source_target_pairs={{0,3},{1,2},{2,1},{3,0},{4,7},{5,6},{6,5},{7,4},{8,11},{9,10},{10,... | collective-permute-start | bytes 196616 | tf_op jit(solution)/shard_map/ppermute | solution.py:27
  66.5 27.8 %collective-permute-start.10 = (f32[128,128]{1,0:T(8,128)S(1)}, f32[128,128]{1,0:T(8,128)}, u32[]{:S(2)}, u32[]{:S(2)}) collective-permute-start(f32[128,128]{1,0:T(8,128)S(1)} %fusion.40), channel_id=1, source_target_pairs={{0,2},{1,3},{2,0},{3,1},{4,6},{5,7},{6,4},{7,5},{8,10},{9,11},{10,... | collective-permute-start | bytes 196616 | tf_op jit(solution)/shard_map/ppermute | solution.py:27
  69.7 24.7 %collective-permute-start.9 = (f32[128,128]{1,0:T(8,128)S(1)}, f32[128,128]{1,0:T(8,128)}, u32[]{:S(2)}, u32[]{:S(2)}) collective-permute-start(f32[128,128]{1,0:T(8,128)S(1)} %fusion.40), channel_id=1, source_target_pairs={{0,1},{1,0},{2,3},{3,2},{4,5},{5,4},{6,7},{7,6},{8,9},{9,8},{10,11... | collective-permute-start | bytes 196616 | tf_op jit(solution)/shard_map/ppermute | solution.py:27
  77.3 2.4 %copy-start.3 = (bf16[448,128]{1,0:T(8,128)(2,1)S(1)}, bf16[448,128]{1,0:T(8,128)(2,1)}, u32[]{:S(2)}) copy-start(bf16[448,128]{1,0:T(8,128)(2,1)} %copy-done.2) | copy-start | bytes 344068
  80.9 19.1 %all-to-all-start.3 = ((bf16[64,16,128]{2,1,0:T(8,128)(2,1)}), bf16[64,16,128]{2,1,0:T(8,128)(2,1)S(1)}, u32[]{:S(2)}, u32[]{:S(2)}) async-start(bf16[64,16,128]{2,1,0:T(8,128)(2,1)} %reshape.56), calls=%async_computation.3 | async-start | bytes 524288 | tf_op jit(solution)/shard_map/all_to_all | solution.py:32
  90.4 5.5 %collective-permute-start.8 = (f32[2,112,128]{2,1,0:T(8,128)S(1)}, f32[2,112,128]{2,1,0:T(8,128)S(1)}, u32[]{:S(2)}, u32[]{:S(2)}) collective-permute-start(f32[2,112,128]{2,1,0:T(8,128)S(1)} %get-tuple-element.4), channel_id=1, source_target_pairs={{0,3},{1,2},{2,1},{3,0},{4,7},{5,6},{6,5},{7,4},{8,11},{9,10},{10,... | collective-permute-start | bytes 344072 | tf_op jit(solution)/shard_map/ppermute | solution.py:27
  90.5 5.4 %collective-permute-start.6 = (f32[2,112,128]{2,1,0:T(8,128)S(1)}, f32[2,112,128]{2,1,0:T(8,128)S(1)}, u32[]{:S(2)}, u32[]{:S(2)}) collective-permute-start(f32[2,112,128]{2,1,0:T(8,128)S(1)} %get-tuple-element.5), channel_id=1, source_target_pairs={{0,1},{1,0},{2,3},{3,2},{4,5},{5,4},{6,7},{7,6},{8,9},{9,8},{10,11... | collective-permute-start | bytes 344072 | tf_op jit(solution)/shard_map/ppermute | solution.py:27
  93.1 6.2 %collective-permute-start.7 = (f32[2,112,128]{2,1,0:T(8,128)S(1)}, f32[2,112,128]{2,1,0:T(8,128)S(1)}, u32[]{:S(2)}, u32[]{:S(2)}) collective-permute-start(f32[2,112,128]{2,1,0:T(8,128)S(1)} %get-tuple-element.6), channel_id=1, source_target_pairs={{0,2},{1,3},{2,0},{3,1},{4,6},{5,7},{6,4},{7,5},{8,10},{9,11},{10,... | collective-permute-start | bytes 344072 | tf_op jit(solution)/shard_map/ppermute | solution.py:27
  100.3 4.7 %collective-permute-start.5 = (f32[128,128]{1,0:T(8,128)S(1)}, f32[128,128]{1,0:T(8,128)S(1)}, u32[]{:S(2)}, u32[]{:S(2)}) collective-permute-start(f32[128,128]{1,0:T(8,128)S(1)} %fusion.10), channel_id=1, source_target_pairs={{0,3},{1,2},{2,1},{3,0},{4,7},{5,6},{6,5},{7,4},{8,11},{9,10},{10,... | collective-permute-start | bytes 196616 | tf_op jit(solution)/shard_map/ppermute | solution.py:27
  101.0 6.5 %collective-permute-start.4 = (f32[128,128]{1,0:T(8,128)S(1)}, f32[128,128]{1,0:T(8,128)S(1)}, u32[]{:S(2)}, u32[]{:S(2)}) collective-permute-start(f32[128,128]{1,0:T(8,128)S(1)} %fusion.10), channel_id=1, source_target_pairs={{0,2},{1,3},{2,0},{3,1},{4,6},{5,7},{6,4},{7,5},{8,10},{9,11},{10,... | collective-permute-start | bytes 196616 | tf_op jit(solution)/shard_map/ppermute | solution.py:27
  104.2 3.3 %collective-permute-start.3 = (f32[128,128]{1,0:T(8,128)S(1)}, f32[128,128]{1,0:T(8,128)S(1)}, u32[]{:S(2)}, u32[]{:S(2)}) collective-permute-start(f32[128,128]{1,0:T(8,128)S(1)} %fusion.10), channel_id=1, source_target_pairs={{0,1},{1,0},{2,3},{3,2},{4,5},{5,4},{6,7},{7,6},{8,9},{9,8},{10,11... | collective-permute-start | bytes 196616 | tf_op jit(solution)/shard_map/ppermute | solution.py:27

commit v2 on v1

v2 whole, which is shorter than its diff:
```python
import functools
import math

import jax
import jax.numpy as jnp
from jax import lax
from jax.experimental import pallas as pl
from jax.experimental.pallas import tpu as pltpu
from jax.sharding import PartitionSpec as P

BS = 128
NB = 64
N_HID = 4
LANES = 128
STEP = 256


def token_groups():
    return [
        [b * N_HID + (q ^ (2 * (b % 2))) for b in range(NB)] for q in range(N_HID)
    ]


def from_partner(value, m):
    return lax.ppermute(value, "hid", [(i, i ^ m) for i in range(N_HID)])


def exchange(rows):
    pieces = rows.reshape(NB, rows.shape[0] // NB, LANES)
    pieces = lax.all_to_all(
        pieces, ("blk", "hid"), 0, 0, tiled=True, axis_index_groups=token_groups()
    )
    return pieces.reshape(rows.shape)


def dot(a, b, dims):
    return lax.dot_general(a, b, (dims, ((), ())), preferred_element_type=jnp.float32)


def mm(a, b):
    return dot(a, b, ((1,), (0,)))


def sum_over_hid(part):
    got = [from_partner(part, m) for m in (1, 2, 3)]
    return (part + got[0]) + (got[1] + got[2])


def put_pieces(spread, value, at):
    chunks = spread.shape[0] // BS
    for j in range(value.shape[1] // LANES):
        spread[pl.ds(at // LANES + j, BS, chunks), :] = value[:, j * LANES : (j + 1) * LANES]


def get_pieces(spread, at, size):
    chunks = spread.shape[0] // BS
    parts = [spread[pl.ds(at // LANES + j, BS, chunks), :] for j in range(size // LANES)]
    return jnp.concatenate(parts, axis=1).astype(jnp.bfloat16)


def first_kernel(quarter_ref, x_ref, first_ref, out_ref, spread):
    del quarter_ref
    first_t = first_ref[0].T
    count = x_ref.shape[0]
    for at in range(0, count, STEP):
        put_pieces(spread, dot(first_t, x_ref[at : at + STEP, :], ((1,), (1,))), at)
    out_ref[...] = spread[...].astype(jnp.bfloat16)


def forward_kernel(in_ref, up_ref, down_t_ref, out_ref, hidden_ref, slope_ref, spread_in, spread):
    spread_in[...] = in_ref[...].astype(jnp.float32)
    up = up_ref[...]
    down_t = down_t_ref[...]
    for at in range(0, hidden_ref.shape[1], STEP):
        preact = mm(up, get_pieces(spread_in, at, STEP))
        cdf = 0.5 * (1.0 + lax.erf(preact * (1.0 / math.sqrt(2.0))))
        dens = jnp.exp(-0.5 * preact * preact) * (1.0 / math.sqrt(2.0 * math.pi))
        hidden = (preact * cdf).astype(jnp.bfloat16)
        hidden_ref[:, at : at + STEP] = hidden
        slope_ref[:, at : at + STEP] = cdf + preact * dens
        put_pieces(spread, mm(down_t, hidden), at)
    out_ref[...] = spread[...].astype(jnp.bfloat16)


def error_kernel(scale, in_ref, last_ref, teacher_ref, out_ref, err_ref, spread_in, spread):
    spread_in[...] = in_ref[...].astype(jnp.float32)
    last = last_ref[0]
    last_t = last.T
    for at in range(0, err_ref.shape[1], STEP):
        student = mm(last_t, get_pieces(spread_in, at, STEP))
        teacher = teacher_ref[:, at : at + STEP].astype(jnp.float32)
        err = ((student - teacher) * scale).astype(jnp.bfloat16)
        err_ref[:, at : at + STEP] = err
        put_pieces(spread, mm(last, err), at)
    out_ref[...] = spread[...].astype(jnp.bfloat16)


def backward_kernel(in_ref, down_ref, up_t_ref, slope_ref, out_ref, grad_ref, spread_in, spread):
    spread_in[...] = in_ref[...].astype(jnp.float32)
    down = down_ref[...]
    up_t = up_t_ref[...]
    for at in range(0, grad_ref.shape[1], STEP):
        grad_hidden = mm(down, get_pieces(spread_in, at, STEP))
        grad = (grad_hidden * slope_ref[:, at : at + STEP]).astype(jnp.bfloat16)
        grad_ref[:, at : at + STEP] = grad
        put_pieces(spread, mm(up_t, grad), at)
    out_ref[...] = spread[...].astype(jnp.bfloat16)


def last_kernel(in_ref, x_t_ref, out_ref, spread_in):
    spread_in[...] = in_ref[...].astype(jnp.float32)
    grad = get_pieces(spread_in, 0, x_t_ref.shape[1])
    out_ref[...] = dot(x_t_ref[...], grad, ((1,), (1,)))


def whole(n):
    return [pl.BlockSpec(memory_space=pltpu.VMEM)] * n


PARAMS = pltpu.CompilerParams(vmem_limit_bytes=16 * 1024 * 1024)


def call(kernel, ins, outs, spreads, rows, flops):
    moved = sum(a.size * a.dtype.itemsize for a in ins) + sum(
        math.prod(o.shape) * o.dtype.itemsize for o in outs
    )
    return pl.pallas_call(
        kernel,
        out_shape=outs,
        in_specs=whole(len(ins)),
        out_specs=whole(len(outs)),
        scratch_shapes=[pltpu.VMEM((rows, LANES), jnp.float32)] * spreads,
        compiler_params=PARAMS,
        cost_estimate=pl.CostEstimate(flops=flops, bytes_accessed=moved, transcendentals=0),
    )(*ins)


def local(inputs, targets, row_order, mix_order, first_factor, up_factor, down_factor, last_factor):
    tokens = inputs.shape[0]
    count = tokens // N_HID
    piece_rows = BS * count // LANES
    loss_scale = 1.0 / math.sqrt(tokens)
    quarter = lax.axis_index("hid") ^ (2 * (lax.axis_index("blk") % 2))
    start = quarter * count
    shape = jax.ShapeDtypeStruct
    pieces = shape((piece_rows, LANES), jnp.bfloat16)

    first_out = pl.pallas_call(
        first_kernel,
        out_shape=pieces,
        grid_spec=pltpu.PrefetchScalarGridSpec(
            num_scalar_prefetch=1,
            grid=(1,),
            in_specs=[
                pl.BlockSpec((count, BS), lambda i, q: (q[0], 0)),
                pl.BlockSpec((1, BS, BS), lambda i, q: (0, 0, 0)),
            ],
            out_specs=pl.BlockSpec((piece_rows, LANES), lambda i, q: (0, 0)),
            scratch_shapes=[pltpu.VMEM((piece_rows, LANES), jnp.float32)],
        ),
        compiler_params=PARAMS,
    )(quarter.astype(jnp.int32)[None], inputs, first_factor)
    up_factor, down_factor, first_out = lax.optimization_barrier((up_factor, down_factor, first_out))
    arrived = exchange(first_out)

    up = jnp.concatenate([up_factor[0]] + [from_partner(up_factor[0], m) for m in (1, 2, 3)])
    down = jnp.concatenate([down_factor[0]] + [from_partner(down_factor[0], m) for m in (1, 2, 3)])
    units = up.shape[0]
    feature_ids = lax.broadcasted_iota(jnp.int32, (BS, BS), 0)
    one_hot = mix_order[None, :] == feature_ids
    up_mixed = dot(up, one_hot.astype(jnp.bfloat16), ((1,), (1,))).astype(jnp.bfloat16)
    up_mixed_t = up_mixed.T
    down_t = down.T
    rows = lax.dynamic_slice_in_dim(row_order, start, count, 0)
    teacher_t = jnp.take(targets, rows, axis=0).T
    x_t = lax.dynamic_slice_in_dim(inputs, start, count, 0).T

    flops = 2 * units * BS * count
    summed, hidden, slope = call(
        forward_kernel,
        (arrived, up_mixed, down_t),
        (pieces, shape((units, count), jnp.bfloat16), shape((units, count), jnp.float32)),
        2, piece_rows, 2 * flops,
    )
    returned = exchange(summed)

    grad_returned, err_grad = call(
        functools.partial(error_kernel, loss_scale),
        (returned, last_factor, teacher_t),
        (pieces, shape((BS, count), jnp.bfloat16)),
        2, piece_rows, flops,
    )
    grad_arrived = exchange(grad_returned)

    grad_grouped, grad_preact = call(
        backward_kernel,
        (grad_arrived, down, up_mixed_t, slope),
        (pieces, shape((units, count), jnp.bfloat16)),
        2, piece_rows, 2 * flops,
    )
    grad_first_out = exchange(grad_grouped)

    grad_last = dot(returned.reshape(BS, count), err_grad, ((1,), (1,)))
    grad_up = dot(grad_preact, arrived.reshape(BS, count), ((1,), (1,)))
    grad_down = dot(hidden, grad_arrived.reshape(BS, count), ((1,), (1,)))
    both = jnp.stack([grad_up.reshape(N_HID, -1, BS), grad_down.reshape(N_HID, -1, BS)], 1)
    got = [both[0]] + [from_partner(both[m], m) for m in (1, 2, 3)]
    both = (got[0] + got[1]) + (got[2] + got[3])
    grad_up = jnp.dot(both[0], one_hot.astype(jnp.float32), precision=lax.Precision.HIGHEST)
    grad_down = both[1]
    grad_last = sum_over_hid(grad_last)

    (grad_first,) = call(
        last_kernel, (grad_first_out, x_t), (shape((BS, BS), jnp.float32),), 1, piece_rows, flops // 4
    )
    grad_first = sum_over_hid(grad_first)
    return (grad_first[None], grad_up[None], grad_down[None], grad_last[None])


def solution(mesh):
    placed = (
        P(None, "blk"),
        P(None, "blk"),
        P(),
        P(),
        P("blk", None, None),
        P("blk", "hid", None),
        P("blk", "hid", None),
        P("blk", None, None),
    )
    return jax.shard_map(
        local,
        mesh=mesh,
        in_specs=placed,
        out_specs=(
            P("blk", None, None),
            P("blk", "hid", None),
            P("blk", "hid", None),
            P("blk", None, None),
        ),
        check_vma=False,
    )
```

time: 109 us -> 112 us (1.028)
  waiting for transfers between devices: 29.7 us -> 19.7 us
  starting transfers between devices: 46.8 us -> 55.8 us
  matrix products: 13 us -> 4.86 us
  local copies, waits for them, and re-layouts: 14.1 us -> 21 us
  Pallas kernels: 0 us -> 5.37 us
    all_to_all x4, waiting for transfers between devices: 23.8 us -> 11.7 us  [exchange(): lax.all_to_all(pieces, ('blk', 'hid'), 0, 0, tiled=True, axis_index_group...]
    all_to_all x4, starting transfers between devices: 31.1 us -> 41.6 us  [exchange(): lax.all_to_all(pieces, ('blk', 'hid'), 0, 0, tiled=True, axis_index_group...]
    dot_general x12 -> x4, matrix products: 12.2 us -> 4.05 us  [dot(): lax.dot_general(a, b, (dims, ((), ())), preferred_element_type=jnp.float32)]
    unnamed x17 -> x39, local copies, waits for them, and re-layouts: 0.88 us -> 8.75 us
    reshape x10 -> x0, local copies, waits for them, and re-layouts: 5.38 us -> none  [the longest x4 3.28 us: exchange(): pieces = rows.reshape(NB, 16, rows.shape[0] * rows.shape[1] // (NB * 16))]
    pallas_call x0 -> x5, Pallas kernels: none -> 5.37 us  [the longest x4 4.36 us: call(): pl.pallas_call(kernel, out_shape=outs, in_specs=whole(len(ins)), out_spec...]
    ppermute x12 -> x15, waiting for transfers between devices: 5.85 us -> 7.95 us  [from_partner(): return lax.ppermute(value, 'hid', [(i, i ^ m) for i in range(N_HID)])]
    another operation x1 -> x3, local copies, waits for them, and re-layouts: 0.76 us -> 2.69 us  [the longest x1 1.77 us: local(): grad_up = dot(grad_preact, arrived.reshape(BS, count), ((1,), (1,)))]
  transfers between devices with their start and end apart: 16 -> 19, of which waited for: 5 -> 10; matrix products, arithmetic and copies ran while one was open for 19% -> 20% of each run, Pallas kernels for 0% -> 2%
where the time goes in v2:
time: 112 us; the launch traced here: 111 us
  starting transfers between devices  55.8 us (50%)
  local copies, waits for them, and re-layouts  21 us (19%)
  waiting for transfers between devices  19.7 us (18%)
  Pallas kernels  5.37 us (5%)
  matrix products  4.86 us (4%)
  other arithmetic  3.94 us (4%)
    all_to_all x4, starting transfers between devices, exchange(): lax.all_to_all(pieces, ('blk', 'hid'), 0, 0, tiled=True, axis_index_group...  41.6 us
    ppermute x15, starting transfers between devices, from_partner(): return lax.ppermute(value, 'hid', [(i, i ^ m) for i in range(N_HID)])  14.1 us
    all_to_all x4, waiting for transfers between devices, exchange(): lax.all_to_all(pieces, ('blk', 'hid'), 0, 0, tiled=True, axis_index_group...  11.7 us
    unnamed x39, local copies, waits for them, and re-layouts  8.75 us
    ppermute x15, waiting for transfers between devices, from_partner(): return lax.ppermute(value, 'hid', [(i, i ^ m) for i in range(N_HID)])  7.95 us
    gather x2, local copies, waits for them, and re-layouts, local(): teacher_t = jnp.take(targets, rows, axis=0).T  6.11 us
    pallas_call x4, Pallas kernels, call(): pl.pallas_call(kernel, out_shape=outs, in_specs=whole(len(ins)), out_spec...  4.36 us
    dot_general x4, matrix products, dot(): lax.dot_general(a, b, (dims, ((), ())), preferred_element_type=jnp.float32)  4.05 us
  transfers between devices with their start and end apart: 19, of which 10 were waited for; matrix products, arithmetic and copies ran while one was open for 20% of the time, Pallas kernels for 2%

profile of v2, /device:TPU:1, one launch (start us, length us, event | category | flops | bytes accessed | tf_op | source)
XLA Modules:
  0.0 111.5 jit_solution(9605207437249620261)
XLA Ops:
  3.8 14.9 %all-to-all-start = ((bf16[64,16,128]{2,1,0:T(8,128)(2,1)}), bf16[64,16,128]{2,1,0:T(8,128)(2,1)S(1)}, u32[]{:S(2)}, u32[]{:S(2)}) async-start(bf16[64,16,128]{2,1,0:T(8,128)(2,1)} %bitcast.1), calls=%async_computation | async-start | bytes 524288 | tf_op jit(solution)/shard_map/all_to_all | solution.py:30
  19.8 1.7 %collective-permute-start.5 = (bf16[112,128]{1,0:T(8,128)(2,1)S(1)}, bf16[112,128]{1,0:T(8,128)(2,1)S(1)}, u32[]{:S(2)}, u32[]{:S(2)}) collective-permute-start(bf16[112,128]{1,0:T(8,128)(2,1)S(1)} %bitcast.68), channel_id=1, source_target_pairs={{0,3},{1,2},{2,1},{3,0},{4,7},{5,6},{6,5},{7,4},{8,11},{9,10},{10,... | collective-permute-start | bytes 86024 | tf_op jit(solution)/shard_map/ppermute | solution.py:25
  21.7 2.0 %collective-permute-start.2 = (bf16[112,128]{1,0:T(8,128)(2,1)S(1)}, bf16[112,128]{1,0:T(8,128)(2,1)S(1)}, u32[]{:S(2)}, u32[]{:S(2)}) collective-permute-start(bf16[112,128]{1,0:T(8,128)(2,1)S(1)} %bitcast.72), channel_id=1, source_target_pairs={{0,3},{1,2},{2,1},{3,0},{4,7},{5,6},{6,5},{7,4},{8,11},{9,10},{10,... | collective-permute-start | bytes 86024 | tf_op jit(solution)/shard_map/ppermute | solution.py:25
  26.0 4.5 %all-to-all-done = bf16[64,16,128]{2,1,0:T(8,128)(2,1)S(1)} async-done(((bf16[64,16,128]{2,1,0:T(8,128)(2,1)}), bf16[64,16,128]{2,1,0:T(8,128)(2,1)S(1)}, u32[]{:S(2)}, u32[]{:S(2)}) %all-to-all-start) | async-done | bytes 262176 | tf_op jit(solution)/shard_map/all_to_all | solution.py:30
  30.5 1.6 %shard_map.112 = (bf16[1024,128]{1,0:T(8,128)(2,1)S(1)}, bf16[448,1024]{1,0:T(8,128)(2,1)S(1)}, f32[448,1024]{1,0:T(8,128)S(1)}) custom-call(bf16[1024,128]{1,0:T(8,128)(2,1)S(1)} %bitcast.58, bf16[448,128]{1,0:T(8,128)(2,1)S(1)} %convolution_convert_fusion.up_ref, bf16[128,448]{1,0:T(8,128)(2,1)S(1)} %copy.20.down_t_ref), custom_call_target="tpu_custom_call" | custom-call | flops 234881024 | bytes 3506176 | tf_op jit(solution)/shard_map/pallas_call | solution.py:127
  33.8 7.6 %all-to-all-start.1 = ((bf16[64,16,128]{2,1,0:T(8,128)(2,1)}), bf16[64,16,128]{2,1,0:T(8,128)(2,1)S(1)}, u32[]{:S(2)}, u32[]{:S(2)}) async-start(bf16[64,16,128]{2,1,0:T(8,128)(2,1)} %bitcast.65), calls=%async_computation.1 | async-start | bytes 524288 | tf_op jit(solution)/shard_map/all_to_all | solution.py:30
  41.5 4.3 %gather_fusion = bf16[1024,128]{1,0:T(8,128)(2,1)} fusion(bf16[4096,128]{1,0:T(8,128)(2,1)S(1)} %copy-done, s32[1024]{0:T(1024)S(1)} %fusion.18), kind=kCustom, calls=%fused_computation | custom fusion | bytes 528384 | tf_op jit(solution)/shard_map/jit(_take)/gather | solution.py:175
  45.8 1.8 %copy.21 = bf16[1024,128]{0,1:T(8,128)(2,1)} copy(bf16[1024,128]{1,0:T(8,128)(2,1)} %gather_fusion) | data formatting | bytes 524288 | tf_op jit(solution)/shard_map/jit(_take)/gather | solution.py:175
  48.6 5.2 %all-to-all-done.1 = bf16[64,16,128]{2,1,0:T(8,128)(2,1)S(1)} async-done(((bf16[64,16,128]{2,1,0:T(8,128)(2,1)}), bf16[64,16,128]{2,1,0:T(8,128)(2,1)S(1)}, u32[]{:S(2)}, u32[]{:S(2)}) %all-to-all-start.1) | async-done | bytes 262176 | tf_op jit(solution)/shard_map/all_to_all | solution.py:30
  55.6 6.7 %all-to-all-start.2 = ((bf16[64,16,128]{2,1,0:T(8,128)(2,1)}), bf16[64,16,128]{2,1,0:T(8,128)(2,1)S(1)}, u32[]{:S(2)}, u32[]{:S(2)}) async-start(bf16[64,16,128]{2,1,0:T(8,128)(2,1)} %bitcast.64), calls=%async_computation.2 | async-start | bytes 524288 | tf_op jit(solution)/shard_map/all_to_all | solution.py:30
  62.3 1.7 %constant_dynamic-slice_fusion = bf16[1024,128]{1,0:T(8,128)(2,1)} fusion(bf16[4096,128]{1,0:T(8,128)(2,1)} %x_ref.1, s32[]{:T(128)S(6)} %select_n.25), kind=kLoop, calls=%fused_computation.39 | loop fusion | bytes 524292 | tf_op jit(solution)/shard_map/dynamic_slice | solution.py:176
  64.0 1.8 %copy.27 = bf16[1024,128]{0,1:T(8,128)(2,1)} copy(bf16[1024,128]{1,0:T(8,128)(2,1)} %constant_dynamic-slice_fusion) | data formatting | bytes 524288
  66.8 1.8 %reshape.69 = bf16[128,1024,1]{1,0,2:T(8,128)(2,1)} reshape(bf16[64,16,128]{2,1,0:T(8,128)(2,1)} %copy-done.2) | data formatting | bytes 524288 | tf_op jit(solution)/shard_map/reshape;reshape | solution.py:204
  69.4 1.9 %fusion.21 = f32[128,128]{1,0:T(8,128)} fusion(bf16[128,1024]{1,0:T(8,128)(2,1)} %reshape_reshape.11, bf16[128,1024]{1,0:T(8,128)(2,1)} %copy-done.10), kind=kOutput, calls=%fused_computation.42 | convolution fusion | flops 33554432 | bytes 589824 | tf_op jit(solution)/shard_map/dot_general | solution.py:37
  72.5 1.6 %collective-permute-start.14 = (f32[128,128]{1,0:T(8,128)}, f32[128,128]{1,0:T(8,128)}, u32[]{:S(2)}, u32[]{:S(2)}) collective-permute-start(f32[128,128]{1,0:T(8,128)} %fusion.21), channel_id=1, source_target_pairs={{0,3},{1,2},{2,1},{3,0},{4,7},{5,6},{6,5},{7,4},{8,11},{9,10},{10,... | collective-permute-start | bytes 196616 | tf_op jit(solution)/shard_map/ppermute | solution.py:25
  75.1 2.0 %shard_map.114 = (bf16[1024,128]{1,0:T(8,128)(2,1)}, bf16[448,1024]{1,0:T(8,128)(2,1)S(1)}) custom-call(bf16[1024,128]{1,0:T(8,128)(2,1)S(1)} %bitcast.56, bf16[448,128]{1,0:T(8,128)(2,1)S(1)} %copy-done.7, bf16[128,448]{1,0:T(8,128)(2,1)S(1)} %bitcast.63, f32[448,1024]{1,0:T(8,128)S(1)} %get-tuple-element.19.slope_ref), custom_call_target="tpu_custom_call" | custom-call | flops 234881024 | bytes 3506176 | tf_op jit(solution)/shard_map/pallas_call | solution.py:127
  78.0 12.4 %all-to-all-start.3 = ((bf16[64,16,128]{2,1,0:T(8,128)(2,1)}), bf16[64,16,128]{2,1,0:T(8,128)(2,1)S(1)}, u32[]{:S(2)}, u32[]{:S(2)}) async-start(bf16[64,16,128]{2,1,0:T(8,128)(2,1)} %bitcast.12), calls=%async_computation.3 | async-start | bytes 524288 | tf_op jit(solution)/shard_map/all_to_all | solution.py:30
  92.7 2.1 %collective-permute-start.11 = (f32[2,112,128]{2,1,0:T(8,128)S(1)}, f32[2,112,128]{2,1,0:T(8,128)S(1)}, u32[]{:S(2)}, u32[]{:S(2)}) collective-permute-start(f32[2,112,128]{2,1,0:T(8,128)S(1)} %get-tuple-element.24), channel_id=1, source_target_pairs={{0,3},{1,2},{2,1},{3,0},{4,7},{5,6},{6,5},{7,4},{8,11},{9,10},{10,... | collective-permute-start | bytes 344072 | tf_op jit(solution)/shard_map/ppermute | solution.py:25
  94.8 1.6 %add_bitcast_fusion = f32[1,128,128]{2,1,0:T(8,128)} fusion(f32[128,128]{1,0:T(8,128)} %collective-permute-done.13, f32[128,128]{1,0:T(8,128)} %collective-permute-done.14, f32[128,128]{1,0:T(8,128)} %fusion.21, f32[128,128]{1,0:T(8,128)} %collective-permute-done.12), kind=kLoop, calls=%fused_computation.30 | loop fusion | flops 49152 | bytes 327680 | tf_op jit(solution)/shard_map/broadcast_in_dim | solution.py:217
  96.9 3.4 %collective-permute-done.11 = f32[2,112,128]{2,1,0:T(8,128)S(1)} collective-permute-done((f32[2,112,128]{2,1,0:T(8,128)S(1)}, f32[2,112,128]{2,1,0:T(8,128)S(1)}, u32[]{:S(2)}, u32[]{:S(2)}) %collective-permute-start.11) | collective-permute-done | bytes 114720 | tf_op jit(solution)/shard_map/ppermute | solution.py:25
  100.9 2.0 %all-to-all-done.3 = bf16[64,16,128]{2,1,0:T(8,128)(2,1)S(1)} async-done(((bf16[64,16,128]{2,1,0:T(8,128)(2,1)}), bf16[64,16,128]{2,1,0:T(8,128)(2,1)S(1)}, u32[]{:S(2)}, u32[]{:S(2)}) %all-to-all-start.3) | async-done | bytes 262176 | tf_op jit(solution)/shard_map/all_to_all | solution.py:30
  103.2 2.4 %collective-permute-start.6 = (f32[128,128]{1,0:T(8,128)S(1)}, f32[128,128]{1,0:T(8,128)S(1)}, u32[]{:S(2)}, u32[]{:S(2)}) collective-permute-start(f32[128,128]{1,0:T(8,128)S(1)} %shard_map.115), channel_id=1, source_target_pairs={{0,1},{1,0},{2,3},{3,2},{4,5},{5,4},{6,7},{7,6},{8,9},{9,8},{10,11... | collective-permute-start | bytes 196616 | tf_op jit(solution)/shard_map/ppermute | solution.py:25
  105.6 1.7 %collective-permute-start.8 = (f32[128,128]{1,0:T(8,128)S(1)}, f32[128,128]{1,0:T(8,128)S(1)}, u32[]{:S(2)}, u32[]{:S(2)}) collective-permute-start(f32[128,128]{1,0:T(8,128)S(1)} %shard_map.115), channel_id=1, source_target_pairs={{0,3},{1,2},{2,1},{3,0},{4,7},{5,6},{6,5},{7,4},{8,11},{9,10},{10,... | collective-permute-start | bytes 196616 | tf_op jit(solution)/shard_map/ppermute | solution.py:25
  109.3 1.6 %collective-permute-done.8 = f32[128,128]{1,0:T(8,128)S(1)} collective-permute-done((f32[128,128]{1,0:T(8,128)S(1)}, f32[128,128]{1,0:T(8,128)S(1)}, u32[]{:S(2)}, u32[]{:S(2)}) %collective-permute-start.8) | collective-permute-done | bytes 65568 | tf_op jit(solution)/shard_map/ppermute | solution.py:25
  (80 shorter events, 22.2 us)
Async XLA Ops:
  0.6 40.8 %copy-start = (bf16[4096,128]{1,0:T(8,128)(2,1)S(1)}, bf16[4096,128]{1,0:T(8,128)(2,1)}, u32[]{:S(2)}) copy-start(bf16[4096,128]{1,0:T(8,128)(2,1)} %param.9) | copy-start | bytes 3145732
  0.6 18.1 %copy-start.15 = (bf16[1,112,128]{2,1,0:T(8,128)(2,1)S(1)}, bf16[1,112,128]{2,1,0:T(8,128)(2,1)}, u32[]{:S(2)}) copy-start(bf16[1,112,128]{2,1,0:T(8,128)(2,1)} %param.14) | copy-start | bytes 86020
  0.7 25.1 %copy-start.17 = (s32[128]{0:T(128)S(1)}, s32[128]{0:T(128)}, u32[]{:S(2)}) copy-start(s32[128]{0:T(128)} %param.11) | copy-start | bytes 1540
  2.7 18.7 %copy-start.18 = (bf16[1,112,128]{2,1,0:T(8,128)(2,1)S(1)}, bf16[1,112,128]{2,1,0:T(8,128)(2,1)}, u32[]{:S(2)}) copy-start(bf16[1,112,128]{2,1,0:T(8,128)(2,1)} %param.13) | copy-start | bytes 86020
  2.8 38.7 %copy-start.16 = (s32[4096]{0:T(1024)S(1)}, s32[4096]{0:T(1024)}, u32[]{:S(2)}) copy-start(s32[4096]{0:T(1024)} %param.10) | copy-start | bytes 49156
  3.8 26.8 %all-to-all-start = ((bf16[64,16,128]{2,1,0:T(8,128)(2,1)}), bf16[64,16,128]{2,1,0:T(8,128)(2,1)S(1)}, u32[]{:S(2)}, u32[]{:S(2)}) async-start(bf16[64,16,128]{2,1,0:T(8,128)(2,1)} %bitcast.1), calls=%async_computation | async-start | bytes 524288 | tf_op jit(solution)/shard_map/all_to_all | solution.py:30
  18.7 2.9 %collective-permute-start.3 = (bf16[112,128]{1,0:T(8,128)(2,1)S(1)}, bf16[112,128]{1,0:T(8,128)(2,1)S(1)}, u32[]{:S(2)}, u32[]{:S(2)}) collective-permute-start(bf16[112,128]{1,0:T(8,128)(2,1)S(1)} %bitcast.66), channel_id=1, source_target_pairs={{0,1},{1,0},{2,3},{3,2},{4,5},{5,4},{6,7},{7,6},{8,9},{9,8},{10,11... | collective-permute-start | bytes 86024 | tf_op jit(solution)/shard_map/ppermute | solution.py:25
  19.8 3.9 %collective-permute-start.4 = (bf16[112,128]{1,0:T(8,128)(2,1)S(1)}, bf16[112,128]{1,0:T(8,128)(2,1)S(1)}, u32[]{:S(2)}, u32[]{:S(2)}) collective-permute-start(bf16[112,128]{1,0:T(8,128)(2,1)S(1)} %bitcast.67), channel_id=1, source_target_pairs={{0,2},{1,3},{2,0},{3,1},{4,6},{5,7},{6,4},{7,5},{8,10},{9,11},{10,... | collective-permute-start | bytes 86024 | tf_op jit(solution)/shard_map/ppermute | solution.py:25
  19.8 4.0 %collective-permute-start.5 = (bf16[112,128]{1,0:T(8,128)(2,1)S(1)}, bf16[112,128]{1,0:T(8,128)(2,1)S(1)}, u32[]{:S(2)}, u32[]{:S(2)}) collective-permute-start(bf16[112,128]{1,0:T(8,128)(2,1)S(1)} %bitcast.68), channel_id=1, source_target_pairs={{0,3},{1,2},{2,1},{3,0},{4,7},{5,6},{6,5},{7,4},{8,11},{9,10},{10,... | collective-permute-start | bytes 86024 | tf_op jit(solution)/shard_map/ppermute | solution.py:25
  21.5 3.0 %collective-permute-start = (bf16[112,128]{1,0:T(8,128)(2,1)S(1)}, bf16[112,128]{1,0:T(8,128)(2,1)S(1)}, u32[]{:S(2)}, u32[]{:S(2)}) collective-permute-start(bf16[112,128]{1,0:T(8,128)(2,1)S(1)} %bitcast.70), channel_id=1, source_target_pairs={{0,1},{1,0},{2,3},{3,2},{4,5},{5,4},{6,7},{7,6},{8,9},{9,8},{10,11... | collective-permute-start | bytes 86024 | tf_op jit(solution)/shard_map/ppermute | solution.py:25
  21.6 3.0 %collective-permute-start.1 = (bf16[112,128]{1,0:T(8,128)(2,1)S(1)}, bf16[112,128]{1,0:T(8,128)(2,1)S(1)}, u32[]{:S(2)}, u32[]{:S(2)}) collective-permute-start(bf16[112,128]{1,0:T(8,128)(2,1)S(1)} %bitcast.71), channel_id=1, source_target_pairs={{0,2},{1,3},{2,0},{3,1},{4,6},{5,7},{6,4},{7,5},{8,10},{9,11},{10,... | collective-permute-start | bytes 86024 | tf_op jit(solution)/shard_map/ppermute | solution.py:25
  21.7 4.1 %collective-permute-start.2 = (bf16[112,128]{1,0:T(8,128)(2,1)S(1)}, bf16[112,128]{1,0:T(8,128)(2,1)S(1)}, u32[]{:S(2)}, u32[]{:S(2)}) collective-permute-start(bf16[112,128]{1,0:T(8,128)(2,1)S(1)} %bitcast.72), channel_id=1, source_target_pairs={{0,3},{1,2},{2,1},{3,0},{4,7},{5,6},{6,5},{7,4},{8,11},{9,10},{10,... | collective-permute-start | bytes 86024 | tf_op jit(solution)/shard_map/ppermute | solution.py:25
  33.8 19.9 %all-to-all-start.1 = ((bf16[64,16,128]{2,1,0:T(8,128)(2,1)}), bf16[64,16,128]{2,1,0:T(8,128)(2,1)S(1)}, u32[]{:S(2)}, u32[]{:S(2)}) async-start(bf16[64,16,128]{2,1,0:T(8,128)(2,1)} %bitcast.65), calls=%async_computation.1 | async-start | bytes 524288 | tf_op jit(solution)/shard_map/all_to_all | solution.py:30
  55.6 18.5 %all-to-all-start.2 = ((bf16[64,16,128]{2,1,0:T(8,128)(2,1)}), bf16[64,16,128]{2,1,0:T(8,128)(2,1)S(1)}, u32[]{:S(2)}, u32[]{:S(2)}) async-start(bf16[64,16,128]{2,1,0:T(8,128)(2,1)} %bitcast.64), calls=%async_computation.2 | async-start | bytes 524288 | tf_op jit(solution)/shard_map/all_to_all | solution.py:30
  71.3 23.5 %collective-permute-start.12 = (f32[128,128]{1,0:T(8,128)}, f32[128,128]{1,0:T(8,128)}, u32[]{:S(2)}, u32[]{:S(2)}) collective-permute-start(f32[128,128]{1,0:T(8,128)} %fusion.21), channel_id=1, source_target_pairs={{0,1},{1,0},{2,3},{3,2},{4,5},{5,4},{6,7},{7,6},{8,9},{9,8},{10,11... | collective-permute-start | bytes 196616 | tf_op jit(solution)/shard_map/ppermute | solution.py:25
  72.5 22.3 %collective-permute-start.13 = (f32[128,128]{1,0:T(8,128)}, f32[128,128]{1,0:T(8,128)}, u32[]{:S(2)}, u32[]{:S(2)}) collective-permute-start(f32[128,128]{1,0:T(8,128)} %fusion.21), channel_id=1, source_target_pairs={{0,2},{1,3},{2,0},{3,1},{4,6},{5,7},{6,4},{7,5},{8,10},{9,11},{10,... | collective-permute-start | bytes 196616 | tf_op jit(solution)/shard_map/ppermute | solution.py:25
  72.5 22.3 %collective-permute-start.14 = (f32[128,128]{1,0:T(8,128)}, f32[128,128]{1,0:T(8,128)}, u32[]{:S(2)}, u32[]{:S(2)}) collective-permute-start(f32[128,128]{1,0:T(8,128)} %fusion.21), channel_id=1, source_target_pairs={{0,3},{1,2},{2,1},{3,0},{4,7},{5,6},{6,5},{7,4},{8,11},{9,10},{10,... | collective-permute-start | bytes 196616 | tf_op jit(solution)/shard_map/ppermute | solution.py:25
  78.0 24.9 %all-to-all-start.3 = ((bf16[64,16,128]{2,1,0:T(8,128)(2,1)}), bf16[64,16,128]{2,1,0:T(8,128)(2,1)S(1)}, u32[]{:S(2)}, u32[]{:S(2)}) async-start(bf16[64,16,128]{2,1,0:T(8,128)(2,1)} %bitcast.12), calls=%async_computation.3 | async-start | bytes 524288 | tf_op jit(solution)/shard_map/all_to_all | solution.py:30
  92.6 4.3 %collective-permute-start.10 = (f32[2,112,128]{2,1,0:T(8,128)S(1)}, f32[2,112,128]{2,1,0:T(8,128)S(1)}, u32[]{:S(2)}, u32[]{:S(2)}) collective-permute-start(f32[2,112,128]{2,1,0:T(8,128)S(1)} %get-tuple-element.26), channel_id=1, source_target_pairs={{0,2},{1,3},{2,0},{3,1},{4,6},{5,7},{6,4},{7,5},{8,10},{9,11},{10,... | collective-permute-start | bytes 344072 | tf_op jit(solution)/shard_map/ppermute | solution.py:25
  92.7 7.6 %collective-permute-start.11 = (f32[2,112,128]{2,1,0:T(8,128)S(1)}, f32[2,112,128]{2,1,0:T(8,128)S(1)}, u32[]{:S(2)}, u32[]{:S(2)}) collective-permute-start(f32[2,112,128]{2,1,0:T(8,128)S(1)} %get-tuple-element.24), channel_id=1, source_target_pairs={{0,3},{1,2},{2,1},{3,0},{4,7},{5,6},{6,5},{7,4},{8,11},{9,10},{10,... | collective-permute-start | bytes 344072 | tf_op jit(solution)/shard_map/ppermute | solution.py:25
  94.8 5.5 %collective-permute-start.9 = (f32[2,112,128]{2,1,0:T(8,128)S(1)}, f32[2,112,128]{2,1,0:T(8,128)S(1)}, u32[]{:S(2)}, u32[]{:S(2)}) collective-permute-start(f32[2,112,128]{2,1,0:T(8,128)S(1)} %get-tuple-element.25), channel_id=1, source_target_pairs={{0,1},{1,0},{2,3},{3,2},{4,5},{5,4},{6,7},{7,6},{8,9},{9,8},{10,11... | collective-permute-start | bytes 344072 | tf_op jit(solution)/shard_map/ppermute | solution.py:25
  103.2 5.0 %collective-permute-start.6 = (f32[128,128]{1,0:T(8,128)S(1)}, f32[128,128]{1,0:T(8,128)S(1)}, u32[]{:S(2)}, u32[]{:S(2)}) collective-permute-start(f32[128,128]{1,0:T(8,128)S(1)} %shard_map.115), channel_id=1, source_target_pairs={{0,1},{1,0},{2,3},{3,2},{4,5},{5,4},{6,7},{7,6},{8,9},{9,8},{10,11... | collective-permute-start | bytes 196616 | tf_op jit(solution)/shard_map/ppermute | solution.py:25
  105.6 3.7 %collective-permute-start.7 = (f32[128,128]{1,0:T(8,128)S(1)}, f32[128,128]{1,0:T(8,128)S(1)}, u32[]{:S(2)}, u32[]{:S(2)}) collective-permute-start(f32[128,128]{1,0:T(8,128)S(1)} %shard_map.115), channel_id=1, source_target_pairs={{0,2},{1,3},{2,0},{3,1},{4,6},{5,7},{6,4},{7,5},{8,10},{9,11},{10,... | collective-permute-start | bytes 196616 | tf_op jit(solution)/shard_map/ppermute | solution.py:25
  105.6 5.2 %collective-permute-start.8 = (f32[128,128]{1,0:T(8,128)S(1)}, f32[128,128]{1,0:T(8,128)S(1)}, u32[]{:S(2)}, u32[]{:S(2)}) collective-permute-start(f32[128,128]{1,0:T(8,128)S(1)} %shard_map.115), channel_id=1, source_target_pairs={{0,3},{1,2},{2,1},{3,0},{4,7},{5,6},{6,5},{7,4},{8,11},{9,10},{10,... | collective-permute-start | bytes 196616 | tf_op jit(solution)/shard_map/ppermute | solution.py:25
  (14 other events, 81.4 us)

commit v3 on v2

v3 whole, which is shorter than its diff:
```python
import functools
import math

import jax
import jax.numpy as jnp
from jax import lax
from jax.experimental import pallas as pl
from jax.experimental.pallas import tpu as pltpu
from jax.sharding import PartitionSpec as P

BS = 128
NB = 64
N_HID = 4
LANES = 128
STEP = 256


def token_groups():
    return [
        [b * N_HID + (q ^ (2 * (b % 2))) for b in range(NB)] for q in range(N_HID)
    ]


def from_partner(value, m):
    return lax.ppermute(value, "hid", [(i, i ^ m) for i in range(N_HID)])


def exchange(rows):
    pieces = rows.reshape(NB, rows.shape[0] // NB, LANES)
    pieces = lax.all_to_all(
        pieces, ("blk", "hid"), 0, 0, tiled=True, axis_index_groups=token_groups()
    )
    return pieces.reshape(rows.shape)


def dot(a, b, dims):
    return lax.dot_general(a, b, (dims, ((), ())), preferred_element_type=jnp.float32)


def mm(a, b):
    return dot(a, b, ((1,), (0,)))


def sum_over_hid(part):
    got = [from_partner(part, m) for m in (1, 2, 3)]
    return (part + got[0]) + (got[1] + got[2])


def own_quarter():
    return lax.axis_index("hid") ^ (2 * (lax.axis_index("blk") % 2))


def put_pieces(spread, value, at):
    chunks = spread.shape[0] // BS
    for j in range(value.shape[1] // LANES):
        spread[pl.ds(at // LANES + j, BS, chunks), :] = value[:, j * LANES : (j + 1) * LANES]


def get_pieces(spread, at, size):
    chunks = spread.shape[0] // BS
    parts = [spread[pl.ds(at // LANES + j, BS, chunks), :] for j in range(size // LANES)]
    return jnp.concatenate(parts, axis=1).astype(jnp.bfloat16)


def keep(scratch, hbm, sems, i, size):
    columns = pl.ds(i * size, size)
    copy = pltpu.make_async_copy(scratch.at[:, columns], hbm.at[:, columns], sems.at[i])
    copy.start()
    return copy


def send_out(spread, buffer, hbm, sems, first_sem):
    half = spread.shape[0] // 2
    copies = []
    for i in range(2):
        rows = pl.ds(i * half, half)
        buffer[rows, :] = spread[rows, :].astype(jnp.bfloat16)
        copies.append(pltpu.make_async_copy(buffer.at[rows], hbm.at[rows], sems.at[first_sem + i]))
        copies[-1].start()
    return copies


def first_kernel(x_hbm, first_ref, out_hbm, x, spread, buffer, sems):
    count = x.shape[0]
    start = own_quarter() * count
    steps = count // STEP
    arrivals = []
    for i in range(steps):
        source = x_hbm.at[pl.ds(pl.multiple_of(start + i * STEP, STEP), STEP)]
        arrivals.append(pltpu.make_async_copy(source, x.at[pl.ds(i * STEP, STEP)], sems.at[i]))
        arrivals[-1].start()
    first_t = first_ref[0].T
    for i in range(steps):
        arrivals[i].wait()
        put_pieces(spread, dot(first_t, x[i * STEP : (i + 1) * STEP, :], ((1,), (1,))), i * STEP)
    for copy in send_out(spread, buffer, out_hbm, sems, steps):
        copy.wait()


def prepare_kernel(
    x_hbm, teacher_ref, mix_ref, *refs
):
    ups, downs = refs[0:4], refs[4:8]
    up_ref, up_t_ref, down_ref, down_t_ref, teacher_t_ref, x_t_ref, x, sem = refs[8:]
    count = x.shape[0]
    start = pl.multiple_of(own_quarter() * count, count)
    arrival = pltpu.make_async_copy(x_hbm.at[pl.ds(start, count)], x, sem)
    arrival.start()
    ids = lax.broadcasted_iota(jnp.int32, (BS, BS), 0)
    one_hot = (mix_ref[...] == ids).astype(jnp.float32).astype(jnp.bfloat16)
    eye = (lax.broadcasted_iota(jnp.int32, (BS, BS), 1) == ids).astype(jnp.float32)
    eye = eye.astype(jnp.bfloat16)
    up = jnp.concatenate([u[0] for u in ups])
    down = jnp.concatenate([d[0] for d in downs])
    down_ref[...] = down
    up_ref[...] = dot(up, one_hot, ((1,), (1,))).astype(jnp.bfloat16)
    up_t_ref[...] = dot(one_hot, up, ((1,), (1,))).astype(jnp.bfloat16)
    down_t_ref[...] = dot(eye, down, ((1,), (1,))).astype(jnp.bfloat16)
    teacher_t_ref[...] = dot(eye, teacher_ref[...], ((1,), (1,))).astype(jnp.bfloat16)
    arrival.wait()
    x_t_ref[...] = dot(eye, x[...], ((1,), (1,))).astype(jnp.bfloat16)


def forward_kernel(
    in_ref, up_ref, down_t_ref, out_ref, slope_ref, hidden_hbm, hidden_ref, spread_in, spread, sems
):
    spread_in[...] = in_ref[...].astype(jnp.float32)
    up = up_ref[...]
    down_t = down_t_ref[...]
    copies = []
    for i in range(hidden_ref.shape[1] // STEP):
        at = i * STEP
        preact = mm(up, get_pieces(spread_in, at, STEP))
        cdf = 0.5 * (1.0 + lax.erf(preact * (1.0 / math.sqrt(2.0))))
        dens = jnp.exp(-0.5 * preact * preact) * (1.0 / math.sqrt(2.0 * math.pi))
        hidden = (preact * cdf).astype(jnp.bfloat16)
        hidden_ref[:, at : at + STEP] = hidden
        copies.append(keep(hidden_ref, hidden_hbm, sems, i, STEP))
        slope_ref[:, at : at + STEP] = cdf + preact * dens
        put_pieces(spread, mm(down_t, hidden), at)
    out_ref[...] = spread[...].astype(jnp.bfloat16)
    for copy in copies:
        copy.wait()


def error_kernel(
    scale, in_ref, last_ref, teacher_ref, out_ref, err_hbm, err_ref, spread_in, spread, sems
):
    spread_in[...] = in_ref[...].astype(jnp.float32)
    last = last_ref[0]
    last_t = last.T
    copies = []
    for i in range(err_ref.shape[1] // STEP):
        at = i * STEP
        student = mm(last_t, get_pieces(spread_in, at, STEP))
        teacher = teacher_ref[:, at : at + STEP].astype(jnp.float32)
        err = ((student - teacher) * scale).astype(jnp.bfloat16)
        err_ref[:, at : at + STEP] = err
        copies.append(keep(err_ref, err_hbm, sems, i, STEP))
        put_pieces(spread, mm(last, err), at)
    out_ref[...] = spread[...].astype(jnp.bfloat16)
    for copy in copies:
        copy.wait()


def backward_kernel(
    in_ref, down_ref, up_t_ref, slope_ref, out_hbm, grad_hbm, grad_ref, spread_in, spread, buffer, sems
):
    spread_in[...] = in_ref[...].astype(jnp.float32)
    down = down_ref[...]
    up_t = up_t_ref[...]
    copies = []
    steps = grad_ref.shape[1] // STEP
    for i in range(steps):
        at = i * STEP
        grad_hidden = mm(down, get_pieces(spread_in, at, STEP))
        grad = (grad_hidden * slope_ref[:, at : at + STEP]).astype(jnp.bfloat16)
        grad_ref[:, at : at + STEP] = grad
        copies.append(keep(grad_ref, grad_hbm, sems, i, STEP))
        put_pieces(spread, mm(up_t, grad), at)
    for copy in copies + send_out(spread, buffer, out_hbm, sems, steps):
        copy.wait()


def weights_kernel(
    arrived_ref, returned_ref, grad_arrived_ref, hidden_ref, grad_ref, err_ref, mine_ref, theirs_ref, spread_in
):
    units, count = hidden_ref.shape
    half = units // 2

    def product(left, pieces_ref):
        spread_in[...] = pieces_ref[...].astype(jnp.float32)
        return dot(left, get_pieces(spread_in, 0, count), ((1,), (1,)))

    up = product(grad_ref[...], arrived_ref)
    mine_ref[0:half, :] = up[:half]
    theirs_ref[0:half, :] = up[half:]
    down = product(hidden_ref[...], grad_arrived_ref)
    mine_ref[half:units, :] = down[:half]
    theirs_ref[half:units, :] = down[half:]
    spread_in[...] = returned_ref[...].astype(jnp.float32)
    last = dot(get_pieces(spread_in, 0, count), err_ref[...], ((1,), (1,)))
    mine_ref[units:, :] = last
    theirs_ref[units:, :] = last


def chip_sum_kernel(mine_ref, got_ref, mine_out, theirs_out):
    quarter = (mine_ref.shape[0] - BS) // 4
    total = mine_ref[...] + got_ref[...]
    mine_out[0:quarter, :] = total[0:quarter]
    theirs_out[0:quarter, :] = total[quarter : 2 * quarter]
    mine_out[quarter : 2 * quarter, :] = total[2 * quarter : 3 * quarter]
    theirs_out[quarter : 2 * quarter, :] = total[3 * quarter : 4 * quarter]
    mine_out[2 * quarter :, :] = total[4 * quarter :]
    theirs_out[2 * quarter :, :] = total[4 * quarter :]


def totals_kernel(mine_ref, got_ref, mix_ref, up_ref, down_ref, last_ref):
    quarter = up_ref.shape[1]
    total = mine_ref[...] + got_ref[...]
    ids = lax.broadcasted_iota(jnp.int32, (BS, BS), 0)
    one_hot = (mix_ref[...] == ids).astype(jnp.float32)
    up_ref[0] = jnp.dot(
        total[0:quarter], one_hot, precision=lax.Precision.HIGHEST, preferred_element_type=jnp.float32
    )
    down_ref[0] = total[quarter : 2 * quarter]
    last_ref[0] = total[2 * quarter :]


def last_kernel(in_ref, x_t_ref, out_ref, spread_in):
    spread_in[...] = in_ref[...].astype(jnp.float32)
    grad = get_pieces(spread_in, 0, x_t_ref.shape[1])
    out_ref[...] = dot(x_t_ref[...], grad, ((1,), (1,)))


VMEM = pl.BlockSpec(memory_space=pltpu.VMEM)
HBM = pl.BlockSpec(memory_space=pltpu.HBM)
BF16 = jnp.bfloat16
F32 = jnp.float32


def call(kernel, ins, outs, scratch, flops, in_specs=None, out_specs=None):
    moved = sum(a.size * a.dtype.itemsize for a in ins) + sum(
        math.prod(o.shape) * o.dtype.itemsize for o in outs
    )
    return pl.pallas_call(
        kernel,
        out_shape=outs,
        in_specs=in_specs or [VMEM] * len(ins),
        out_specs=out_specs or [VMEM] * len(outs),
        scratch_shapes=scratch,
        compiler_params=pltpu.CompilerParams(vmem_limit_bytes=16 * 1024 * 1024),
        cost_estimate=pl.CostEstimate(flops=flops, bytes_accessed=moved, transcendentals=0),
    )(*ins)


def local(inputs, targets, row_order, mix_order, first_factor, up_factor, down_factor, last_factor):
    tokens = inputs.shape[0]
    count = tokens // N_HID
    steps = count // STEP
    piece_rows = BS * count // LANES
    loss_scale = 1.0 / math.sqrt(tokens)
    quarter_units = up_factor.shape[1]
    units = quarter_units * N_HID
    mix_row = mix_order[None, :]
    shape = jax.ShapeDtypeStruct
    pieces = shape((piece_rows, LANES), BF16)
    spread = pltpu.VMEM((piece_rows, LANES), F32)
    buffer = pltpu.VMEM((piece_rows, LANES), BF16)
    sems = pltpu.SemaphoreType.DMA((steps + 2,))
    flops = 2 * units * BS * count
    small = 2 * BS * BS * count

    (first_out,) = call(
        first_kernel,
        (inputs, first_factor),
        (pieces,),
        [pltpu.VMEM((count, BS), BF16), spread, buffer, sems],
        small,
        [HBM, VMEM],
        [HBM],
    )
    up_factor, down_factor, first_out = lax.optimization_barrier((up_factor, down_factor, first_out))
    arrived = exchange(first_out)

    up_far, down_far = from_partner(up_factor, 2), from_partner(down_factor, 2)
    ups = (up_factor, up_far, from_partner(up_factor, 1), from_partner(up_far, 1))
    downs = (down_factor, down_far, from_partner(down_factor, 1), from_partner(down_far, 1))
    rows = lax.dynamic_slice_in_dim(row_order, own_quarter() * count, count, 0)
    teacher = targets.at[rows].get(mode="promise_in_bounds")
    up_mixed, up_mixed_t, down, down_t, teacher_t, x_t = call(
        prepare_kernel,
        (inputs, teacher, mix_row) + ups + downs,
        (
            shape((units, BS), BF16),
            shape((BS, units), BF16),
            shape((units, BS), BF16),
            shape((BS, units), BF16),
            shape((BS, count), BF16),
            shape((BS, count), BF16),
        ),
        [pltpu.VMEM((count, BS), BF16), pltpu.SemaphoreType.DMA],
        2 * small,
        [HBM] + [VMEM] * 10,
    )

    summed, slope, hidden = call(
        forward_kernel,
        (arrived, up_mixed, down_t),
        (pieces, shape((units, count), F32), shape((units, count), BF16)),
        [pltpu.VMEM((units, count), BF16), spread, spread, sems],
        2 * flops,
        out_specs=[VMEM, VMEM, HBM],
    )
    returned = exchange(summed)

    grad_returned, err_grad = call(
        functools.partial(error_kernel, loss_scale),
        (returned, last_factor, teacher_t),
        (pieces, shape((BS, count), BF16)),
        [pltpu.VMEM((BS, count), BF16), spread, spread, sems],
        2 * small,
        out_specs=[VMEM, HBM],
    )
    grad_arrived = exchange(grad_returned)

    grad_grouped, grad_preact = call(
        backward_kernel,
        (grad_arrived, down, up_mixed_t, slope),
        (pieces, shape((units, count), BF16)),
        [pltpu.VMEM((units, count), BF16), spread, spread, buffer, sems],
        2 * flops,
        out_specs=[HBM, HBM],
    )
    grad_first_out = exchange(grad_grouped)

    half_rows = shape((units + BS, BS), F32)
    mine, theirs = call(
        weights_kernel,
        (arrived, returned, grad_arrived, hidden, grad_preact, err_grad),
        (half_rows, half_rows),
        [spread],
        2 * flops + small,
    )
    quarter_rows = shape((units // 2 + BS, BS), F32)
    mine, theirs = call(
        chip_sum_kernel, (mine, from_partner(theirs, 1)), (quarter_rows, quarter_rows), [], 0
    )
    factor_grad = shape((1, quarter_units, BS), F32)
    grad_up, grad_down, grad_last = call(
        totals_kernel,
        (mine, from_partner(theirs, 2), mix_row),
        (factor_grad, factor_grad, shape((1, BS, BS), F32)),
        [],
        0,
    )

    (grad_first,) = call(
        last_kernel, (grad_first_out, x_t), (shape((BS, BS), F32),), [spread], small
    )
    grad_first = sum_over_hid(grad_first)
    return (grad_first[None], grad_up, grad_down, grad_last)


def solution(mesh):
    placed = (
        P(None, "blk"),
        P(None, "blk"),
        P(),
        P(),
        P("blk", None, None),
        P("blk", "hid", None),
        P("blk", "hid", None),
        P("blk", None, None),
    )
    return jax.shard_map(
        local,
        mesh=mesh,
        in_specs=placed,
        out_specs=(
            P("blk", None, None),
            P("blk", "hid", None),
            P("blk", "hid", None),
            P("blk", None, None),
        ),
        check_vma=False,
    )
```

time: 112 us -> 114 us (1.018)
  blocking collectives: 0 us -> 42.3 us
  starting transfers between devices: 55.8 us -> 34 us
  waiting for transfers between devices: 19.7 us -> 10.1 us
  local copies, waits for them, and re-layouts: 21 us -> 14.9 us
  matrix products: 4.86 us -> 0 us
  Pallas kernels: 5.37 us -> 10.1 us
  other arithmetic: 3.94 us -> 1.34 us
    all_to_all x0 -> x2, blocking collectives: none -> 42.3 us  [exchange(): lax.all_to_all(pieces, ('blk', 'hid'), 0, 0, tiled=True, axis_index_group...]
    all_to_all x4 -> x2, starting transfers between devices: 41.6 us -> 21.7 us  [exchange(): lax.all_to_all(pieces, ('blk', 'hid'), 0, 0, tiled=True, axis_index_group...]
    all_to_all x4 -> x2, waiting for transfers between devices: 11.7 us -> 6.41 us  [exchange(): lax.all_to_all(pieces, ('blk', 'hid'), 0, 0, tiled=True, axis_index_group...]
    dot_general x5 -> x0, matrix products: 4.86 us -> none  [the longest x4 4.05 us: dot(): lax.dot_general(a, b, (dims, ((), ())), preferred_element_type=jnp.float32)]
    pallas_call x5 -> x9, Pallas kernels: 5.37 us -> 10.1 us  [call(): pl.pallas_call(kernel, out_shape=outs, in_specs=in_specs or [VMEM] * len(...]
    ppermute x15 -> x11, waiting for transfers between devices: 7.95 us -> 3.67 us  [from_partner(): return lax.ppermute(value, 'hid', [(i, i ^ m) for i in range(N_HID)])]
    unnamed x39 -> x44, local copies, waits for them, and re-layouts: 8.75 us -> 11.7 us
    gather x2 -> x1, local copies, waits for them, and re-layouts: 6.11 us -> 3.2 us  [local(): teacher = targets.at[rows].get(mode='promise_in_bounds')]
  transfers between devices with their start and end apart: 19 -> 13, of which waited for: 10 -> 3; matrix products, arithmetic and copies ran while one was open for 20% -> 3% of each run, Pallas kernels for 2% -> 2%
where the time goes in v3:
time: 114 us
  blocking collectives  42.3 us (37%)
  starting transfers between devices  34 us (30%)
  local copies, waits for them, and re-layouts  14.9 us (13%)
  Pallas kernels  10.1 us (9%)
  waiting for transfers between devices  10.1 us (9%)
  other arithmetic  1.34 us (1%)
    all_to_all x2, blocking collectives, exchange(): lax.all_to_all(pieces, ('blk', 'hid'), 0, 0, tiled=True, axis_index_group...  42.3 us
    all_to_all x2, starting transfers between devices, exchange(): lax.all_to_all(pieces, ('blk', 'hid'), 0, 0, tiled=True, axis_index_group...  21.7 us
    ppermute x11, starting transfers between devices, from_partner(): return lax.ppermute(value, 'hid', [(i, i ^ m) for i in range(N_HID)])  12.3 us
    unnamed x44, local copies, waits for them, and re-layouts  11.7 us
    pallas_call x9, Pallas kernels, call(): pl.pallas_call(kernel, out_shape=outs, in_specs=in_specs or [VMEM] * len(...  10.1 us
    all_to_all x2, waiting for transfers between devices, exchange(): lax.all_to_all(pieces, ('blk', 'hid'), 0, 0, tiled=True, axis_index_group...  6.41 us
    ppermute x11, waiting for transfers between devices, from_partner(): return lax.ppermute(value, 'hid', [(i, i ^ m) for i in range(N_HID)])  3.67 us
    gather x1, local copies, waits for them, and re-layouts, local(): teacher = targets.at[rows].get(mode='promise_in_bounds')  3.2 us
  transfers between devices with their start and end apart: 13, of which 3 were waited for; matrix products, arithmetic and copies ran while one was open for 3% of the time, Pallas kernels for 2%

profile of v3, /device:TPU:1, one launch (start us, length us, event | category | flops | bytes accessed | tf_op | source)
XLA Modules:
  0.0 113.6 jit_solution(6231644322106895197)
XLA Ops:
  0.7 1.3 %copy-done.1 = bf16[4096,128]{1,0:T(8,128)(2,1)S(1)} copy-done((bf16[4096,128]{1,0:T(8,128)(2,1)S(1)}, bf16[4096,128]{1,0:T(8,128)(2,1)}, u32[]{:S(2)}) %copy-start.1) | copy-done | bytes 1048600
  2.7 1.9 %shard_map.111 = bf16[1024,128]{1,0:T(8,128)(2,1)} custom-call(bf16[4096,128]{1,0:T(8,128)(2,1)S(1)} %copy-done.1, bf16[1,128,128]{2,1,0:T(8,128)(2,1)S(1)} %copy-done.14), custom_call_target="tpu_custom_call" | custom-call | flops 33554432 | bytes 1343488 | tf_op jit(solution)/shard_map/pallas_call | solution.py:246
  4.6 14.9 %all-to-all-start = ((bf16[64,16,128]{2,1,0:T(8,128)(2,1)}), bf16[64,16,128]{2,1,0:T(8,128)(2,1)S(1)}, u32[]{:S(2)}, u32[]{:S(2)}) async-start(bf16[64,16,128]{2,1,0:T(8,128)(2,1)} %bitcast), calls=%async_computation | async-start | bytes 524288 | tf_op jit(solution)/shard_map/all_to_all | solution.py:30
  19.7 1.4 %collective-permute-start.3 = (bf16[1,112,128]{2,1,0:T(8,128)(2,1)S(1)}, bf16[1,112,128]{2,1,0:T(8,128)(2,1)S(1)}, u32[]{:S(2)}, u32[]{:S(2)}) collective-permute-start(bf16[1,112,128]{2,1,0:T(8,128)(2,1)S(1)} %copy-done.16), channel_id=1, source_target_pairs={{0,2},{1,3},{2,0},{3,1},{4,6},{5,7},{6,4},{7,5},{8,10},{9,11},{10,... | collective-permute-start | bytes 86024 | tf_op jit(solution)/shard_map/ppermute | solution.py:25
  21.2 1.5 %collective-permute-start.1 = (bf16[1,112,128]{2,1,0:T(8,128)(2,1)S(1)}, bf16[1,112,128]{2,1,0:T(8,128)(2,1)S(1)}, u32[]{:S(2)}, u32[]{:S(2)}) collective-permute-start(bf16[1,112,128]{2,1,0:T(8,128)(2,1)S(1)} %copy-done.15), channel_id=1, source_target_pairs={{0,1},{1,0},{2,3},{3,2},{4,5},{5,4},{6,7},{7,6},{8,9},{9,8},{10,11... | collective-permute-start | bytes 86024 | tf_op jit(solution)/shard_map/ppermute | solution.py:25
  22.7 1.8 %collective-permute-start.2 = (bf16[1,112,128]{2,1,0:T(8,128)(2,1)S(1)}, bf16[1,112,128]{2,1,0:T(8,128)(2,1)S(1)}, u32[]{:S(2)}, u32[]{:S(2)}) collective-permute-start(bf16[1,112,128]{2,1,0:T(8,128)(2,1)S(1)} %collective-permute-done.refs_1_), channel_id=1, source_target_pairs={{0,1},{1,0},{2,3},{3,2},{4,5},{5,4},{6,7},{7,6},{8,9},{9,8},{10,11... | collective-permute-start | bytes 86024 | tf_op jit(solution)/shard_map/ppermute | solution.py:25
  25.5 3.2 %gather_fusion = bf16[1024,128]{1,0:T(8,128)(2,1)S(1)} fusion(bf16[4096,128]{1,0:T(8,128)(2,1)S(1)} %copy-done, s32[1024]{0:T(1024)S(1)} %fusion), kind=kCustom, calls=%fused_computation | custom fusion | bytes 528384 | tf_op jit(solution)/shard_map/gather | solution.py:290
  33.5 0.9 copy-done.19
  34.4 0.9 copy-done.21
  35.3 2.2 %shard_map.113 = (bf16[1024,128]{1,0:T(8,128)(2,1)S(1)}, f32[448,1024]{1,0:T(8,128)S(1)}, bf16[448,1024]{1,0:T(8,128)(2,1)S(1)}) custom-call(bf16[1024,128]{1,0:T(8,128)(2,1)S(1)} %bitcast.16, bf16[448,128]{1,0:T(8,128)(2,1)S(1)} %copy-done.21, bf16[128,448]{1,0:T(8,128)(2,1)S(1)} %copy-done.19), custom_call_target="tpu_custom_call" | custom-call | flops 234881024 | bytes 3506176 | tf_op jit(solution)/shard_map/pallas_call | solution.py:246
  37.5 24.4 %all_to_all.20 = bf16[64,16,128]{2,1,0:T(8,128)(2,1)S(1)} all-to-all(bf16[64,16,128]{2,1,0:T(8,128)(2,1)S(1)} %bitcast.18), channel_id=1, replica_groups={{0,6,8,14,16,22,24,30,32,38,40,46,48,54,56,62,64,70,72,78,80,86,88,94,9..., dimensions={0} | all-to-all | bytes 524288 | tf_op jit(solution)/shard_map/all_to_all | solution.py:30
  62.0 0.9 copy-done.8
  63.7 1.0 shard_map.114
  64.7 17.9 %all_to_all.21 = bf16[64,16,128]{2,1,0:T(8,128)(2,1)S(1)} all-to-all(bf16[64,16,128]{2,1,0:T(8,128)(2,1)S(1)} %bitcast.19), channel_id=1, replica_groups={{0,6,8,14,16,22,24,30,32,38,40,46,48,54,56,62,64,70,72,78,80,86,88,94,9..., dimensions={0} | all-to-all | bytes 524288 | tf_op jit(solution)/shard_map/all_to_all | solution.py:30
  82.6 2.4 %shard_map.115 = (bf16[1024,128]{1,0:T(8,128)(2,1)}, bf16[448,1024]{1,0:T(8,128)(2,1)S(1)}) custom-call(bf16[1024,128]{1,0:T(8,128)(2,1)S(1)} %bitcast.11, bf16[448,128]{1,0:T(8,128)(2,1)S(1)} %copy-done.12, bf16[128,448]{1,0:T(8,128)(2,1)S(1)} %copy-done.10, f32[448,1024]{1,0:T(8,128)S(1)} %get-tuple-element.37.slope_ref), custom_call_target="tpu_custom_call" | custom-call | flops 234881024 | bytes 3506176 | tf_op jit(solution)/shard_map/pallas_call | solution.py:246
  85.0 0.9 copy-done.3
  85.9 6.8 %all-to-all-start.3 = ((bf16[64,16,128]{2,1,0:T(8,128)(2,1)}), bf16[64,16,128]{2,1,0:T(8,128)(2,1)S(1)}, u32[]{:S(2)}, u32[]{:S(2)}) async-start(bf16[64,16,128]{2,1,0:T(8,128)(2,1)} %bitcast.7), calls=%async_computation.3 | async-start | bytes 524288 | tf_op jit(solution)/shard_map/all_to_all | solution.py:30
  92.7 1.2 %copy-done.4 = bf16[448,1024]{1,0:T(8,128)(2,1)S(1)} copy-done((bf16[448,1024]{1,0:T(8,128)(2,1)S(1)}, bf16[448,1024]{1,0:T(8,128)(2,1)}, u32[]{:S(2)}) %copy-start.4) | copy-done | bytes 917528
  94.7 1.9 %collective-permute-start.9 = (f32[576,128]{1,0:T(8,128)S(1)}, f32[576,128]{1,0:T(8,128)S(1)}, u32[]{:S(2)}, u32[]{:S(2)}) collective-permute-start(f32[576,128]{1,0:T(8,128)S(1)} %get-tuple-element.44), channel_id=1, source_target_pairs={{0,1},{1,0},{2,3},{3,2},{4,5},{5,4},{6,7},{7,6},{8,9},{9,8},{10,11... | collective-permute-start | bytes 884744 | tf_op jit(solution)/shard_map/ppermute | solution.py:25
  96.6 1.2 %collective-permute-done.9.got_ref = f32[576,128]{1,0:T(8,128)S(1)} collective-permute-done((f32[576,128]{1,0:T(8,128)S(1)}, f32[576,128]{1,0:T(8,128)S(1)}, u32[]{:S(2)}, u32[]{:S(2)}) %collective-permute-start.9) | collective-permute-done | bytes 294944 | tf_op jit(solution)/shard_map/ppermute | solution.py:25
  97.9 6.4 %all-to-all-done.3 = bf16[64,16,128]{2,1,0:T(8,128)(2,1)S(1)} async-done(((bf16[64,16,128]{2,1,0:T(8,128)(2,1)}), bf16[64,16,128]{2,1,0:T(8,128)(2,1)S(1)}, u32[]{:S(2)}, u32[]{:S(2)}) %all-to-all-start.3) | async-done | bytes 262176 | tf_op jit(solution)/shard_map/all_to_all | solution.py:30
  105.4 4.3 %collective-permute-start.7 = (f32[128,128]{1,0:T(8,128)S(1)}, f32[128,128]{1,0:T(8,128)S(1)}, u32[]{:S(2)}, u32[]{:S(2)}) collective-permute-start(f32[128,128]{1,0:T(8,128)S(1)} %shard_map.116), channel_id=1, source_target_pairs={{0,2},{1,3},{2,0},{3,1},{4,6},{5,7},{6,4},{7,5},{8,10},{9,11},{10,... | collective-permute-start | bytes 196616 | tf_op jit(solution)/shard_map/ppermute | solution.py:25
  109.7 0.8 shard_map.119
  110.5 2.4 %collective-permute-done.7 = f32[128,128]{1,0:T(8,128)S(1)} collective-permute-done((f32[128,128]{1,0:T(8,128)S(1)}, f32[128,128]{1,0:T(8,128)S(1)}, u32[]{:S(2)}, u32[]{:S(2)}) %collective-permute-start.7) | collective-permute-done | bytes 65568 | tf_op jit(solution)/shard_map/ppermute | solution.py:25
  (60 shorter events, 10.0 us)
Async XLA Ops:
  0.6 24.9 %copy-start = (bf16[4096,128]{1,0:T(8,128)(2,1)S(1)}, bf16[4096,128]{1,0:T(8,128)(2,1)}, u32[]{:S(2)}) copy-start(bf16[4096,128]{1,0:T(8,128)(2,1)} %param.9) | copy-start | bytes 3145732
  0.6 1.3 %copy-start.1 = (bf16[4096,128]{1,0:T(8,128)(2,1)S(1)}, bf16[4096,128]{1,0:T(8,128)(2,1)}, u32[]{:S(2)}) copy-start(bf16[4096,128]{1,0:T(8,128)(2,1)} %x_hbm.3) | copy-start | bytes 3145732
  2.7 16.9 %copy-start.15 = (bf16[1,112,128]{2,1,0:T(8,128)(2,1)S(1)}, bf16[1,112,128]{2,1,0:T(8,128)(2,1)}, u32[]{:S(2)}) copy-start(bf16[1,112,128]{2,1,0:T(8,128)(2,1)} %refs_0_) | copy-start | bytes 86020
  2.7 17.0 %copy-start.16 = (bf16[1,112,128]{2,1,0:T(8,128)(2,1)S(1)}, bf16[1,112,128]{2,1,0:T(8,128)(2,1)}, u32[]{:S(2)}) copy-start(bf16[1,112,128]{2,1,0:T(8,128)(2,1)} %refs_4_) | copy-start | bytes 86020
  2.7 26.1 %copy-start.2 = (bf16[4096,128]{1,0:T(8,128)(2,1)S(1)}, bf16[4096,128]{1,0:T(8,128)(2,1)}, u32[]{:S(2)}) copy-start(bf16[4096,128]{1,0:T(8,128)(2,1)} %x_hbm.3) | copy-start | bytes 3145732
  2.7 26.1 %copy-start.17 = (s32[128]{0:T(128)S(1)}, s32[128]{0:T(128)}, u32[]{:S(2)}) copy-start(s32[128]{0:T(128)} %param.11) | copy-start | bytes 1540
  4.6 28.8 %all-to-all-start = ((bf16[64,16,128]{2,1,0:T(8,128)(2,1)}), bf16[64,16,128]{2,1,0:T(8,128)(2,1)S(1)}, u32[]{:S(2)}, u32[]{:S(2)}) async-start(bf16[64,16,128]{2,1,0:T(8,128)(2,1)} %bitcast), calls=%async_computation | async-start | bytes 524288 | tf_op jit(solution)/shard_map/all_to_all | solution.py:30
  19.6 3.1 %collective-permute-start = (bf16[1,112,128]{2,1,0:T(8,128)(2,1)S(1)}, bf16[1,112,128]{2,1,0:T(8,128)(2,1)S(1)}, u32[]{:S(2)}, u32[]{:S(2)}) collective-permute-start(bf16[1,112,128]{2,1,0:T(8,128)(2,1)S(1)} %copy-done.15), channel_id=1, source_target_pairs={{0,2},{1,3},{2,0},{3,1},{4,6},{5,7},{6,4},{7,5},{8,10},{9,11},{10,... | collective-permute-start | bytes 86024 | tf_op jit(solution)/shard_map/ppermute | solution.py:25
  19.7 4.8 %collective-permute-start.3 = (bf16[1,112,128]{2,1,0:T(8,128)(2,1)S(1)}, bf16[1,112,128]{2,1,0:T(8,128)(2,1)S(1)}, u32[]{:S(2)}, u32[]{:S(2)}) collective-permute-start(bf16[1,112,128]{2,1,0:T(8,128)(2,1)S(1)} %copy-done.16), channel_id=1, source_target_pairs={{0,2},{1,3},{2,0},{3,1},{4,6},{5,7},{6,4},{7,5},{8,10},{9,11},{10,... | collective-permute-start | bytes 86024 | tf_op jit(solution)/shard_map/ppermute | solution.py:25
  21.2 7.6 %collective-permute-start.1 = (bf16[1,112,128]{2,1,0:T(8,128)(2,1)S(1)}, bf16[1,112,128]{2,1,0:T(8,128)(2,1)S(1)}, u32[]{:S(2)}, u32[]{:S(2)}) collective-permute-start(bf16[1,112,128]{2,1,0:T(8,128)(2,1)S(1)} %copy-done.15), channel_id=1, source_target_pairs={{0,1},{1,0},{2,3},{3,2},{4,5},{5,4},{6,7},{7,6},{8,9},{9,8},{10,11... | collective-permute-start | bytes 86024 | tf_op jit(solution)/shard_map/ppermute | solution.py:25
  22.7 6.1 %collective-permute-start.4 = (bf16[1,112,128]{2,1,0:T(8,128)(2,1)S(1)}, bf16[1,112,128]{2,1,0:T(8,128)(2,1)S(1)}, u32[]{:S(2)}, u32[]{:S(2)}) collective-permute-start(bf16[1,112,128]{2,1,0:T(8,128)(2,1)S(1)} %copy-done.16), channel_id=1, source_target_pairs={{0,1},{1,0},{2,3},{3,2},{4,5},{5,4},{6,7},{7,6},{8,9},{9,8},{10,11... | collective-permute-start | bytes 86024 | tf_op jit(solution)/shard_map/ppermute | solution.py:25
  22.7 6.1 %collective-permute-start.2 = (bf16[1,112,128]{2,1,0:T(8,128)(2,1)S(1)}, bf16[1,112,128]{2,1,0:T(8,128)(2,1)S(1)}, u32[]{:S(2)}, u32[]{:S(2)}) collective-permute-start(bf16[1,112,128]{2,1,0:T(8,128)(2,1)S(1)} %collective-permute-done.refs_1_), channel_id=1, source_target_pairs={{0,1},{1,0},{2,3},{3,2},{4,5},{5,4},{6,7},{7,6},{8,9},{9,8},{10,11... | collective-permute-start | bytes 86024 | tf_op jit(solution)/shard_map/ppermute | solution.py:25
  24.5 4.2 %collective-permute-start.5 = (bf16[1,112,128]{2,1,0:T(8,128)(2,1)S(1)}, bf16[1,112,128]{2,1,0:T(8,128)(2,1)S(1)}, u32[]{:S(2)}, u32[]{:S(2)}) collective-permute-start(bf16[1,112,128]{2,1,0:T(8,128)(2,1)S(1)} %collective-permute-done.3.refs_5_), channel_id=1, source_target_pairs={{0,1},{1,0},{2,3},{3,2},{4,5},{5,4},{6,7},{7,6},{8,9},{9,8},{10,11... | collective-permute-start | bytes 86024 | tf_op jit(solution)/shard_map/ppermute | solution.py:25
  33.5 49.1 %copy-start.10 = (bf16[128,448]{1,0:T(8,128)(2,1)S(1)}, bf16[128,448]{1,0:T(8,128)(2,1)}, u32[]{:S(2)}) copy-start(bf16[128,448]{1,0:T(8,128)(2,1)} %copy-done.9) | copy-start | bytes 344068
  33.5 49.1 %copy-start.12 = (bf16[448,128]{1,0:T(8,128)(2,1)S(1)}, bf16[448,128]{1,0:T(8,128)(2,1)}, u32[]{:S(2)}) copy-start(bf16[448,128]{1,0:T(8,128)(2,1)} %copy-done.11) | copy-start | bytes 344068
  62.0 1.0 copy-start.8
  85.9 18.4 %copy-start.6 = (bf16[128,1024]{1,0:T(8,128)(2,1)S(1)}, bf16[128,1024]{1,0:T(8,128)(2,1)}, u32[]{:S(2)}) copy-start(bf16[128,1024]{1,0:T(8,128)(2,1)} %copy-done.5) | copy-start | bytes 786436
  85.9 18.4 %all-to-all-start.3 = ((bf16[64,16,128]{2,1,0:T(8,128)(2,1)}), bf16[64,16,128]{2,1,0:T(8,128)(2,1)S(1)}, u32[]{:S(2)}, u32[]{:S(2)}) async-start(bf16[64,16,128]{2,1,0:T(8,128)(2,1)} %bitcast.7), calls=%async_computation.3 | async-start | bytes 524288 | tf_op jit(solution)/shard_map/all_to_all | solution.py:30
  92.7 1.2 %copy-start.4 = (bf16[448,1024]{1,0:T(8,128)(2,1)S(1)}, bf16[448,1024]{1,0:T(8,128)(2,1)}, u32[]{:S(2)}) copy-start(bf16[448,1024]{1,0:T(8,128)(2,1)} %copy-done.3) | copy-start | bytes 2752516
  94.7 3.1 %collective-permute-start.9 = (f32[576,128]{1,0:T(8,128)S(1)}, f32[576,128]{1,0:T(8,128)S(1)}, u32[]{:S(2)}, u32[]{:S(2)}) collective-permute-start(f32[576,128]{1,0:T(8,128)S(1)} %get-tuple-element.44), channel_id=1, source_target_pairs={{0,1},{1,0},{2,3},{3,2},{4,5},{5,4},{6,7},{7,6},{8,9},{9,8},{10,11... | collective-permute-start | bytes 884744 | tf_op jit(solution)/shard_map/ppermute | solution.py:25
  97.8 11.9 %collective-permute-start.10 = (f32[352,128]{1,0:T(8,128)S(1)}, f32[352,128]{1,0:T(8,128)S(1)}, u32[]{:S(2)}, u32[]{:S(2)}) collective-permute-start(f32[352,128]{1,0:T(8,128)S(1)} %get-tuple-element.46), channel_id=1, source_target_pairs={{0,2},{1,3},{2,0},{3,1},{4,6},{5,7},{6,4},{7,5},{8,10},{9,11},{10,... | collective-permute-start | bytes 540680 | tf_op jit(solution)/shard_map/ppermute | solution.py:25
  104.6 5.9 %collective-permute-start.8 = (f32[128,128]{1,0:T(8,128)S(1)}, f32[128,128]{1,0:T(8,128)S(1)}, u32[]{:S(2)}, u32[]{:S(2)}) collective-permute-start(f32[128,128]{1,0:T(8,128)S(1)} %shard_map.116), channel_id=1, source_target_pairs={{0,3},{1,2},{2,1},{3,0},{4,7},{5,6},{6,5},{7,4},{8,11},{9,10},{10,... | collective-permute-start | bytes 196616 | tf_op jit(solution)/shard_map/ppermute | solution.py:25
  105.4 7.6 %collective-permute-start.7 = (f32[128,128]{1,0:T(8,128)S(1)}, f32[128,128]{1,0:T(8,128)S(1)}, u32[]{:S(2)}, u32[]{:S(2)}) collective-permute-start(f32[128,128]{1,0:T(8,128)S(1)} %shard_map.116), channel_id=1, source_target_pairs={{0,2},{1,3},{2,0},{3,1},{4,6},{5,7},{6,4},{7,5},{8,10},{9,11},{10,... | collective-permute-start | bytes 196616 | tf_op jit(solution)/shard_map/ppermute | solution.py:25
  109.7 3.3 %collective-permute-start.6 = (f32[128,128]{1,0:T(8,128)S(1)}, f32[128,128]{1,0:T(8,128)S(1)}, u32[]{:S(2)}, u32[]{:S(2)}) collective-permute-start(f32[128,128]{1,0:T(8,128)S(1)} %shard_map.116), channel_id=1, source_target_pairs={{0,1},{1,0},{2,3},{3,2},{4,5},{5,4},{6,7},{7,6},{8,9},{9,8},{10,11... | collective-permute-start | bytes 196616 | tf_op jit(solution)/shard_map/ppermute | solution.py:25
  (11 other events, 8.3 us)

commit v4 on v3

v4 whole, which is shorter than its diff:
```python
import functools
import math

import jax
import jax.numpy as jnp
from jax import lax
from jax.experimental import pallas as pl
from jax.experimental.pallas import tpu as pltpu
from jax.sharding import PartitionSpec as P

BS = 128
NB = 64
N_HID = 4
LANES = 128
STEP = 256


def token_groups():
    return [
        [b * N_HID + (q ^ (2 * (b % 2))) for b in range(NB)] for q in range(N_HID)
    ]


def from_partner(value, m):
    return lax.ppermute(value, "hid", [(i, i ^ m) for i in range(N_HID)])


def exchange(rows):
    pieces = rows.reshape(NB, rows.shape[0] // NB, LANES)
    pieces = lax.all_to_all(
        pieces, ("blk", "hid"), 0, 0, tiled=True, axis_index_groups=token_groups()
    )
    return pieces.reshape(rows.shape)


def dot(a, b, dims):
    return lax.dot_general(a, b, (dims, ((), ())), preferred_element_type=jnp.float32)


def mm(a, b):
    return dot(a, b, ((1,), (0,)))


def sum_over_hid(part):
    got = [from_partner(part, m) for m in (1, 2, 3)]
    return (part + got[0]) + (got[1] + got[2])


def own_quarter():
    return lax.axis_index("hid") ^ (2 * (lax.axis_index("blk") % 2))


def put_pieces(spread, value, at):
    chunks = spread.shape[0] // BS
    for j in range(value.shape[1] // LANES):
        spread[pl.ds(at // LANES + j, BS, chunks), :] = value[:, j * LANES : (j + 1) * LANES]


def get_pieces(spread, at, size):
    chunks = spread.shape[0] // BS
    parts = [spread[pl.ds(at // LANES + j, BS, chunks), :] for j in range(size // LANES)]
    return jnp.concatenate(parts, axis=1).astype(jnp.bfloat16)


def send_out(spread, buffer, hbm, sems, first_sem):
    half = spread.shape[0] // 2
    copies = []
    for i in range(2):
        rows = pl.ds(i * half, half)
        buffer[rows, :] = spread[rows, :].astype(jnp.bfloat16)
        copies.append(pltpu.make_async_copy(buffer.at[rows], hbm.at[rows], sems.at[first_sem + i]))
        copies[-1].start()
    return copies


def first_kernel(
    x_hbm, first_hbm, up_hbm, down_hbm, order_hbm, out_hbm, packed_hbm, x_own_hbm, rows_hbm,
    x, first, spread, buffer, sems,
):
    count = x.shape[0]
    start = own_quarter() * count
    order_rows = rows_hbm.shape[0]
    steps = count // STEP
    units = up_hbm.shape[1]
    fetch_first = pltpu.make_async_copy(first_hbm, first, sems.at[steps])
    fetch_first.start()
    arrivals = []
    for i in range(steps):
        source = x_hbm.at[pl.ds(pl.multiple_of(start + i * STEP, STEP), STEP)]
        arrivals.append(pltpu.make_async_copy(source, x.at[pl.ds(i * STEP, STEP)], sems.at[i]))
        arrivals[-1].start()
    pack = [
        pltpu.make_async_copy(up_hbm.at[0], packed_hbm.at[pl.ds(0, units)], sems.at[steps + 1]),
        pltpu.make_async_copy(down_hbm.at[0], packed_hbm.at[pl.ds(units, units)], sems.at[steps + 2]),
        pltpu.make_async_copy(
            order_hbm.at[pl.ds(pl.multiple_of(own_quarter() * order_rows, order_rows), order_rows)],
            rows_hbm,
            sems.at[steps + 6],
        ),
    ]
    for copy in pack:
        copy.start()
    fetch_first.wait()
    first_t = first[0].T
    for i in range(steps):
        arrivals[i].wait()
        put_pieces(spread, dot(first_t, x[i * STEP : (i + 1) * STEP, :], ((1,), (1,))), i * STEP)
    copies = send_out(spread, buffer, out_hbm, sems, steps + 3)
    own = pltpu.make_async_copy(x, x_own_hbm, sems.at[steps + 5])
    own.start()
    for copy in pack + copies + [own]:
        copy.wait()


def unit_matrix():
    ids = lax.broadcasted_iota(jnp.int32, (BS, BS), 0)
    eye = (lax.broadcasted_iota(jnp.int32, (BS, BS), 1) == ids).astype(jnp.float32)
    return eye.astype(jnp.bfloat16)


def prepare_kernel(
    own_ref, far_ref, near_ref, other_ref, mix_ref, up_ref, down_t_ref, up_t_hbm, down_hbm, up_t, down, sems
):
    units = own_ref.shape[0] // 2
    refs = (own_ref, far_ref, near_ref, other_ref)
    ids = lax.broadcasted_iota(jnp.int32, (BS, BS), 0)
    one_hot = (mix_ref[...] == ids).astype(jnp.float32).astype(jnp.bfloat16)
    for i, ref in enumerate(refs):
        down[i * units : (i + 1) * units, :] = ref[units:, :]
    copies = [pltpu.make_async_copy(down, down_hbm, sems.at[0])]
    copies[0].start()
    up = jnp.concatenate([ref[0:units, :] for ref in refs])
    up_t[...] = dot(one_hot, up, ((1,), (1,))).astype(jnp.bfloat16)
    copies.append(pltpu.make_async_copy(up_t, up_t_hbm, sems.at[1]))
    copies[1].start()
    up_ref[...] = dot(up, one_hot, ((1,), (1,))).astype(jnp.bfloat16)
    down_t_ref[...] = dot(unit_matrix(), down[...], ((1,), (1,))).astype(jnp.bfloat16)
    for copy in copies:
        copy.wait()


def turn_kernel(in_ref, out_ref):
    out_ref[...] = dot(unit_matrix(), in_ref[...], ((1,), (1,))).astype(jnp.bfloat16)


def forward_kernel(
    in_ref, up_ref, down_t_ref, out_ref, slope_ref, hidden_ref, spread_in, spread
):
    spread_in[...] = in_ref[...].astype(jnp.float32)
    up = up_ref[...]
    down_t = down_t_ref[...]
    for at in range(0, hidden_ref.shape[1], STEP):
        preact = mm(up, get_pieces(spread_in, at, STEP))
        cdf = 0.5 * (1.0 + lax.erf(preact * (1.0 / math.sqrt(2.0))))
        dens = jnp.exp(-0.5 * preact * preact) * (1.0 / math.sqrt(2.0 * math.pi))
        hidden = (preact * cdf).astype(jnp.bfloat16)
        hidden_ref[:, at : at + STEP] = hidden
        slope_ref[:, at : at + STEP] = cdf + preact * dens
        put_pieces(spread, mm(down_t, hidden), at)
    out_ref[...] = spread[...].astype(jnp.bfloat16)


def error_kernel(scale, in_ref, last_ref, teacher_ref, out_ref, grad_ref, spread_in, spread):
    spread_in[...] = in_ref[...].astype(jnp.float32)
    last = last_ref[0]
    last_t = last.T
    grad_last = None
    for at in range(0, teacher_ref.shape[1], STEP):
        returned = get_pieces(spread_in, at, STEP)
        teacher = teacher_ref[:, at : at + STEP].astype(jnp.float32)
        err = ((mm(last_t, returned) - teacher) * scale).astype(jnp.bfloat16)
        put_pieces(spread, mm(last, err), at)
        part = dot(returned, err, ((1,), (1,)))
        grad_last = part if grad_last is None else grad_last + part
    out_ref[...] = spread[...].astype(jnp.bfloat16)
    grad_ref[...] = grad_last


def backward_kernel(
    in_ref, down_ref, up_t_ref, slope_ref, hidden_ref, out_hbm, grad_hbm, hidden_hbm,
    grad_ref, spread_in, spread, buffer, sems,
):
    copies = [pltpu.make_async_copy(hidden_ref, hidden_hbm, sems.at[2])]
    copies[0].start()
    spread_in[...] = in_ref[...].astype(jnp.float32)
    down = down_ref[...]
    up_t = up_t_ref[...]
    for i in range(grad_ref.shape[1] // STEP):
        columns = pl.ds(i * STEP, STEP)
        grad_hidden = mm(down, get_pieces(spread_in, i * STEP, STEP))
        grad = (grad_hidden * slope_ref[:, columns]).astype(jnp.bfloat16)
        grad_ref[:, columns] = grad
        copies.append(
            pltpu.make_async_copy(grad_ref.at[:, columns], grad_hbm.at[:, columns], sems.at[3 + i])
        )
        copies[-1].start()
        put_pieces(spread, mm(up_t, grad), i * STEP)
    for copy in send_out(spread, buffer, out_hbm, sems, 0) + copies:
        copy.wait()


def weights_kernel(
    arrived_hbm, grad_arrived_ref, hidden_hbm, grad_hbm, last_ref, mine_ref, theirs_ref,
    arrived, hidden, grad, spread_in, sems,
):
    units, count = hidden.shape
    half = units // 2
    copies = [
        pltpu.make_async_copy(hidden_hbm, hidden, sems.at[0]),
        pltpu.make_async_copy(arrived_hbm, arrived, sems.at[1]),
        pltpu.make_async_copy(grad_hbm, grad, sems.at[2]),
    ]
    for copy in copies:
        copy.start()

    def product(left):
        return dot(left[...], get_pieces(spread_in, 0, count), ((1,), (1,)))

    mine_ref[units:, :] = last_ref[...]
    theirs_ref[units:, :] = last_ref[...]
    spread_in[...] = grad_arrived_ref[...].astype(jnp.float32)
    copies[0].wait()
    down = product(hidden)
    mine_ref[half:units, :] = down[:half]
    theirs_ref[half:units, :] = down[half:]
    copies[1].wait()
    spread_in[...] = arrived[...].astype(jnp.float32)
    copies[2].wait()
    up = product(grad)
    mine_ref[0:half, :] = up[:half]
    theirs_ref[0:half, :] = up[half:]


def chip_sum_kernel(mine_ref, got_ref, mine_out, theirs_out):
    quarter = (mine_ref.shape[0] - BS) // 4
    total = mine_ref[...] + got_ref[...]
    mine_out[0:quarter, :] = total[0:quarter]
    theirs_out[0:quarter, :] = total[quarter : 2 * quarter]
    mine_out[quarter : 2 * quarter, :] = total[2 * quarter : 3 * quarter]
    theirs_out[quarter : 2 * quarter, :] = total[3 * quarter : 4 * quarter]
    mine_out[2 * quarter :, :] = total[4 * quarter :]
    theirs_out[2 * quarter :, :] = total[4 * quarter :]


def totals_kernel(mine_ref, got_ref, mix_ref, up_ref, down_ref, last_ref):
    quarter = up_ref.shape[1]
    total = mine_ref[...] + got_ref[...]
    ids = lax.broadcasted_iota(jnp.int32, (BS, BS), 0)
    one_hot = (mix_ref[...] == ids).astype(jnp.float32)
    up_ref[0] = jnp.dot(
        total[0:quarter], one_hot, precision=lax.Precision.HIGHEST, preferred_element_type=jnp.float32
    )
    down_ref[0] = total[quarter : 2 * quarter]
    last_ref[0] = total[2 * quarter :]


def last_kernel(in_ref, x_ref, out_ref, spread_in):
    spread_in[...] = in_ref[...].astype(jnp.float32)
    grad = get_pieces(spread_in, 0, x_ref.shape[0])
    out_ref[...] = mm(grad, x_ref[...]).T


VMEM = pl.BlockSpec(memory_space=pltpu.VMEM)
HBM = pl.BlockSpec(memory_space=pltpu.HBM)
BF16 = jnp.bfloat16
F32 = jnp.float32


def call(kernel, ins, outs, scratch, flops, in_specs=None, out_specs=None, pin=True):
    moved = sum(a.size * a.dtype.itemsize for a in ins) + sum(
        math.prod(o.shape) * o.dtype.itemsize for o in outs
    )
    if in_specs:
        ins = [
            pltpu.with_memory_space_constraint(a, pltpu.HBM) if spec is HBM else a
            for a, spec in zip(ins, in_specs)
        ]
    places = out_specs or [VMEM] * len(outs)
    if pin:
        outs = tuple(
            (pltpu.HBM if spec is HBM else pltpu.VMEM)(o.shape, o.dtype) for o, spec in zip(outs, places)
        )
    return pl.pallas_call(
        kernel,
        out_shape=outs,
        in_specs=in_specs or [VMEM] * len(ins),
        out_specs=out_specs or [VMEM] * len(outs),
        scratch_shapes=scratch,
        compiler_params=pltpu.CompilerParams(vmem_limit_bytes=16 * 1024 * 1024),
        cost_estimate=pl.CostEstimate(flops=flops, bytes_accessed=moved, transcendentals=0),
    )(*ins)


def local(inputs, targets, row_order, mix_order, first_factor, up_factor, down_factor, last_factor):
    tokens = inputs.shape[0]
    count = tokens // N_HID
    steps = count // STEP
    piece_rows = BS * count // LANES
    loss_scale = 1.0 / math.sqrt(tokens)
    quarter_units = up_factor.shape[1]
    units = quarter_units * N_HID
    mix_row = mix_order[None, :]
    shape = jax.ShapeDtypeStruct
    pieces = shape((piece_rows, LANES), BF16)
    spread = pltpu.VMEM((piece_rows, LANES), F32)
    buffer = pltpu.VMEM((piece_rows, LANES), BF16)
    flops = 2 * units * BS * count
    small = 2 * BS * BS * count
    two_sems = pltpu.SemaphoreType.DMA((2,))

    first_out, weights, x_own, rows = call(
        first_kernel,
        (inputs, first_factor, up_factor, down_factor, row_order.reshape(-1, LANES)),
        (
            pieces,
            shape((2 * quarter_units, BS), BF16),
            shape((count, BS), BF16),
            shape((count // LANES, LANES), jnp.int32),
        ),
        [
            pltpu.VMEM((count, BS), BF16),
            pltpu.VMEM((1, BS, BS), BF16),
            spread,
            buffer,
            pltpu.SemaphoreType.DMA((steps + 7,)),
        ],
        small,
        [HBM] * 5,
        [HBM] * 4,
    )
    far = from_partner(weights, 2)
    arrived = exchange(first_out)

    teacher = targets.at[rows.reshape(count)].get(mode="promise_in_bounds")
    (teacher_t,) = call(turn_kernel, (teacher,), (shape((BS, count), BF16),), [], small)
    up_mixed, down_t, up_mixed_t, down = call(
        prepare_kernel,
        (weights, far, from_partner(weights, 1), from_partner(weights, 3), mix_row),
        (
            shape((units, BS), BF16),
            shape((BS, units), BF16),
            shape((BS, units), BF16),
            shape((units, BS), BF16),
        ),
        [pltpu.VMEM((BS, units), BF16), pltpu.VMEM((units, BS), BF16), two_sems],
        small,
        out_specs=[VMEM, VMEM, HBM, HBM],
    )
    teacher_t, arrived = lax.optimization_barrier((teacher_t, arrived))

    summed, slope, hidden = call(
        forward_kernel,
        (arrived, up_mixed, down_t),
        (pieces, shape((units, count), F32), shape((units, count), BF16)),
        [spread, spread],
        2 * flops,
    )
    returned = exchange(summed)

    grad_returned, grad_last = call(
        functools.partial(error_kernel, loss_scale),
        (returned, last_factor, teacher_t),
        (pieces, shape((BS, BS), F32)),
        [spread, spread],
        3 * small,
    )
    grad_arrived = exchange(grad_returned)

    grad_grouped, grad_preact, hidden = call(
        backward_kernel,
        (grad_arrived, down, up_mixed_t, slope, hidden),
        (pieces, shape((units, count), BF16), shape((units, count), BF16)),
        [
            pltpu.VMEM((units, count), BF16),
            spread,
            spread,
            buffer,
            pltpu.SemaphoreType.DMA((steps + 3,)),
        ],
        2 * flops,
        out_specs=[HBM, HBM, HBM],
    )
    grad_first_out = exchange(grad_grouped)

    half_rows = shape((units + BS, BS), F32)
    mine, theirs = call(
        weights_kernel,
        (arrived, grad_arrived, hidden, grad_preact, grad_last),
        (half_rows, half_rows),
        [
            buffer,
            pltpu.VMEM((units, count), BF16),
            pltpu.VMEM((units, count), BF16),
            spread,
            pltpu.SemaphoreType.DMA((3,)),
        ],
        2 * flops,
        [HBM, VMEM, HBM, HBM, VMEM],
    )
    quarter_rows = shape((units // 2 + BS, BS), F32)
    mine, theirs = call(
        chip_sum_kernel, (mine, from_partner(theirs, 1)), (quarter_rows, quarter_rows), [], 0
    )
    factor_grad = shape((1, quarter_units, BS), F32)
    grad_up, grad_down, grad_last = call(
        totals_kernel,
        (mine, from_partner(theirs, 2), mix_row),
        (factor_grad, factor_grad, shape((1, BS, BS), F32)),
        [],
        0,
        pin=False,
    )

    (grad_first,) = call(
        last_kernel, (grad_first_out, x_own), (shape((BS, BS), F32),), [spread], small
    )
    grad_first = sum_over_hid(grad_first)
    return (grad_first[None], grad_up, grad_down, grad_last)


def solution(mesh):
    placed = (
        P(None, "blk"),
        P(None, "blk"),
        P(),
        P(),
        P("blk", None, None),
        P("blk", "hid", None),
        P("blk", "hid", None),
        P("blk", None, None),
    )
    return jax.shard_map(
        local,
        mesh=mesh,
        in_specs=placed,
        out_specs=(
            P("blk", None, None),
            P("blk", "hid", None),
            P("blk", "hid", None),
            P("blk", None, None),
        ),
        check_vma=False,
    )
```

time: 114 us -> 101 us (0.89)
  local copies, waits for them, and re-layouts: 14.9 us -> 3.25 us
  blocking collectives: 42.3 us -> 37.5 us
  waiting for transfers between devices: 10.1 us -> 13.5 us
  starting transfers between devices: 34 us -> 31.6 us
  Pallas kernels: 10.1 us -> 12.4 us
    unnamed x44 -> x16, local copies, waits for them, and re-layouts: 11.7 us -> 0.04 us
    all_to_all x2, blocking collectives: 42.3 us -> 37.5 us  [exchange(): lax.all_to_all(pieces, ('blk', 'hid'), 0, 0, tiled=True, axis_index_group...]
    all_to_all x2, waiting for transfers between devices: 6.41 us -> 9.88 us  [exchange(): lax.all_to_all(pieces, ('blk', 'hid'), 0, 0, tiled=True, axis_index_group...]
    pallas_call x9 -> x10, Pallas kernels: 10.1 us -> 12.4 us  [call(): pl.pallas_call(kernel, out_shape=outs, in_specs=in_specs or [VMEM] * len(...]
    ppermute x11 -> x8, starting transfers between devices: 12.3 us -> 10.4 us  [from_partner(): return lax.ppermute(value, 'hid', [(i, i ^ m) for i in range(N_HID)])]
    ppermute x11 -> x8, waiting for transfers between devices: 3.67 us -> 3.66 us  [from_partner(): return lax.ppermute(value, 'hid', [(i, i ^ m) for i in range(N_HID)])]
  transfers between devices with their start and end apart: 13 -> 10, of which waited for: 3 -> 4; matrix products, arithmetic and copies ran while one was open for 3% -> 4% of each run, Pallas kernels for 2% -> 5%
where the time goes in v4:
time: 101 us; the launch traced here: 100 us
  blocking collectives  37.5 us (37%)
  starting transfers between devices  31.6 us (31%)
  waiting for transfers between devices  13.5 us (13%)
  Pallas kernels  12.4 us (12%)
  local copies, waits for them, and re-layouts  3.25 us (3%)
  other arithmetic  1.34 us (1%)
    all_to_all x2, blocking collectives, exchange(): lax.all_to_all(pieces, ('blk', 'hid'), 0, 0, tiled=True, axis_index_group...  37.5 us
    all_to_all x2, starting transfers between devices, exchange(): lax.all_to_all(pieces, ('blk', 'hid'), 0, 0, tiled=True, axis_index_group...  21.1 us
    pallas_call x10, Pallas kernels, call(): pl.pallas_call(kernel, out_shape=outs, in_specs=in_specs or [VMEM] * len(...  12.4 us
    ppermute x8, starting transfers between devices, from_partner(): return lax.ppermute(value, 'hid', [(i, i ^ m) for i in range(N_HID)])  10.4 us
    all_to_all x2, waiting for transfers between devices, exchange(): lax.all_to_all(pieces, ('blk', 'hid'), 0, 0, tiled=True, axis_index_group...  9.88 us
    ppermute x8, waiting for transfers between devices, from_partner(): return lax.ppermute(value, 'hid', [(i, i ^ m) for i in range(N_HID)])  3.66 us
    gather x1, local copies, waits for them, and re-layouts, local(): teacher = targets.at[rows.reshape(count)].get(mode='promise_in_bounds')  3.21 us
  transfers between devices with their start and end apart: 10, of which 4 were waited for; matrix products, arithmetic and copies ran while one was open for 4% of the time, Pallas kernels for 5%

profile of v4, /device:TPU:1, one launch (start us, length us, event | category | flops | bytes accessed | tf_op | source)
XLA Modules:
  0.0 100.5 jit_solution(7125930857990951246)
XLA Ops:
  0.6 3.1 %shard_map.111 = (bf16[1024,128]{1,0:T(8,128)(2,1)}, bf16[224,128]{1,0:T(8,128)(2,1)}, bf16[1024,128]{1,0:T(8,128)(2,1)}, s32[8,128]{1,0:T(8,128)}) custom-call(bf16[4096,128]{1,0:T(8,128)(2,1)} %x_hbm.1, bf16[1,128,128]{2,1,0:T(8,128)(2,1)} %first_hbm.1, bf16[1,112,128]{2,1,0:T(8,128)(2,1)} %up_hbm.1, bf16[1,112,128]{2,1,0:T(8,128)(2,1)} %down_hbm.1, ...), custom_call_target="tpu_custom_call" | custom-call | flops 33554432 | bytes 1740800 | tf_op jit(solution)/shard_map/pallas_call | solution.py:283
  3.8 15.1 %all-to-all-start = ((bf16[64,16,128]{2,1,0:T(8,128)(2,1)}), bf16[64,16,128]{2,1,0:T(8,128)(2,1)S(1)}, u32[]{:S(2)}, u32[]{:S(2)}) async-start(bf16[64,16,128]{2,1,0:T(8,128)(2,1)} %bitcast.24), calls=%async_computation | async-start | bytes 524288 | tf_op jit(solution)/shard_map/all_to_all | solution.py:30
  18.9 0.8 collective-permute-start.2
  19.6 0.4 collective-permute-start.1
  20.0 1.3 %collective-permute-start = (bf16[224,128]{1,0:T(8,128)(2,1)}, bf16[224,128]{1,0:T(8,128)(2,1)S(1)}, u32[]{:S(2)}, u32[]{:S(2)}) collective-permute-start(bf16[224,128]{1,0:T(8,128)(2,1)} %get-tuple-element.32.own_ref), channel_id=1, source_target_pairs={{0,2},{1,3},{2,0},{3,1},{4,6},{5,7},{6,4},{7,5},{8,10},{9,11},{10,... | collective-permute-start | bytes 172040 | tf_op jit(solution)/shard_map/ppermute | solution.py:25
  21.3 0.7 compare_select_fusion
  22.0 3.2 %gather_fusion = bf16[1024,128]{1,0:T(8,128)(2,1)S(1)} fusion(bf16[4096,128]{1,0:T(8,128)(2,1)S(1)} %copy-done, s32[1024]{0:T(1024)S(1)} %broadcast_clamp_fusion), kind=kCustom, calls=%fused_computation | custom fusion | bytes 528384 | tf_op jit(solution)/shard_map/gather | solution.py:334
  25.5 0.9 shard_map.113
  26.4 4.3 %all-to-all-done = bf16[64,16,128]{2,1,0:T(8,128)(2,1)S(1)} async-done(((bf16[64,16,128]{2,1,0:T(8,128)(2,1)}), bf16[64,16,128]{2,1,0:T(8,128)(2,1)S(1)}, u32[]{:S(2)}, u32[]{:S(2)}) %all-to-all-start) | async-done | bytes 262176 | tf_op jit(solution)/shard_map/all_to_all | solution.py:30
  30.7 1.6 %shard_map.114 = (bf16[1024,128]{1,0:T(8,128)(2,1)S(1)}, f32[448,1024]{1,0:T(8,128)S(1)}, bf16[448,1024]{1,0:T(8,128)(2,1)S(1)}) custom-call(bf16[1024,128]{1,0:T(8,128)(2,1)S(1)} %bitcast.16, bf16[448,128]{1,0:T(8,128)(2,1)S(1)} %get-tuple-element.33.up_ref, bf16[128,448]{1,0:T(8,128)(2,1)S(1)} %get-tuple-element.34.down_t_ref), custom_call_target="tpu_custom_call" | custom-call | flops 234881024 | bytes 3506176 | tf_op jit(solution)/shard_map/pallas_call | solution.py:283
  32.3 19.5 %all_to_all.20 = bf16[64,16,128]{2,1,0:T(8,128)(2,1)S(1)} all-to-all(bf16[64,16,128]{2,1,0:T(8,128)(2,1)S(1)} %bitcast.20), channel_id=1, replica_groups={{0,6,8,14,16,22,24,30,32,38,40,46,48,54,56,62,64,70,72,78,80,86,88,94,9..., dimensions={0} | all-to-all | bytes 524288 | tf_op jit(solution)/shard_map/all_to_all | solution.py:30
  51.8 0.9 shard_map.115
  52.7 18.1 %all_to_all.21 = bf16[64,16,128]{2,1,0:T(8,128)(2,1)S(1)} all-to-all(bf16[64,16,128]{2,1,0:T(8,128)(2,1)S(1)} %bitcast.21), channel_id=1, replica_groups={{0,6,8,14,16,22,24,30,32,38,40,46,48,54,56,62,64,70,72,78,80,86,88,94,9..., dimensions={0} | all-to-all | bytes 524288 | tf_op jit(solution)/shard_map/all_to_all | solution.py:30
  70.7 2.0 %shard_map.116 = (bf16[1024,128]{1,0:T(8,128)(2,1)}, bf16[448,1024]{1,0:T(8,128)(2,1)}, bf16[448,1024]{1,0:T(8,128)(2,1)}) custom-call(bf16[1024,128]{1,0:T(8,128)(2,1)S(1)} %bitcast.14, bf16[448,128]{1,0:T(8,128)(2,1)S(1)} %copy-done.4, bf16[128,448]{1,0:T(8,128)(2,1)S(1)} %copy-done.3, f32[448,1024]{1,0:T(8,128)S(1)} %get-tuple-element.40.slope_ref, ...), custom_call_target="tpu_custom_call" | custom-call | flops 234881024 | bytes 5341184 | tf_op jit(solution)/shard_map/pallas_call | solution.py:283
  72.8 6.0 %all-to-all-start.3 = ((bf16[64,16,128]{2,1,0:T(8,128)(2,1)}), bf16[64,16,128]{2,1,0:T(8,128)(2,1)S(1)}, u32[]{:S(2)}, u32[]{:S(2)}) async-start(bf16[64,16,128]{2,1,0:T(8,128)(2,1)} %bitcast.25), calls=%async_computation.3 | async-start | bytes 524288 | tf_op jit(solution)/shard_map/all_to_all | solution.py:30
  78.8 2.5 %shard_map.118 = (f32[576,128]{1,0:T(8,128)S(1)}, f32[576,128]{1,0:T(8,128)S(1)}) custom-call(bf16[1024,128]{1,0:T(8,128)(2,1)} %bitcast.17, bf16[1024,128]{1,0:T(8,128)(2,1)S(1)} %bitcast.15, bf16[448,1024]{1,0:T(8,128)(2,1)} %get-tuple-element.44.hidden_hbm, bf16[448,1024]{1,0:T(8,128)(2,1)} %get-tuple-element.45.grad_hbm, ...), custom_call_target="tpu_custom_call" | custom-call | flops 234881024 | bytes 3014656 | tf_op jit(solution)/shard_map/pallas_call | solution.py:283
  81.3 2.4 %collective-permute-start.6 = (f32[576,128]{1,0:T(8,128)S(1)}, f32[576,128]{1,0:T(8,128)S(1)}, u32[]{:S(2)}, u32[]{:S(2)}) collective-permute-start(f32[576,128]{1,0:T(8,128)S(1)} %get-tuple-element.48), channel_id=1, source_target_pairs={{0,1},{1,0},{2,3},{3,2},{4,5},{5,4},{6,7},{7,6},{8,9},{9,8},{10,11... | collective-permute-start | bytes 884744 | tf_op jit(solution)/shard_map/ppermute | solution.py:25
  83.8 1.2 %collective-permute-done.6.got_ref = f32[576,128]{1,0:T(8,128)S(1)} collective-permute-done((f32[576,128]{1,0:T(8,128)S(1)}, f32[576,128]{1,0:T(8,128)S(1)}, u32[]{:S(2)}, u32[]{:S(2)}) %collective-permute-start.6) | collective-permute-done | bytes 294944 | tf_op jit(solution)/shard_map/ppermute | solution.py:25
  85.1 5.6 %all-to-all-done.3 = bf16[64,16,128]{2,1,0:T(8,128)(2,1)S(1)} async-done(((bf16[64,16,128]{2,1,0:T(8,128)(2,1)}), bf16[64,16,128]{2,1,0:T(8,128)(2,1)S(1)}, u32[]{:S(2)}, u32[]{:S(2)}) %all-to-all-start.3) | async-done | bytes 262176 | tf_op jit(solution)/shard_map/all_to_all | solution.py:30
  90.7 0.3 shard_map.117
  91.3 5.3 %collective-permute-start.4 = (f32[128,128]{1,0:T(8,128)S(1)}, f32[128,128]{1,0:T(8,128)S(1)}, u32[]{:S(2)}, u32[]{:S(2)}) collective-permute-start(f32[128,128]{1,0:T(8,128)S(1)} %shard_map.117), channel_id=1, source_target_pairs={{0,2},{1,3},{2,0},{3,1},{4,6},{5,7},{6,4},{7,5},{8,10},{9,11},{10,... | collective-permute-start | bytes 196616 | tf_op jit(solution)/shard_map/ppermute | solution.py:25
  96.5 0.8 shard_map.120
  97.4 2.4 %collective-permute-done.4 = f32[128,128]{1,0:T(8,128)S(1)} collective-permute-done((f32[128,128]{1,0:T(8,128)S(1)}, f32[128,128]{1,0:T(8,128)S(1)}, u32[]{:S(2)}, u32[]{:S(2)}) %collective-permute-start.4) | collective-permute-done | bytes 65568 | tf_op jit(solution)/shard_map/ppermute | solution.py:25
  99.8 0.6 add_bitcast_fusion
  (28 shorter events, 0.6 us)
Async XLA Ops:
  0.6 21.3 %copy-start = (bf16[4096,128]{1,0:T(8,128)(2,1)S(1)}, bf16[4096,128]{1,0:T(8,128)(2,1)}, u32[]{:S(2)}) copy-start(bf16[4096,128]{1,0:T(8,128)(2,1)} %param.9) | copy-start | bytes 3145732
  3.7 21.7 %copy-start.5 = (bf16[224,128]{1,0:T(8,128)(2,1)S(1)}, bf16[224,128]{1,0:T(8,128)(2,1)}, u32[]{:S(2)}) copy-start(bf16[224,128]{1,0:T(8,128)(2,1)} %get-tuple-element.32.own_ref) | copy-start | bytes 172036
  3.8 21.7 %copy-start.7 = (s32[128]{0:T(128)S(1)}, s32[128]{0:T(128)}, u32[]{:S(2)}) copy-start(s32[128]{0:T(128)} %param.11) | copy-start | bytes 1540
  3.8 26.9 %all-to-all-start = ((bf16[64,16,128]{2,1,0:T(8,128)(2,1)}), bf16[64,16,128]{2,1,0:T(8,128)(2,1)S(1)}, u32[]{:S(2)}, u32[]{:S(2)}) async-start(bf16[64,16,128]{2,1,0:T(8,128)(2,1)} %bitcast.24), calls=%async_computation | async-start | bytes 524288 | tf_op jit(solution)/shard_map/all_to_all | solution.py:30
  18.9 6.6 %collective-permute-start.2 = (bf16[224,128]{1,0:T(8,128)(2,1)}, bf16[224,128]{1,0:T(8,128)(2,1)S(1)}, u32[]{:S(2)}, u32[]{:S(2)}) collective-permute-start(bf16[224,128]{1,0:T(8,128)(2,1)} %get-tuple-element.32.own_ref), channel_id=1, source_target_pairs={{0,3},{1,2},{2,1},{3,0},{4,7},{5,6},{6,5},{7,4},{8,11},{9,10},{10,... | collective-permute-start | bytes 172040 | tf_op jit(solution)/shard_map/ppermute | solution.py:25
  19.6 5.8 %collective-permute-start.1 = (bf16[224,128]{1,0:T(8,128)(2,1)}, bf16[224,128]{1,0:T(8,128)(2,1)S(1)}, u32[]{:S(2)}, u32[]{:S(2)}) collective-permute-start(bf16[224,128]{1,0:T(8,128)(2,1)} %get-tuple-element.32.own_ref), channel_id=1, source_target_pairs={{0,1},{1,0},{2,3},{3,2},{4,5},{5,4},{6,7},{7,6},{8,9},{9,8},{10,11... | collective-permute-start | bytes 172040 | tf_op jit(solution)/shard_map/ppermute | solution.py:25
  20.0 5.4 %collective-permute-start = (bf16[224,128]{1,0:T(8,128)(2,1)}, bf16[224,128]{1,0:T(8,128)(2,1)S(1)}, u32[]{:S(2)}, u32[]{:S(2)}) collective-permute-start(bf16[224,128]{1,0:T(8,128)(2,1)} %get-tuple-element.32.own_ref), channel_id=1, source_target_pairs={{0,2},{1,3},{2,0},{3,1},{4,6},{5,7},{6,4},{7,5},{8,10},{9,11},{10,... | collective-permute-start | bytes 172040 | tf_op jit(solution)/shard_map/ppermute | solution.py:25
  22.0 29.8 %copy-start.6 = (bf16[1,128,128]{2,1,0:T(8,128)(2,1)S(1)}, bf16[1,128,128]{2,1,0:T(8,128)(2,1)}, u32[]{:S(2)}) copy-start(bf16[1,128,128]{2,1,0:T(8,128)(2,1)} %last_ref.1) | copy-start | bytes 98308
  26.4 44.4 %copy-start.3 = (bf16[128,448]{1,0:T(8,128)(2,1)S(1)}, bf16[128,448]{1,0:T(8,128)(2,1)}, u32[]{:S(2)}) copy-start(bf16[128,448]{1,0:T(8,128)(2,1)} %get-tuple-element.39.up_t_ref) | copy-start | bytes 344068
  26.4 44.3 %copy-start.4 = (bf16[448,128]{1,0:T(8,128)(2,1)S(1)}, bf16[448,128]{1,0:T(8,128)(2,1)}, u32[]{:S(2)}) copy-start(bf16[448,128]{1,0:T(8,128)(2,1)} %get-tuple-element.38.down_ref) | copy-start | bytes 344068
  30.7 42.1 %copy-start.1 = (bf16[64,16,128]{2,1,0:T(8,128)(2,1)}, bf16[64,16,128]{2,1,0:T(8,128)(2,1)S(1)}, u32[]{:S(2)}) copy-start(bf16[64,16,128]{2,1,0:T(8,128)(2,1)S(1)} %all-to-all-done) | copy-start | bytes 786436
  72.8 17.9 %copy-start.2 = (bf16[1024,128]{1,0:T(8,128)(2,1)S(1)}, bf16[1024,128]{1,0:T(8,128)(2,1)}, u32[]{:S(2)}) copy-start(bf16[1024,128]{1,0:T(8,128)(2,1)} %get-tuple-element.43.x_ref) | copy-start | bytes 786436
  72.8 17.9 %all-to-all-start.3 = ((bf16[64,16,128]{2,1,0:T(8,128)(2,1)}), bf16[64,16,128]{2,1,0:T(8,128)(2,1)S(1)}, u32[]{:S(2)}, u32[]{:S(2)}) async-start(bf16[64,16,128]{2,1,0:T(8,128)(2,1)} %bitcast.25), calls=%async_computation.3 | async-start | bytes 524288 | tf_op jit(solution)/shard_map/all_to_all | solution.py:30
  81.3 3.7 %collective-permute-start.6 = (f32[576,128]{1,0:T(8,128)S(1)}, f32[576,128]{1,0:T(8,128)S(1)}, u32[]{:S(2)}, u32[]{:S(2)}) collective-permute-start(f32[576,128]{1,0:T(8,128)S(1)} %get-tuple-element.48), channel_id=1, source_target_pairs={{0,1},{1,0},{2,3},{3,2},{4,5},{5,4},{6,7},{7,6},{8,9},{9,8},{10,11... | collective-permute-start | bytes 884744 | tf_op jit(solution)/shard_map/ppermute | solution.py:25
  85.0 11.5 %collective-permute-start.7 = (f32[352,128]{1,0:T(8,128)S(1)}, f32[352,128]{1,0:T(8,128)S(1)}, u32[]{:S(2)}, u32[]{:S(2)}) collective-permute-start(f32[352,128]{1,0:T(8,128)S(1)} %get-tuple-element.50), channel_id=1, source_target_pairs={{0,2},{1,3},{2,0},{3,1},{4,6},{5,7},{6,4},{7,5},{8,10},{9,11},{10,... | collective-permute-start | bytes 540680 | tf_op jit(solution)/shard_map/ppermute | solution.py:25
  91.0 6.3 %collective-permute-start.5 = (f32[128,128]{1,0:T(8,128)S(1)}, f32[128,128]{1,0:T(8,128)S(1)}, u32[]{:S(2)}, u32[]{:S(2)}) collective-permute-start(f32[128,128]{1,0:T(8,128)S(1)} %shard_map.117), channel_id=1, source_target_pairs={{0,3},{1,2},{2,1},{3,0},{4,7},{5,6},{6,5},{7,4},{8,11},{9,10},{10,... | collective-permute-start | bytes 196616 | tf_op jit(solution)/shard_map/ppermute | solution.py:25
  91.3 8.6 %collective-permute-start.4 = (f32[128,128]{1,0:T(8,128)S(1)}, f32[128,128]{1,0:T(8,128)S(1)}, u32[]{:S(2)}, u32[]{:S(2)}) collective-permute-start(f32[128,128]{1,0:T(8,128)S(1)} %shard_map.117), channel_id=1, source_target_pairs={{0,2},{1,3},{2,0},{3,1},{4,6},{5,7},{6,4},{7,5},{8,10},{9,11},{10,... | collective-permute-start | bytes 196616 | tf_op jit(solution)/shard_map/ppermute | solution.py:25
  96.5 3.3 %collective-permute-start.3 = (f32[128,128]{1,0:T(8,128)S(1)}, f32[128,128]{1,0:T(8,128)S(1)}, u32[]{:S(2)}, u32[]{:S(2)}) collective-permute-start(f32[128,128]{1,0:T(8,128)S(1)} %shard_map.117), channel_id=1, source_target_pairs={{0,1},{1,0},{2,3},{3,2},{4,5},{5,4},{6,7},{7,6},{8,9},{9,8},{10,11... | collective-permute-start | bytes 196616 | tf_op jit(solution)/shard_map/ppermute | solution.py:25

commit v5 on v4

--- a/solution.py
+++ b/solution.py
@@ -12,7 +12,7 @@
 NB = 64
 N_HID = 4
 LANES = 128
-STEP = 256
+STEP = 1024
 
 
 def token_groups():
@@ -42,8 +42,8 @@
 
 
 def sum_over_hid(part):
-    got = [from_partner(part, m) for m in (1, 2, 3)]
-    return (part + got[0]) + (got[1] + got[2])
+    got = [from_partner(part, m).astype(jnp.float32) for m in (1, 2, 3)]
+    return (part.astype(jnp.float32) + got[0]) + (got[1] + got[2])
 
 
 def own_quarter():
@@ -102,12 +102,12 @@
         copy.start()
     fetch_first.wait()
     first_t = first[0].T
-    for i in range(steps):
-        arrivals[i].wait()
-        put_pieces(spread, dot(first_t, x[i * STEP : (i + 1) * STEP, :], ((1,), (1,))), i * STEP)
-    copies = send_out(spread, buffer, out_hbm, sems, steps + 3)
+    for arrival in arrivals:
+        arrival.wait()
     own = pltpu.make_async_copy(x, x_own_hbm, sems.at[steps + 5])
     own.start()
+    put_pieces(spread, dot(first_t, x[...], ((1,), (1,))), 0)
+    copies = send_out(spread, buffer, out_hbm, sems, steps + 3)
     for copy in pack + copies + [own]:
         copy.wait()
 
@@ -257,7 +257,7 @@
 def last_kernel(in_ref, x_ref, out_ref, spread_in):
     spread_in[...] = in_ref[...].astype(jnp.float32)
     grad = get_pieces(spread_in, 0, x_ref.shape[0])
-    out_ref[...] = mm(grad, x_ref[...]).T
+    out_ref[...] = mm(grad, x_ref[...]).T.astype(jnp.bfloat16)
 
 
 VMEM = pl.BlockSpec(memory_space=pltpu.VMEM)
@@ -331,11 +331,13 @@
     far = from_partner(weights, 2)
     arrived = exchange(first_out)
 
-    teacher = targets.at[rows.reshape(count)].get(mode="promise_in_bounds")
+    teacher = targets.at[rows.reshape(count)].get(mode="promise_in_bounds", wrap_negative_indices=False)
+    weights, far, teacher = lax.optimization_barrier((weights, far, teacher))
+    near, other = from_partner(weights, 1), from_partner(far, 1)
     (teacher_t,) = call(turn_kernel, (teacher,), (shape((BS, count), BF16),), [], small)
     up_mixed, down_t, up_mixed_t, down = call(
         prepare_kernel,
-        (weights, far, from_partner(weights, 1), from_partner(weights, 3), mix_row),
+        (weights, far, near, other, mix_row),
         (
             shape((units, BS), BF16),
             shape((BS, units), BF16),
@@ -412,7 +414,7 @@
     )
 
     (grad_first,) = call(
-        last_kernel, (grad_first_out, x_own), (shape((BS, BS), F32),), [spread], small
+        last_kernel, (grad_first_out, x_own), (shape((BS, BS), BF16),), [spread], small
     )
     grad_first = sum_over_hid(grad_first)
     return (grad_first[None], grad_up, grad_down, grad_last)

time: 101 us -> 99.1 us (0.981)
  starting transfers between devices: 31.6 us -> 30.2 us
  Pallas kernels: 12.4 us -> 11.2 us
    ppermute x8, starting transfers between devices: 10.4 us -> 8.56 us  [from_partner(): return lax.ppermute(value, 'hid', [(i, i ^ m) for i in range(N_HID)])]
    pallas_call x10, Pallas kernels: 12.4 us -> 11.2 us  [call(): pl.pallas_call(kernel, out_shape=outs, in_specs=in_specs or [VMEM] * len(...]
  transfers between devices with their start and end apart: 10 -> 10, of which waited for: 4 -> 6; matrix products, arithmetic and copies ran while one was open for 4% -> 4% of each run, Pallas kernels for 5% -> 5%
where the time goes in v5:
time: 99.1 us; the launch traced here: 98.7 us
  blocking collectives  38.1 us (38%)
  starting transfers between devices  30.2 us (30%)
  waiting for transfers between devices  13.8 us (14%)
  Pallas kernels  11.2 us (11%)
  local copies, waits for them, and re-layouts  3.24 us (3%)
  other arithmetic  1.34 us (1%)
    all_to_all x2, blocking collectives, exchange(): lax.all_to_all(pieces, ('blk', 'hid'), 0, 0, tiled=True, axis_index_group...  38.1 us
    all_to_all x2, starting transfers between devices, exchange(): lax.all_to_all(pieces, ('blk', 'hid'), 0, 0, tiled=True, axis_index_group...  21.7 us
    pallas_call x10, Pallas kernels, call(): pl.pallas_call(kernel, out_shape=outs, in_specs=in_specs or [VMEM] * len(...  11.2 us
    all_to_all x2, waiting for transfers between devices, exchange(): lax.all_to_all(pieces, ('blk', 'hid'), 0, 0, tiled=True, axis_index_group...  10.4 us
    ppermute x8, starting transfers between devices, from_partner(): return lax.ppermute(value, 'hid', [(i, i ^ m) for i in range(N_HID)])  8.56 us
    ppermute x8, waiting for transfers between devices, from_partner(): return lax.ppermute(value, 'hid', [(i, i ^ m) for i in range(N_HID)])  3.4 us
    gather x1, local copies, waits for them, and re-layouts, local(): targets.at[rows.reshape(count)]  3.2 us
  transfers between devices with their start and end apart: 10, of which 6 were waited for; matrix products, arithmetic and copies ran while one was open for 4% of the time, Pallas kernels for 5%

profile of v5, /device:TPU:1, one launch (start us, length us, event | category | flops | bytes accessed | tf_op | source)
XLA Modules:
  0.0 98.7 jit_solution(3169962520331523418)
XLA Ops:
  0.6 3.1 %shard_map.111 = (bf16[1024,128]{1,0:T(8,128)(2,1)}, bf16[224,128]{1,0:T(8,128)(2,1)}, bf16[1024,128]{1,0:T(8,128)(2,1)}, s32[8,128]{1,0:T(8,128)}) custom-call(bf16[4096,128]{1,0:T(8,128)(2,1)} %x_hbm.1, bf16[1,128,128]{2,1,0:T(8,128)(2,1)} %first_hbm.1, bf16[1,112,128]{2,1,0:T(8,128)(2,1)} %up_hbm.1, bf16[1,112,128]{2,1,0:T(8,128)(2,1)} %down_hbm.1, ...), custom_call_target="tpu_custom_call" | custom-call | flops 33554432 | bytes 1740800 | tf_op jit(solution)/shard_map/pallas_call | solution.py:283
  3.7 15.1 %all-to-all-start = ((bf16[64,16,128]{2,1,0:T(8,128)(2,1)}), bf16[64,16,128]{2,1,0:T(8,128)(2,1)S(1)}, u32[]{:S(2)}, u32[]{:S(2)}) async-start(bf16[64,16,128]{2,1,0:T(8,128)(2,1)} %bitcast.24), calls=%async_computation | async-start | bytes 524288 | tf_op jit(solution)/shard_map/all_to_all | solution.py:30
  18.9 0.7 bitcast_clamp_fusion
  19.6 3.2 %gather_fusion = bf16[1024,128]{1,0:T(8,128)(2,1)S(1)} fusion(bf16[4096,128]{1,0:T(8,128)(2,1)S(1)} %copy-done, s32[1024]{0:T(1024)S(1)} %bitcast_clamp_fusion), kind=kCustom, calls=%fused_computation | custom fusion | bytes 528384 | tf_op jit(solution)/shard_map/gather | solution.py:334
  22.8 1.4 %collective-permute-start.1 = (bf16[224,128]{1,0:T(8,128)(2,1)S(1)}, bf16[224,128]{1,0:T(8,128)(2,1)S(1)}, u32[]{:S(2)}, u32[]{:S(2)}) collective-permute-start(bf16[224,128]{1,0:T(8,128)(2,1)S(1)} %copy-done.5), channel_id=1, source_target_pairs={{0,1},{1,0},{2,3},{3,2},{4,5},{5,4},{6,7},{7,6},{8,9},{9,8},{10,11... | collective-permute-start | bytes 172040 | tf_op jit(solution)/shard_map/ppermute | solution.py:25
  24.5 0.7 collective-permute-done.1.near_ref
  25.1 0.4 collective-permute-done.2.other_ref
  25.5 0.9 shard_map.113
  26.4 4.3 %all-to-all-done = bf16[64,16,128]{2,1,0:T(8,128)(2,1)S(1)} async-done(((bf16[64,16,128]{2,1,0:T(8,128)(2,1)}), bf16[64,16,128]{2,1,0:T(8,128)(2,1)S(1)}, u32[]{:S(2)}, u32[]{:S(2)}) %all-to-all-start) | async-done | bytes 262176 | tf_op jit(solution)/shard_map/all_to_all | solution.py:30
  30.7 1.2 %shard_map.114 = (bf16[1024,128]{1,0:T(8,128)(2,1)S(1)}, f32[448,1024]{1,0:T(8,128)S(1)}, bf16[448,1024]{1,0:T(8,128)(2,1)S(1)}) custom-call(bf16[1024,128]{1,0:T(8,128)(2,1)S(1)} %bitcast.16, bf16[448,128]{1,0:T(8,128)(2,1)S(1)} %get-tuple-element.39.up_ref, bf16[128,448]{1,0:T(8,128)(2,1)S(1)} %get-tuple-element.40.down_t_ref), custom_call_target="tpu_custom_call" | custom-call | flops 234881024 | bytes 3506176 | tf_op jit(solution)/shard_map/pallas_call | solution.py:283
  31.9 20.3 %all_to_all.20 = bf16[64,16,128]{2,1,0:T(8,128)(2,1)S(1)} all-to-all(bf16[64,16,128]{2,1,0:T(8,128)(2,1)S(1)} %bitcast.20), channel_id=1, replica_groups={{0,6,8,14,16,22,24,30,32,38,40,46,48,54,56,62,64,70,72,78,80,86,88,94,9..., dimensions={0} | all-to-all | bytes 524288 | tf_op jit(solution)/shard_map/all_to_all | solution.py:30
  52.2 0.6 shard_map.115
  52.8 17.8 %all_to_all.21 = bf16[64,16,128]{2,1,0:T(8,128)(2,1)S(1)} all-to-all(bf16[64,16,128]{2,1,0:T(8,128)(2,1)S(1)} %bitcast.21), channel_id=1, replica_groups={{0,6,8,14,16,22,24,30,32,38,40,46,48,54,56,62,64,70,72,78,80,86,88,94,9..., dimensions={0} | all-to-all | bytes 524288 | tf_op jit(solution)/shard_map/all_to_all | solution.py:30
  70.6 1.5 %shard_map.116 = (bf16[1024,128]{1,0:T(8,128)(2,1)}, bf16[448,1024]{1,0:T(8,128)(2,1)}, bf16[448,1024]{1,0:T(8,128)(2,1)}) custom-call(bf16[1024,128]{1,0:T(8,128)(2,1)S(1)} %bitcast.14, bf16[448,128]{1,0:T(8,128)(2,1)S(1)} %copy-done.4, bf16[128,448]{1,0:T(8,128)(2,1)S(1)} %copy-done.3, f32[448,1024]{1,0:T(8,128)S(1)} %get-tuple-element.46.slope_ref, ...), custom_call_target="tpu_custom_call" | custom-call | flops 234881024 | bytes 5341184 | tf_op jit(solution)/shard_map/pallas_call | solution.py:283
  72.2 6.6 %all-to-all-start.3 = ((bf16[64,16,128]{2,1,0:T(8,128)(2,1)}), bf16[64,16,128]{2,1,0:T(8,128)(2,1)S(1)}, u32[]{:S(2)}, u32[]{:S(2)}) async-start(bf16[64,16,128]{2,1,0:T(8,128)(2,1)} %bitcast.25), calls=%async_computation.3 | async-start | bytes 524288 | tf_op jit(solution)/shard_map/all_to_all | solution.py:30
  78.8 2.5 %shard_map.118 = (f32[576,128]{1,0:T(8,128)S(1)}, f32[576,128]{1,0:T(8,128)S(1)}) custom-call(bf16[1024,128]{1,0:T(8,128)(2,1)} %bitcast.17, bf16[1024,128]{1,0:T(8,128)(2,1)S(1)} %bitcast.15, bf16[448,1024]{1,0:T(8,128)(2,1)} %get-tuple-element.50.hidden_hbm, bf16[448,1024]{1,0:T(8,128)(2,1)} %get-tuple-element.51.grad_hbm, ...), custom_call_target="tpu_custom_call" | custom-call | flops 234881024 | bytes 3014656 | tf_op jit(solution)/shard_map/pallas_call | solution.py:283
  81.3 1.9 %collective-permute-start.6 = (f32[576,128]{1,0:T(8,128)S(1)}, f32[576,128]{1,0:T(8,128)S(1)}, u32[]{:S(2)}, u32[]{:S(2)}) collective-permute-start(f32[576,128]{1,0:T(8,128)S(1)} %get-tuple-element.54), channel_id=1, source_target_pairs={{0,1},{1,0},{2,3},{3,2},{4,5},{5,4},{6,7},{7,6},{8,9},{9,8},{10,11... | collective-permute-start | bytes 884744 | tf_op jit(solution)/shard_map/ppermute | solution.py:25
  83.1 1.2 %collective-permute-done.6.got_ref = f32[576,128]{1,0:T(8,128)S(1)} collective-permute-done((f32[576,128]{1,0:T(8,128)S(1)}, f32[576,128]{1,0:T(8,128)S(1)}, u32[]{:S(2)}, u32[]{:S(2)}) %collective-permute-start.6) | collective-permute-done | bytes 294944 | tf_op jit(solution)/shard_map/ppermute | solution.py:25
  84.5 6.1 %all-to-all-done.3 = bf16[64,16,128]{2,1,0:T(8,128)(2,1)S(1)} async-done(((bf16[64,16,128]{2,1,0:T(8,128)(2,1)}), bf16[64,16,128]{2,1,0:T(8,128)(2,1)S(1)}, u32[]{:S(2)}, u32[]{:S(2)}) %all-to-all-start.3) | async-done | bytes 262176 | tf_op jit(solution)/shard_map/all_to_all | solution.py:30
  90.9 0.7 collective-permute-start.5
  91.7 4.3 %collective-permute-start.4 = (bf16[128,128]{1,0:T(8,128)(2,1)S(1)}, bf16[128,128]{1,0:T(8,128)(2,1)S(1)}, u32[]{:S(2)}, u32[]{:S(2)}) collective-permute-start(bf16[128,128]{1,0:T(8,128)(2,1)S(1)} %shard_map.117), channel_id=1, source_target_pairs={{0,2},{1,3},{2,0},{3,1},{4,6},{5,7},{6,4},{7,5},{8,10},{9,11},{10,... | collective-permute-start | bytes 98312 | tf_op jit(solution)/shard_map/ppermute | solution.py:25
  96.0 0.8 shard_map.120
  96.8 1.2 %collective-permute-done.4 = bf16[128,128]{1,0:T(8,128)(2,1)S(1)} collective-permute-done((bf16[128,128]{1,0:T(8,128)(2,1)S(1)}, bf16[128,128]{1,0:T(8,128)(2,1)S(1)}, u32[]{:S(2)}, u32[]{:S(2)}) %collective-permute-start.4) | collective-permute-done | bytes 32800 | tf_op jit(solution)/shard_map/ppermute | solution.py:25
  98.0 0.6 add_bitcast_fusion
  (27 shorter events, 0.8 us)
Async XLA Ops:
  0.6 19.0 %copy-start = (bf16[4096,128]{1,0:T(8,128)(2,1)S(1)}, bf16[4096,128]{1,0:T(8,128)(2,1)}, u32[]{:S(2)}) copy-start(bf16[4096,128]{1,0:T(8,128)(2,1)} %param.9) | copy-start | bytes 3145732
  3.7 19.1 %copy-start.5 = (bf16[224,128]{1,0:T(8,128)(2,1)S(1)}, bf16[224,128]{1,0:T(8,128)(2,1)}, u32[]{:S(2)}) copy-start(bf16[224,128]{1,0:T(8,128)(2,1)} %get-tuple-element.37.own_ref) | copy-start | bytes 172036
  3.7 21.8 %copy-start.7 = (s32[128]{0:T(128)S(1)}, s32[128]{0:T(128)}, u32[]{:S(2)}) copy-start(s32[128]{0:T(128)} %param.11) | copy-start | bytes 1540
  3.7 26.9 %all-to-all-start = ((bf16[64,16,128]{2,1,0:T(8,128)(2,1)}), bf16[64,16,128]{2,1,0:T(8,128)(2,1)S(1)}, u32[]{:S(2)}, u32[]{:S(2)}) async-start(bf16[64,16,128]{2,1,0:T(8,128)(2,1)} %bitcast.24), calls=%async_computation | async-start | bytes 524288 | tf_op jit(solution)/shard_map/all_to_all | solution.py:30
  18.8 4.0 %collective-permute-start = (bf16[224,128]{1,0:T(8,128)(2,1)}, bf16[224,128]{1,0:T(8,128)(2,1)S(1)}, u32[]{:S(2)}, u32[]{:S(2)}) collective-permute-start(bf16[224,128]{1,0:T(8,128)(2,1)} %get-tuple-element.37.own_ref), channel_id=1, source_target_pairs={{0,2},{1,3},{2,0},{3,1},{4,6},{5,7},{6,4},{7,5},{8,10},{9,11},{10,... | collective-permute-start | bytes 172040 | tf_op jit(solution)/shard_map/ppermute | solution.py:25
  19.6 32.6 %copy-start.6 = (bf16[1,128,128]{2,1,0:T(8,128)(2,1)S(1)}, bf16[1,128,128]{2,1,0:T(8,128)(2,1)}, u32[]{:S(2)}) copy-start(bf16[1,128,128]{2,1,0:T(8,128)(2,1)} %last_ref.1) | copy-start | bytes 98308
  22.8 2.3 %collective-permute-start.1 = (bf16[224,128]{1,0:T(8,128)(2,1)S(1)}, bf16[224,128]{1,0:T(8,128)(2,1)S(1)}, u32[]{:S(2)}, u32[]{:S(2)}) collective-permute-start(bf16[224,128]{1,0:T(8,128)(2,1)S(1)} %copy-done.5), channel_id=1, source_target_pairs={{0,1},{1,0},{2,3},{3,2},{4,5},{5,4},{6,7},{7,6},{8,9},{9,8},{10,11... | collective-permute-start | bytes 172040 | tf_op jit(solution)/shard_map/ppermute | solution.py:25
  24.3 1.2 %collective-permute-start.2 = (bf16[224,128]{1,0:T(8,128)(2,1)S(1)}, bf16[224,128]{1,0:T(8,128)(2,1)S(1)}, u32[]{:S(2)}, u32[]{:S(2)}) collective-permute-start(bf16[224,128]{1,0:T(8,128)(2,1)S(1)} %collective-permute-done.far_ref), channel_id=1, source_target_pairs={{0,1},{1,0},{2,3},{3,2},{4,5},{5,4},{6,7},{7,6},{8,9},{9,8},{10,11... | collective-permute-start | bytes 172040 | tf_op jit(solution)/shard_map/ppermute | solution.py:25
  26.4 44.2 %copy-start.3 = (bf16[128,448]{1,0:T(8,128)(2,1)S(1)}, bf16[128,448]{1,0:T(8,128)(2,1)}, u32[]{:S(2)}) copy-start(bf16[128,448]{1,0:T(8,128)(2,1)} %get-tuple-element.45.up_t_ref) | copy-start | bytes 344068
  26.4 44.2 %copy-start.4 = (bf16[448,128]{1,0:T(8,128)(2,1)S(1)}, bf16[448,128]{1,0:T(8,128)(2,1)}, u32[]{:S(2)}) copy-start(bf16[448,128]{1,0:T(8,128)(2,1)} %get-tuple-element.44.down_ref) | copy-start | bytes 344068
  30.7 41.5 %copy-start.1 = (bf16[64,16,128]{2,1,0:T(8,128)(2,1)}, bf16[64,16,128]{2,1,0:T(8,128)(2,1)S(1)}, u32[]{:S(2)}) copy-start(bf16[64,16,128]{2,1,0:T(8,128)(2,1)S(1)} %all-to-all-done) | copy-start | bytes 786436
  72.2 18.4 %copy-start.2 = (bf16[1024,128]{1,0:T(8,128)(2,1)S(1)}, bf16[1024,128]{1,0:T(8,128)(2,1)}, u32[]{:S(2)}) copy-start(bf16[1024,128]{1,0:T(8,128)(2,1)} %get-tuple-element.49.x_ref) | copy-start | bytes 786436
  72.2 18.4 %all-to-all-start.3 = ((bf16[64,16,128]{2,1,0:T(8,128)(2,1)}), bf16[64,16,128]{2,1,0:T(8,128)(2,1)S(1)}, u32[]{:S(2)}, u32[]{:S(2)}) async-start(bf16[64,16,128]{2,1,0:T(8,128)(2,1)} %bitcast.25), calls=%async_computation.3 | async-start | bytes 524288 | tf_op jit(solution)/shard_map/all_to_all | solution.py:30
  81.3 3.1 %collective-permute-start.6 = (f32[576,128]{1,0:T(8,128)S(1)}, f32[576,128]{1,0:T(8,128)S(1)}, u32[]{:S(2)}, u32[]{:S(2)}) collective-permute-start(f32[576,128]{1,0:T(8,128)S(1)} %get-tuple-element.54), channel_id=1, source_target_pairs={{0,1},{1,0},{2,3},{3,2},{4,5},{5,4},{6,7},{7,6},{8,9},{9,8},{10,11... | collective-permute-start | bytes 884744 | tf_op jit(solution)/shard_map/ppermute | solution.py:25
  84.4 11.6 %collective-permute-start.7 = (f32[352,128]{1,0:T(8,128)S(1)}, f32[352,128]{1,0:T(8,128)S(1)}, u32[]{:S(2)}, u32[]{:S(2)}) collective-permute-start(f32[352,128]{1,0:T(8,128)S(1)} %get-tuple-element.56), channel_id=1, source_target_pairs={{0,2},{1,3},{2,0},{3,1},{4,6},{5,7},{6,4},{7,5},{8,10},{9,11},{10,... | collective-permute-start | bytes 540680 | tf_op jit(solution)/shard_map/ppermute | solution.py:25
  90.9 5.9 %collective-permute-start.5 = (bf16[128,128]{1,0:T(8,128)(2,1)S(1)}, bf16[128,128]{1,0:T(8,128)(2,1)S(1)}, u32[]{:S(2)}, u32[]{:S(2)}) collective-permute-start(bf16[128,128]{1,0:T(8,128)(2,1)S(1)} %shard_map.117), channel_id=1, source_target_pairs={{0,3},{1,2},{2,1},{3,0},{4,7},{5,6},{6,5},{7,4},{8,11},{9,10},{10,... | collective-permute-start | bytes 98312 | tf_op jit(solution)/shard_map/ppermute | solution.py:25
  91.7 6.4 %collective-permute-start.4 = (bf16[128,128]{1,0:T(8,128)(2,1)S(1)}, bf16[128,128]{1,0:T(8,128)(2,1)S(1)}, u32[]{:S(2)}, u32[]{:S(2)}) collective-permute-start(bf16[128,128]{1,0:T(8,128)(2,1)S(1)} %shard_map.117), channel_id=1, source_target_pairs={{0,2},{1,3},{2,0},{3,1},{4,6},{5,7},{6,4},{7,5},{8,10},{9,11},{10,... | collective-permute-start | bytes 98312 | tf_op jit(solution)/shard_map/ppermute | solution.py:25
  96.0 2.0 %collective-permute-start.3 = (bf16[128,128]{1,0:T(8,128)(2,1)S(1)}, bf16[128,128]{1,0:T(8,128)(2,1)S(1)}, u32[]{:S(2)}, u32[]{:S(2)}) collective-permute-start(bf16[128,128]{1,0:T(8,128)(2,1)S(1)} %shard_map.117), channel_id=1, source_target_pairs={{0,1},{1,0},{2,3},{3,2},{4,5},{5,4},{6,7},{7,6},{8,9},{9,8},{10,11... | collective-permute-start | bytes 98312 | tf_op jit(solution)/shard_map/ppermute | solution.py:25

commit v6 on v5

--- a/solution.py
+++ b/solution.py
@@ -75,40 +75,34 @@
 
 def first_kernel(
     x_hbm, first_hbm, up_hbm, down_hbm, order_hbm, out_hbm, packed_hbm, x_own_hbm, rows_hbm,
-    x, first, spread, buffer, sems,
+    x, first, packed, rows, spread, buffer, sems,
 ):
     count = x.shape[0]
-    start = own_quarter() * count
-    order_rows = rows_hbm.shape[0]
-    steps = count // STEP
     units = up_hbm.shape[1]
-    fetch_first = pltpu.make_async_copy(first_hbm, first, sems.at[steps])
-    fetch_first.start()
-    arrivals = []
-    for i in range(steps):
-        source = x_hbm.at[pl.ds(pl.multiple_of(start + i * STEP, STEP), STEP)]
-        arrivals.append(pltpu.make_async_copy(source, x.at[pl.ds(i * STEP, STEP)], sems.at[i]))
-        arrivals[-1].start()
-    pack = [
-        pltpu.make_async_copy(up_hbm.at[0], packed_hbm.at[pl.ds(0, units)], sems.at[steps + 1]),
-        pltpu.make_async_copy(down_hbm.at[0], packed_hbm.at[pl.ds(units, units)], sems.at[steps + 2]),
-        pltpu.make_async_copy(
-            order_hbm.at[pl.ds(pl.multiple_of(own_quarter() * order_rows, order_rows), order_rows)],
-            rows_hbm,
-            sems.at[steps + 6],
-        ),
+    order_rows = rows.shape[0]
+    start = pl.multiple_of(own_quarter() * count, count)
+    order_start = pl.multiple_of(own_quarter() * order_rows, order_rows)
+    fetch = [
+        (x_hbm.at[pl.ds(start, count)], x),
+        (first_hbm, first),
+        (up_hbm.at[0], packed.at[pl.ds(0, units)]),
+        (down_hbm.at[0], packed.at[pl.ds(units, units)]),
+        (order_hbm.at[pl.ds(order_start, order_rows)], rows),
     ]
-    for copy in pack:
+    fetch = [pltpu.make_async_copy(a, b, sems.at[i]) for i, (a, b) in enumerate(fetch)]
+    for copy in fetch:
         copy.start()
-    fetch_first.wait()
+    fetch[1].wait()
     first_t = first[0].T
-    for arrival in arrivals:
-        arrival.wait()
-    own = pltpu.make_async_copy(x, x_own_hbm, sems.at[steps + 5])
-    own.start()
+    fetch[0].wait()
     put_pieces(spread, dot(first_t, x[...], ((1,), (1,))), 0)
-    copies = send_out(spread, buffer, out_hbm, sems, steps + 3)
-    for copy in pack + copies + [own]:
+    copies = send_out(spread, buffer, out_hbm, sems, 5)
+    for copy in fetch[2:]:
+        copy.wait()
+    for i, (source, target) in enumerate(((x, x_own_hbm), (packed, packed_hbm), (rows, rows_hbm))):
+        copies.append(pltpu.make_async_copy(source, target, sems.at[7 + i]))
+        copies[-1].start()
+    for copy in copies:
         copy.wait()
 
 
@@ -177,58 +171,28 @@
 
 
 def backward_kernel(
-    in_ref, down_ref, up_t_ref, slope_ref, hidden_ref, out_hbm, grad_hbm, hidden_hbm,
-    grad_ref, spread_in, spread, buffer, sems,
+    in_ref, down_ref, up_t_ref, slope_ref, hidden_ref, arrived_ref, last_ref,
+    out_hbm, mine_ref, theirs_ref, spread_in, spread, buffer, sems,
 ):
-    copies = [pltpu.make_async_copy(hidden_ref, hidden_hbm, sems.at[2])]
-    copies[0].start()
+    units, count = hidden_ref.shape
+    half = units // 2
     spread_in[...] = in_ref[...].astype(jnp.float32)
-    down = down_ref[...]
-    up_t = up_t_ref[...]
-    for i in range(grad_ref.shape[1] // STEP):
-        columns = pl.ds(i * STEP, STEP)
-        grad_hidden = mm(down, get_pieces(spread_in, i * STEP, STEP))
-        grad = (grad_hidden * slope_ref[:, columns]).astype(jnp.bfloat16)
-        grad_ref[:, columns] = grad
-        copies.append(
-            pltpu.make_async_copy(grad_ref.at[:, columns], grad_hbm.at[:, columns], sems.at[3 + i])
-        )
-        copies[-1].start()
-        put_pieces(spread, mm(up_t, grad), i * STEP)
-    for copy in send_out(spread, buffer, out_hbm, sems, 0) + copies:
-        copy.wait()
-
-
-def weights_kernel(
-    arrived_hbm, grad_arrived_ref, hidden_hbm, grad_hbm, last_ref, mine_ref, theirs_ref,
-    arrived, hidden, grad, spread_in, sems,
-):
-    units, count = hidden.shape
-    half = units // 2
-    copies = [
-        pltpu.make_async_copy(hidden_hbm, hidden, sems.at[0]),
-        pltpu.make_async_copy(arrived_hbm, arrived, sems.at[1]),
-        pltpu.make_async_copy(grad_hbm, grad, sems.at[2]),
-    ]
-    for copy in copies:
-        copy.start()
-
-    def product(left):
-        return dot(left[...], get_pieces(spread_in, 0, count), ((1,), (1,)))
-
+    grad_out = get_pieces(spread_in, 0, count)
+    grad_hidden = mm(down_ref[...], grad_out)
+    grad = (grad_hidden * slope_ref[...]).astype(jnp.bfloat16)
+    put_pieces(spread, mm(up_t_ref[...], grad), 0)
+    copies = send_out(spread, buffer, out_hbm, sems, 0)
     mine_ref[units:, :] = last_ref[...]
     theirs_ref[units:, :] = last_ref[...]
-    spread_in[...] = grad_arrived_ref[...].astype(jnp.float32)
-    copies[0].wait()
-    down = product(hidden)
+    down = dot(hidden_ref[...], grad_out, ((1,), (1,)))
     mine_ref[half:units, :] = down[:half]
     theirs_ref[half:units, :] = down[half:]
-    copies[1].wait()
-    spread_in[...] = arrived[...].astype(jnp.float32)
-    copies[2].wait()
-    up = product(grad)
+    spread_in[...] = arrived_ref[...].astype(jnp.float32)
+    up = dot(grad, get_pieces(spread_in, 0, count), ((1,), (1,)))
     mine_ref[0:half, :] = up[:half]
     theirs_ref[0:half, :] = up[half:]
+    for copy in copies:
+        copy.wait()
 
 
 def chip_sum_kernel(mine_ref, got_ref, mine_out, theirs_out):
@@ -320,9 +284,11 @@
         [
             pltpu.VMEM((count, BS), BF16),
             pltpu.VMEM((1, BS, BS), BF16),
+            pltpu.VMEM((2 * quarter_units, BS), BF16),
+            pltpu.VMEM((count // LANES, LANES), jnp.int32),
             spread,
             buffer,
-            pltpu.SemaphoreType.DMA((steps + 7,)),
+            pltpu.SemaphoreType.DMA((10,)),
         ],
         small,
         [HBM] * 5,
@@ -368,37 +334,17 @@
     )
     grad_arrived = exchange(grad_returned)
 
-    grad_grouped, grad_preact, hidden = call(
+    half_rows = shape((units + BS, BS), F32)
+    grad_grouped, mine, theirs = call(
         backward_kernel,
-        (grad_arrived, down, up_mixed_t, slope, hidden),
-        (pieces, shape((units, count), BF16), shape((units, count), BF16)),
-        [
-            pltpu.VMEM((units, count), BF16),
-            spread,
-            spread,
-            buffer,
-            pltpu.SemaphoreType.DMA((steps + 3,)),
-        ],
-        2 * flops,
-        out_specs=[HBM, HBM, HBM],
+        (grad_arrived, down, up_mixed_t, slope, hidden, arrived, grad_last),
+        (pieces, half_rows, half_rows),
+        [spread, spread, buffer, two_sems],
+        4 * flops,
+        out_specs=[HBM, VMEM, VMEM],
     )
     grad_first_out = exchange(grad_grouped)
 
-    half_rows = shape((units + BS, BS), F32)
-    mine, theirs = call(
-        weights_kernel,
-        (arrived, grad_arrived, hidden, grad_preact, grad_last),
-        (half_rows, half_rows),
-        [
-            buffer,
-            pltpu.VMEM((units, count), BF16),
-            pltpu.VMEM((units, count), BF16),
-            spread,
-            pltpu.SemaphoreType.DMA((3,)),
-        ],
-        2 * flops,
-        [HBM, VMEM, HBM, HBM, VMEM],
-    )
     quarter_rows = shape((units // 2 + BS, BS), F32)
     mine, theirs = call(
         chip_sum_kernel, (mine, from_partner(theirs, 1)), (quarter_rows, quarter_rows), [], 0

time: 99.1 us -> 97.9 us (0.988)
  Pallas kernels: 11.2 us -> 7.67 us
  waiting for transfers between devices: 13.8 us -> 16.2 us
    pallas_call x10 -> x9, Pallas kernels: 11.2 us -> 7.67 us  [call(): pl.pallas_call(kernel, out_shape=outs, in_specs=in_specs or [VMEM] * len(...]
    all_to_all x2, waiting for transfers between devices: 10.4 us -> 12.8 us  [exchange(): lax.all_to_all(pieces, ('blk', 'hid'), 0, 0, tiled=True, axis_index_group...]
  transfers between devices with their start and end apart: 10 -> 10, of which waited for: 6 -> 6; matrix products, arithmetic and copies ran while one was open for 4% -> 4% of each run, Pallas kernels for 5% -> 2%
where the time goes in v6:
time: 97.9 us; the launch traced here: 97.5 us
  blocking collectives  38.1 us (39%)
  starting transfers between devices  30.1 us (31%)
  waiting for transfers between devices  16.2 us (17%)
  Pallas kernels  7.67 us (8%)
  local copies, waits for them, and re-layouts  3.24 us (3%)
  other arithmetic  1.34 us (1%)
    all_to_all x2, blocking collectives, exchange(): lax.all_to_all(pieces, ('blk', 'hid'), 0, 0, tiled=True, axis_index_group...  38.1 us
    all_to_all x2, starting transfers between devices, exchange(): lax.all_to_all(pieces, ('blk', 'hid'), 0, 0, tiled=True, axis_index_group...  21.5 us
    all_to_all x2, waiting for transfers between devices, exchange(): lax.all_to_all(pieces, ('blk', 'hid'), 0, 0, tiled=True, axis_index_group...  12.8 us
    ppermute x8, starting transfers between devices, from_partner(): return lax.ppermute(value, 'hid', [(i, i ^ m) for i in range(N_HID)])  8.58 us
    pallas_call x9, Pallas kernels, call(): pl.pallas_call(kernel, out_shape=outs, in_specs=in_specs or [VMEM] * len(...  7.67 us
    ppermute x8, waiting for transfers between devices, from_partner(): return lax.ppermute(value, 'hid', [(i, i ^ m) for i in range(N_HID)])  3.41 us
    gather x1, local copies, waits for them, and re-layouts, local(): targets.at[rows.reshape(count)]  3.2 us
  transfers between devices with their start and end apart: 10, of which 6 were waited for; matrix products, arithmetic and copies ran while one was open for 4% of the time, Pallas kernels for 2%

profile of v6, /device:TPU:1, one launch (start us, length us, event | category | flops | bytes accessed | tf_op | source)
XLA Modules:
  0.0 97.5 jit_solution(5735521433725508607)
XLA Ops:
  0.6 2.2 %shard_map.111 = (bf16[1024,128]{1,0:T(8,128)(2,1)}, bf16[224,128]{1,0:T(8,128)(2,1)}, bf16[1024,128]{1,0:T(8,128)(2,1)}, s32[8,128]{1,0:T(8,128)}) custom-call(bf16[4096,128]{1,0:T(8,128)(2,1)} %x_hbm.1, bf16[1,128,128]{2,1,0:T(8,128)(2,1)} %first_hbm.1, bf16[1,112,128]{2,1,0:T(8,128)(2,1)} %up_hbm.1, bf16[1,112,128]{2,1,0:T(8,128)(2,1)} %down_hbm.1, ...), custom_call_target="tpu_custom_call" | custom-call | flops 33554432 | bytes 1740800 | tf_op jit(solution)/shard_map/pallas_call | solution.py:247
  2.9 15.1 %all-to-all-start = ((bf16[64,16,128]{2,1,0:T(8,128)(2,1)}), bf16[64,16,128]{2,1,0:T(8,128)(2,1)S(1)}, u32[]{:S(2)}, u32[]{:S(2)}) async-start(bf16[64,16,128]{2,1,0:T(8,128)(2,1)} %bitcast.23), calls=%async_computation | async-start | bytes 524288 | tf_op jit(solution)/shard_map/all_to_all | solution.py:30
  18.0 0.7 bitcast_clamp_fusion
  18.7 3.2 %gather_fusion = bf16[1024,128]{1,0:T(8,128)(2,1)S(1)} fusion(bf16[4096,128]{1,0:T(8,128)(2,1)S(1)} %copy-done, s32[1024]{0:T(1024)S(1)} %bitcast_clamp_fusion), kind=kCustom, calls=%fused_computation | custom fusion | bytes 528384 | tf_op jit(solution)/shard_map/gather | solution.py:300
  22.0 1.4 %collective-permute-start.1 = (bf16[224,128]{1,0:T(8,128)(2,1)S(1)}, bf16[224,128]{1,0:T(8,128)(2,1)S(1)}, u32[]{:S(2)}, u32[]{:S(2)}) collective-permute-start(bf16[224,128]{1,0:T(8,128)(2,1)S(1)} %copy-done.4), channel_id=1, source_target_pairs={{0,1},{1,0},{2,3},{3,2},{4,5},{5,4},{6,7},{7,6},{8,9},{9,8},{10,11... | collective-permute-start | bytes 172040 | tf_op jit(solution)/shard_map/ppermute | solution.py:25
  23.6 0.7 collective-permute-done.1.near_ref
  24.3 0.4 collective-permute-done.2.other_ref
  24.6 0.9 shard_map.113
  25.5 4.2 %all-to-all-done = bf16[64,16,128]{2,1,0:T(8,128)(2,1)S(1)} async-done(((bf16[64,16,128]{2,1,0:T(8,128)(2,1)}), bf16[64,16,128]{2,1,0:T(8,128)(2,1)S(1)}, u32[]{:S(2)}, u32[]{:S(2)}) %all-to-all-start) | async-done | bytes 262176 | tf_op jit(solution)/shard_map/all_to_all | solution.py:30
  29.8 1.2 %shard_map.114 = (bf16[1024,128]{1,0:T(8,128)(2,1)S(1)}, f32[448,1024]{1,0:T(8,128)S(1)}, bf16[448,1024]{1,0:T(8,128)(2,1)S(1)}) custom-call(bf16[1024,128]{1,0:T(8,128)(2,1)S(1)} %bitcast.14, bf16[448,128]{1,0:T(8,128)(2,1)S(1)} %get-tuple-element.37.up_ref, bf16[128,448]{1,0:T(8,128)(2,1)S(1)} %get-tuple-element.38.down_t_ref), custom_call_target="tpu_custom_call" | custom-call | flops 234881024 | bytes 3506176 | tf_op jit(solution)/shard_map/pallas_call | solution.py:247
  31.0 20.3 %all_to_all.20 = bf16[64,16,128]{2,1,0:T(8,128)(2,1)S(1)} all-to-all(bf16[64,16,128]{2,1,0:T(8,128)(2,1)S(1)} %bitcast.19), channel_id=1, replica_groups={{0,6,8,14,16,22,24,30,32,38,40,46,48,54,56,62,64,70,72,78,80,86,88,94,9..., dimensions={0} | all-to-all | bytes 524288 | tf_op jit(solution)/shard_map/all_to_all | solution.py:30
  51.3 0.6 shard_map.115
  51.9 17.8 %all_to_all.21 = bf16[64,16,128]{2,1,0:T(8,128)(2,1)S(1)} all-to-all(bf16[64,16,128]{2,1,0:T(8,128)(2,1)S(1)} %bitcast.20), channel_id=1, replica_groups={{0,6,8,14,16,22,24,30,32,38,40,46,48,54,56,62,64,70,72,78,80,86,88,94,9..., dimensions={0} | all-to-all | bytes 524288 | tf_op jit(solution)/shard_map/all_to_all | solution.py:30
  69.7 1.4 %shard_map.116 = (bf16[1024,128]{1,0:T(8,128)(2,1)}, f32[576,128]{1,0:T(8,128)S(1)}, f32[576,128]{1,0:T(8,128)S(1)}) custom-call(bf16[1024,128]{1,0:T(8,128)(2,1)S(1)} %bitcast.16, bf16[448,128]{1,0:T(8,128)(2,1)S(1)} %copy-done.3, bf16[128,448]{1,0:T(8,128)(2,1)S(1)} %copy-done.2, f32[448,1024]{1,0:T(8,128)S(1)} %get-tuple-element.44.slope_ref, ...), custom_call_target="tpu_custom_call" | custom-call | flops 469762048 | bytes 4423680 | tf_op jit(solution)/shard_map/pallas_call | solution.py:247
  71.1 6.4 %all-to-all-start.3 = ((bf16[64,16,128]{2,1,0:T(8,128)(2,1)}), bf16[64,16,128]{2,1,0:T(8,128)(2,1)S(1)}, u32[]{:S(2)}, u32[]{:S(2)}) async-start(bf16[64,16,128]{2,1,0:T(8,128)(2,1)} %bitcast.24), calls=%async_computation.3 | async-start | bytes 524288 | tf_op jit(solution)/shard_map/all_to_all | solution.py:30
  77.6 1.9 %collective-permute-start.6 = (f32[576,128]{1,0:T(8,128)S(1)}, f32[576,128]{1,0:T(8,128)S(1)}, u32[]{:S(2)}, u32[]{:S(2)}) collective-permute-start(f32[576,128]{1,0:T(8,128)S(1)} %get-tuple-element.50), channel_id=1, source_target_pairs={{0,1},{1,0},{2,3},{3,2},{4,5},{5,4},{6,7},{7,6},{8,9},{9,8},{10,11... | collective-permute-start | bytes 884744 | tf_op jit(solution)/shard_map/ppermute | solution.py:25
  79.4 1.2 %collective-permute-done.6.got_ref = f32[576,128]{1,0:T(8,128)S(1)} collective-permute-done((f32[576,128]{1,0:T(8,128)S(1)}, f32[576,128]{1,0:T(8,128)S(1)}, u32[]{:S(2)}, u32[]{:S(2)}) %collective-permute-start.6) | collective-permute-done | bytes 294944 | tf_op jit(solution)/shard_map/ppermute | solution.py:25
  80.8 8.6 %all-to-all-done.3 = bf16[64,16,128]{2,1,0:T(8,128)(2,1)S(1)} async-done(((bf16[64,16,128]{2,1,0:T(8,128)(2,1)}), bf16[64,16,128]{2,1,0:T(8,128)(2,1)S(1)}, u32[]{:S(2)}, u32[]{:S(2)}) %all-to-all-start.3) | async-done | bytes 262176 | tf_op jit(solution)/shard_map/all_to_all | solution.py:30
  89.4 0.3 shard_map.117
  89.7 0.8 collective-permute-start.5
  90.5 4.3 %collective-permute-start.4 = (bf16[128,128]{1,0:T(8,128)(2,1)S(1)}, bf16[128,128]{1,0:T(8,128)(2,1)S(1)}, u32[]{:S(2)}, u32[]{:S(2)}) collective-permute-start(bf16[128,128]{1,0:T(8,128)(2,1)S(1)} %shard_map.117), channel_id=1, source_target_pairs={{0,2},{1,3},{2,0},{3,1},{4,6},{5,7},{6,4},{7,5},{8,10},{9,11},{10,... | collective-permute-start | bytes 98312 | tf_op jit(solution)/shard_map/ppermute | solution.py:25
  94.8 0.8 shard_map.119
  95.6 1.2 %collective-permute-done.4 = bf16[128,128]{1,0:T(8,128)(2,1)S(1)} collective-permute-done((bf16[128,128]{1,0:T(8,128)(2,1)S(1)}, bf16[128,128]{1,0:T(8,128)(2,1)S(1)}, u32[]{:S(2)}, u32[]{:S(2)}) %collective-permute-start.4) | collective-permute-done | bytes 32800 | tf_op jit(solution)/shard_map/ppermute | solution.py:25
  96.8 0.6 add_bitcast_fusion
  (24 shorter events, 0.5 us)
Async XLA Ops:
  0.6 18.1 %copy-start = (bf16[4096,128]{1,0:T(8,128)(2,1)S(1)}, bf16[4096,128]{1,0:T(8,128)(2,1)}, u32[]{:S(2)}) copy-start(bf16[4096,128]{1,0:T(8,128)(2,1)} %param.9) | copy-start | bytes 3145732
  2.8 19.1 %copy-start.4 = (bf16[224,128]{1,0:T(8,128)(2,1)S(1)}, bf16[224,128]{1,0:T(8,128)(2,1)}, u32[]{:S(2)}) copy-start(bf16[224,128]{1,0:T(8,128)(2,1)} %get-tuple-element.35.own_ref) | copy-start | bytes 172036
  2.9 21.8 %copy-start.6 = (s32[128]{0:T(128)S(1)}, s32[128]{0:T(128)}, u32[]{:S(2)}) copy-start(s32[128]{0:T(128)} %param.11) | copy-start | bytes 1540
  2.9 26.9 %all-to-all-start = ((bf16[64,16,128]{2,1,0:T(8,128)(2,1)}), bf16[64,16,128]{2,1,0:T(8,128)(2,1)S(1)}, u32[]{:S(2)}, u32[]{:S(2)}) async-start(bf16[64,16,128]{2,1,0:T(8,128)(2,1)} %bitcast.23), calls=%async_computation | async-start | bytes 524288 | tf_op jit(solution)/shard_map/all_to_all | solution.py:30
  17.9 4.0 %collective-permute-start = (bf16[224,128]{1,0:T(8,128)(2,1)}, bf16[224,128]{1,0:T(8,128)(2,1)S(1)}, u32[]{:S(2)}, u32[]{:S(2)}) collective-permute-start(bf16[224,128]{1,0:T(8,128)(2,1)} %get-tuple-element.35.own_ref), channel_id=1, source_target_pairs={{0,2},{1,3},{2,0},{3,1},{4,6},{5,7},{6,4},{7,5},{8,10},{9,11},{10,... | collective-permute-start | bytes 172040 | tf_op jit(solution)/shard_map/ppermute | solution.py:25
  18.7 32.6 %copy-start.5 = (bf16[1,128,128]{2,1,0:T(8,128)(2,1)S(1)}, bf16[1,128,128]{2,1,0:T(8,128)(2,1)}, u32[]{:S(2)}) copy-start(bf16[1,128,128]{2,1,0:T(8,128)(2,1)} %last_ref.1) | copy-start | bytes 98308
  22.0 2.3 %collective-permute-start.1 = (bf16[224,128]{1,0:T(8,128)(2,1)S(1)}, bf16[224,128]{1,0:T(8,128)(2,1)S(1)}, u32[]{:S(2)}, u32[]{:S(2)}) collective-permute-start(bf16[224,128]{1,0:T(8,128)(2,1)S(1)} %copy-done.4), channel_id=1, source_target_pairs={{0,1},{1,0},{2,3},{3,2},{4,5},{5,4},{6,7},{7,6},{8,9},{9,8},{10,11... | collective-permute-start | bytes 172040 | tf_op jit(solution)/shard_map/ppermute | solution.py:25
  23.4 1.2 %collective-permute-start.2 = (bf16[224,128]{1,0:T(8,128)(2,1)S(1)}, bf16[224,128]{1,0:T(8,128)(2,1)S(1)}, u32[]{:S(2)}, u32[]{:S(2)}) collective-permute-start(bf16[224,128]{1,0:T(8,128)(2,1)S(1)} %collective-permute-done.far_ref), channel_id=1, source_target_pairs={{0,1},{1,0},{2,3},{3,2},{4,5},{5,4},{6,7},{7,6},{8,9},{9,8},{10,11... | collective-permute-start | bytes 172040 | tf_op jit(solution)/shard_map/ppermute | solution.py:25
  25.5 44.2 %copy-start.2 = (bf16[128,448]{1,0:T(8,128)(2,1)S(1)}, bf16[128,448]{1,0:T(8,128)(2,1)}, u32[]{:S(2)}) copy-start(bf16[128,448]{1,0:T(8,128)(2,1)} %get-tuple-element.43.up_t_ref) | copy-start | bytes 344068
  25.5 44.2 %copy-start.3 = (bf16[448,128]{1,0:T(8,128)(2,1)S(1)}, bf16[448,128]{1,0:T(8,128)(2,1)}, u32[]{:S(2)}) copy-start(bf16[448,128]{1,0:T(8,128)(2,1)} %get-tuple-element.42.down_ref) | copy-start | bytes 344068
  69.7 19.6 %copy-start.1 = (bf16[1024,128]{1,0:T(8,128)(2,1)S(1)}, bf16[1024,128]{1,0:T(8,128)(2,1)}, u32[]{:S(2)}) copy-start(bf16[1024,128]{1,0:T(8,128)(2,1)} %get-tuple-element.48.x_ref) | copy-start | bytes 786436
  71.1 18.3 %all-to-all-start.3 = ((bf16[64,16,128]{2,1,0:T(8,128)(2,1)}), bf16[64,16,128]{2,1,0:T(8,128)(2,1)S(1)}, u32[]{:S(2)}, u32[]{:S(2)}) async-start(bf16[64,16,128]{2,1,0:T(8,128)(2,1)} %bitcast.24), calls=%async_computation.3 | async-start | bytes 524288 | tf_op jit(solution)/shard_map/all_to_all | solution.py:30
  77.6 3.1 %collective-permute-start.6 = (f32[576,128]{1,0:T(8,128)S(1)}, f32[576,128]{1,0:T(8,128)S(1)}, u32[]{:S(2)}, u32[]{:S(2)}) collective-permute-start(f32[576,128]{1,0:T(8,128)S(1)} %get-tuple-element.50), channel_id=1, source_target_pairs={{0,1},{1,0},{2,3},{3,2},{4,5},{5,4},{6,7},{7,6},{8,9},{9,8},{10,11... | collective-permute-start | bytes 884744 | tf_op jit(solution)/shard_map/ppermute | solution.py:25
  80.7 14.1 %collective-permute-start.7 = (f32[352,128]{1,0:T(8,128)S(1)}, f32[352,128]{1,0:T(8,128)S(1)}, u32[]{:S(2)}, u32[]{:S(2)}) collective-permute-start(f32[352,128]{1,0:T(8,128)S(1)} %get-tuple-element.52), channel_id=1, source_target_pairs={{0,2},{1,3},{2,0},{3,1},{4,6},{5,7},{6,4},{7,5},{8,10},{9,11},{10,... | collective-permute-start | bytes 540680 | tf_op jit(solution)/shard_map/ppermute | solution.py:25
  89.7 5.9 %collective-permute-start.5 = (bf16[128,128]{1,0:T(8,128)(2,1)S(1)}, bf16[128,128]{1,0:T(8,128)(2,1)S(1)}, u32[]{:S(2)}, u32[]{:S(2)}) collective-permute-start(bf16[128,128]{1,0:T(8,128)(2,1)S(1)} %shard_map.117), channel_id=1, source_target_pairs={{0,3},{1,2},{2,1},{3,0},{4,7},{5,6},{6,5},{7,4},{8,11},{9,10},{10,... | collective-permute-start | bytes 98312 | tf_op jit(solution)/shard_map/ppermute | solution.py:25
  90.5 6.4 %collective-permute-start.4 = (bf16[128,128]{1,0:T(8,128)(2,1)S(1)}, bf16[128,128]{1,0:T(8,128)(2,1)S(1)}, u32[]{:S(2)}, u32[]{:S(2)}) collective-permute-start(bf16[128,128]{1,0:T(8,128)(2,1)S(1)} %shard_map.117), channel_id=1, source_target_pairs={{0,2},{1,3},{2,0},{3,1},{4,6},{5,7},{6,4},{7,5},{8,10},{9,11},{10,... | collective-permute-start | bytes 98312 | tf_op jit(solution)/shard_map/ppermute | solution.py:25
  94.8 2.0 %collective-permute-start.3 = (bf16[128,128]{1,0:T(8,128)(2,1)S(1)}, bf16[128,128]{1,0:T(8,128)(2,1)S(1)}, u32[]{:S(2)}, u32[]{:S(2)}) collective-permute-start(bf16[128,128]{1,0:T(8,128)(2,1)S(1)} %shard_map.117), channel_id=1, source_target_pairs={{0,1},{1,0},{2,3},{3,2},{4,5},{5,4},{6,7},{7,6},{8,9},{9,8},{10,11... | collective-permute-start | bytes 98312 | tf_op jit(solution)/shard_map/ppermute | solution.py:25

commit v7 on v6

--- a/solution.py
+++ b/solution.py
@@ -13,12 +13,13 @@
 N_HID = 4
 LANES = 128
 STEP = 1024
+LEADER = 53
 
 
 def token_groups():
-    return [
-        [b * N_HID + (q ^ (2 * (b % 2))) for b in range(NB)] for q in range(N_HID)
-    ]
+    order = list(range(NB))
+    order[0], order[LEADER] = LEADER, 0
+    return [[b * N_HID + (q ^ (2 * (b % 2))) for b in order] for q in range(N_HID)]
 
 
 def from_partner(value, m):
@@ -62,7 +63,20 @@
     return jnp.concatenate(parts, axis=1).astype(jnp.bfloat16)
 
 
+def trade_leader(spread):
+    size = spread.shape[0] // NB
+    leader = spread[LEADER * size : (LEADER + 1) * size, :]
+    spread[LEADER * size : (LEADER + 1) * size, :] = spread[0:size, :]
+    spread[0:size, :] = leader
+
+
+def take_in(spread, ref):
+    spread[...] = ref[...].astype(jnp.float32)
+    trade_leader(spread)
+
+
 def send_out(spread, buffer, hbm, sems, first_sem):
+    trade_leader(spread)
     half = spread.shape[0] // 2
     copies = []
     for i in range(2):
@@ -140,7 +154,7 @@
 def forward_kernel(
     in_ref, up_ref, down_t_ref, out_ref, slope_ref, hidden_ref, spread_in, spread
 ):
-    spread_in[...] = in_ref[...].astype(jnp.float32)
+    take_in(spread_in, in_ref)
     up = up_ref[...]
     down_t = down_t_ref[...]
     for at in range(0, hidden_ref.shape[1], STEP):
@@ -151,11 +165,12 @@
         hidden_ref[:, at : at + STEP] = hidden
         slope_ref[:, at : at + STEP] = cdf + preact * dens
         put_pieces(spread, mm(down_t, hidden), at)
+    trade_leader(spread)
     out_ref[...] = spread[...].astype(jnp.bfloat16)
 
 
 def error_kernel(scale, in_ref, last_ref, teacher_ref, out_ref, grad_ref, spread_in, spread):
-    spread_in[...] = in_ref[...].astype(jnp.float32)
+    take_in(spread_in, in_ref)
     last = last_ref[0]
     last_t = last.T
     grad_last = None
@@ -166,6 +181,7 @@
         put_pieces(spread, mm(last, err), at)
         part = dot(returned, err, ((1,), (1,)))
         grad_last = part if grad_last is None else grad_last + part
+    trade_leader(spread)
     out_ref[...] = spread[...].astype(jnp.bfloat16)
     grad_ref[...] = grad_last
 
@@ -176,7 +192,7 @@
 ):
     units, count = hidden_ref.shape
     half = units // 2
-    spread_in[...] = in_ref[...].astype(jnp.float32)
+    take_in(spread_in, in_ref)
     grad_out = get_pieces(spread_in, 0, count)
     grad_hidden = mm(down_ref[...], grad_out)
     grad = (grad_hidden * slope_ref[...]).astype(jnp.bfloat16)
@@ -187,7 +203,7 @@
     down = dot(hidden_ref[...], grad_out, ((1,), (1,)))
     mine_ref[half:units, :] = down[:half]
     theirs_ref[half:units, :] = down[half:]
-    spread_in[...] = arrived_ref[...].astype(jnp.float32)
+    take_in(spread_in, arrived_ref)
     up = dot(grad, get_pieces(spread_in, 0, count), ((1,), (1,)))
     mine_ref[0:half, :] = up[:half]
     theirs_ref[0:half, :] = up[half:]
@@ -219,7 +235,7 @@
 
 
 def last_kernel(in_ref, x_ref, out_ref, spread_in):
-    spread_in[...] = in_ref[...].astype(jnp.float32)
+    take_in(spread_in, in_ref)
     grad = get_pieces(spread_in, 0, x_ref.shape[0])
     out_ref[...] = mm(grad, x_ref[...]).T.astype(jnp.bfloat16)
 

time: 97.9 us -> 91.2 us (0.932)
  waiting for transfers between devices: 16.2 us -> 4.52 us
  starting transfers between devices: 30.1 us -> 37.7 us
  blocking collectives: 38.1 us -> 35.6 us
    all_to_all x2, waiting for transfers between devices: 12.8 us -> 1.12 us  [exchange(): lax.all_to_all(pieces, ('blk', 'hid'), 0, 0, tiled=True, axis_index_group...]
    all_to_all x2, starting transfers between devices: 21.5 us -> 27.8 us  [exchange(): lax.all_to_all(pieces, ('blk', 'hid'), 0, 0, tiled=True, axis_index_group...]
    all_to_all x2, blocking collectives: 38.1 us -> 35.6 us  [exchange(): lax.all_to_all(pieces, ('blk', 'hid'), 0, 0, tiled=True, axis_index_group...]
    ppermute x8, starting transfers between devices: 8.58 us -> 9.89 us  [from_partner(): return lax.ppermute(value, 'hid', [(i, i ^ m) for i in range(N_HID)])]
  transfers between devices with their start and end apart: 10 -> 10, of which waited for: 6 -> 5; matrix products, arithmetic and copies ran while one was open for 4% -> 4% of each run, Pallas kernels for 2% -> 3%
where the time goes in v7:
time: 91.2 us; the launch traced here: 90.8 us
  starting transfers between devices  37.7 us (41%)
  blocking collectives  35.6 us (39%)
  Pallas kernels  7.69 us (8%)
  waiting for transfers between devices  4.52 us (5%)
  local copies, waits for them, and re-layouts  3.24 us (4%)
  other arithmetic  1.34 us (1%)
    all_to_all x2, blocking collectives, exchange(): lax.all_to_all(pieces, ('blk', 'hid'), 0, 0, tiled=True, axis_index_group...  35.6 us
    all_to_all x2, starting transfers between devices, exchange(): lax.all_to_all(pieces, ('blk', 'hid'), 0, 0, tiled=True, axis_index_group...  27.8 us
    ppermute x8, starting transfers between devices, from_partner(): return lax.ppermute(value, 'hid', [(i, i ^ m) for i in range(N_HID)])  9.89 us
    pallas_call x9, Pallas kernels, call(): pl.pallas_call(kernel, out_shape=outs, in_specs=in_specs or [VMEM] * len(...  7.69 us
    ppermute x8, waiting for transfers between devices, from_partner(): return lax.ppermute(value, 'hid', [(i, i ^ m) for i in range(N_HID)])  3.4 us
    gather x1, local copies, waits for them, and re-layouts, local(): targets.at[rows.reshape(count)]  3.2 us
  transfers between devices with their start and end apart: 10, of which 5 were waited for; matrix products, arithmetic and copies ran while one was open for 4% of the time, Pallas kernels for 3%

profile of v7, /device:TPU:1, one launch (start us, length us, event | category | flops | bytes accessed | tf_op | source)
XLA Modules:
  0.0 90.8 jit_solution(15225724134962582616)
XLA Ops:
  0.6 2.2 %shard_map.111 = (bf16[1024,128]{1,0:T(8,128)(2,1)}, bf16[224,128]{1,0:T(8,128)(2,1)}, bf16[1024,128]{1,0:T(8,128)(2,1)}, s32[8,128]{1,0:T(8,128)}) custom-call(bf16[4096,128]{1,0:T(8,128)(2,1)} %x_hbm.1, bf16[1,128,128]{2,1,0:T(8,128)(2,1)} %first_hbm.1, bf16[1,112,128]{2,1,0:T(8,128)(2,1)} %up_hbm.1, bf16[1,112,128]{2,1,0:T(8,128)(2,1)} %down_hbm.1, ...), custom_call_target="tpu_custom_call" | custom-call | flops 33554432 | bytes 1740800 | tf_op jit(solution)/shard_map/pallas_call | solution.py:263
  2.9 16.3 %all-to-all-start = ((bf16[64,16,128]{2,1,0:T(8,128)(2,1)}), bf16[64,16,128]{2,1,0:T(8,128)(2,1)S(1)}, u32[]{:S(2)}, u32[]{:S(2)}) async-start(bf16[64,16,128]{2,1,0:T(8,128)(2,1)} %bitcast.23), calls=%async_computation | async-start | bytes 524288 | tf_op jit(solution)/shard_map/all_to_all | solution.py:31
  19.3 0.7 bitcast_clamp_fusion
  20.0 3.2 %gather_fusion = bf16[1024,128]{1,0:T(8,128)(2,1)S(1)} fusion(bf16[4096,128]{1,0:T(8,128)(2,1)S(1)} %copy-done, s32[1024]{0:T(1024)S(1)} %bitcast_clamp_fusion), kind=kCustom, calls=%fused_computation | custom fusion | bytes 528384 | tf_op jit(solution)/shard_map/gather | solution.py:316
  23.2 1.4 %collective-permute-start.1 = (bf16[224,128]{1,0:T(8,128)(2,1)S(1)}, bf16[224,128]{1,0:T(8,128)(2,1)S(1)}, u32[]{:S(2)}, u32[]{:S(2)}) collective-permute-start(bf16[224,128]{1,0:T(8,128)(2,1)S(1)} %copy-done.4), channel_id=1, source_target_pairs={{0,1},{1,0},{2,3},{3,2},{4,5},{5,4},{6,7},{7,6},{8,9},{9,8},{10,11... | collective-permute-start | bytes 172040 | tf_op jit(solution)/shard_map/ppermute | solution.py:26
  24.6 0.2 shard_map.112.teacher_ref
  24.9 0.7 collective-permute-done.1.near_ref
  25.5 0.4 collective-permute-done.2.other_ref
  25.9 0.9 shard_map.113
  26.8 1.2 %shard_map.114 = (bf16[1024,128]{1,0:T(8,128)(2,1)S(1)}, f32[448,1024]{1,0:T(8,128)S(1)}, bf16[448,1024]{1,0:T(8,128)(2,1)S(1)}) custom-call(bf16[1024,128]{1,0:T(8,128)(2,1)S(1)} %bitcast.14, bf16[448,128]{1,0:T(8,128)(2,1)S(1)} %get-tuple-element.37.up_ref, bf16[128,448]{1,0:T(8,128)(2,1)S(1)} %get-tuple-element.38.down_t_ref), custom_call_target="tpu_custom_call" | custom-call | flops 234881024 | bytes 3506176 | tf_op jit(solution)/shard_map/pallas_call | solution.py:263
  28.0 18.3 %all_to_all.20 = bf16[64,16,128]{2,1,0:T(8,128)(2,1)S(1)} all-to-all(bf16[64,16,128]{2,1,0:T(8,128)(2,1)S(1)} %bitcast.19), channel_id=1, replica_groups={{214,6,8,14,16,22,24,30,32,38,40,46,48,54,56,62,64,70,72,78,80,86,88,94..., dimensions={0} | all-to-all | bytes 524288 | tf_op jit(solution)/shard_map/all_to_all | solution.py:31
  46.3 0.6 shard_map.115
  46.9 17.2 %all_to_all.21 = bf16[64,16,128]{2,1,0:T(8,128)(2,1)S(1)} all-to-all(bf16[64,16,128]{2,1,0:T(8,128)(2,1)S(1)} %bitcast.20), channel_id=1, replica_groups={{214,6,8,14,16,22,24,30,32,38,40,46,48,54,56,62,64,70,72,78,80,86,88,94..., dimensions={0} | all-to-all | bytes 524288 | tf_op jit(solution)/shard_map/all_to_all | solution.py:31
  64.2 1.4 %shard_map.116 = (bf16[1024,128]{1,0:T(8,128)(2,1)}, f32[576,128]{1,0:T(8,128)S(1)}, f32[576,128]{1,0:T(8,128)S(1)}) custom-call(bf16[1024,128]{1,0:T(8,128)(2,1)S(1)} %bitcast.16, bf16[448,128]{1,0:T(8,128)(2,1)S(1)} %copy-done.3, bf16[128,448]{1,0:T(8,128)(2,1)S(1)} %copy-done.2, f32[448,1024]{1,0:T(8,128)S(1)} %get-tuple-element.44.slope_ref, ...), custom_call_target="tpu_custom_call" | custom-call | flops 469762048 | bytes 4423680 | tf_op jit(solution)/shard_map/pallas_call | solution.py:263
  65.5 11.5 %all-to-all-start.3 = ((bf16[64,16,128]{2,1,0:T(8,128)(2,1)}), bf16[64,16,128]{2,1,0:T(8,128)(2,1)S(1)}, u32[]{:S(2)}, u32[]{:S(2)}) async-start(bf16[64,16,128]{2,1,0:T(8,128)(2,1)} %bitcast.24), calls=%async_computation.3 | async-start | bytes 524288 | tf_op jit(solution)/shard_map/all_to_all | solution.py:31
  77.0 3.2 %collective-permute-start.6 = (f32[576,128]{1,0:T(8,128)S(1)}, f32[576,128]{1,0:T(8,128)S(1)}, u32[]{:S(2)}, u32[]{:S(2)}) collective-permute-start(f32[576,128]{1,0:T(8,128)S(1)} %get-tuple-element.50), channel_id=1, source_target_pairs={{0,1},{1,0},{2,3},{3,2},{4,5},{5,4},{6,7},{7,6},{8,9},{9,8},{10,11... | collective-permute-start | bytes 884744 | tf_op jit(solution)/shard_map/ppermute | solution.py:26
  80.2 1.2 %collective-permute-done.6.got_ref = f32[576,128]{1,0:T(8,128)S(1)} collective-permute-done((f32[576,128]{1,0:T(8,128)S(1)}, f32[576,128]{1,0:T(8,128)S(1)}, u32[]{:S(2)}, u32[]{:S(2)}) %collective-permute-start.6) | collective-permute-done | bytes 294944 | tf_op jit(solution)/shard_map/ppermute | solution.py:26
  81.5 1.1 %all-to-all-done.3 = bf16[64,16,128]{2,1,0:T(8,128)(2,1)S(1)} async-done(((bf16[64,16,128]{2,1,0:T(8,128)(2,1)}), bf16[64,16,128]{2,1,0:T(8,128)(2,1)S(1)}, u32[]{:S(2)}, u32[]{:S(2)}) %all-to-all-start.3) | async-done | bytes 262176 | tf_op jit(solution)/shard_map/all_to_all | solution.py:31
  82.7 0.3 shard_map.117
  83.0 1.5 %collective-permute-start.5 = (bf16[128,128]{1,0:T(8,128)(2,1)S(1)}, bf16[128,128]{1,0:T(8,128)(2,1)S(1)}, u32[]{:S(2)}, u32[]{:S(2)}) collective-permute-start(bf16[128,128]{1,0:T(8,128)(2,1)S(1)} %shard_map.117), channel_id=1, source_target_pairs={{0,3},{1,2},{2,1},{3,0},{4,7},{5,6},{6,5},{7,4},{8,11},{9,10},{10,... | collective-permute-start | bytes 98312 | tf_op jit(solution)/shard_map/ppermute | solution.py:26
  84.6 3.6 %collective-permute-start.4 = (bf16[128,128]{1,0:T(8,128)(2,1)S(1)}, bf16[128,128]{1,0:T(8,128)(2,1)S(1)}, u32[]{:S(2)}, u32[]{:S(2)}) collective-permute-start(bf16[128,128]{1,0:T(8,128)(2,1)S(1)} %shard_map.117), channel_id=1, source_target_pairs={{0,2},{1,3},{2,0},{3,1},{4,6},{5,7},{6,4},{7,5},{8,10},{9,11},{10,... | collective-permute-start | bytes 98312 | tf_op jit(solution)/shard_map/ppermute | solution.py:26
  88.2 0.8 shard_map.119
  89.0 1.2 %collective-permute-done.4 = bf16[128,128]{1,0:T(8,128)(2,1)S(1)} collective-permute-done((bf16[128,128]{1,0:T(8,128)(2,1)S(1)}, bf16[128,128]{1,0:T(8,128)(2,1)S(1)}, u32[]{:S(2)}, u32[]{:S(2)}) %collective-permute-start.4) | collective-permute-done | bytes 32800 | tf_op jit(solution)/shard_map/ppermute | solution.py:26
  90.2 0.6 add_bitcast_fusion
  (24 shorter events, 0.3 us)
Async XLA Ops:
  0.6 19.3 %copy-start = (bf16[4096,128]{1,0:T(8,128)(2,1)S(1)}, bf16[4096,128]{1,0:T(8,128)(2,1)}, u32[]{:S(2)}) copy-start(bf16[4096,128]{1,0:T(8,128)(2,1)} %param.9) | copy-start | bytes 3145732
  2.9 20.3 %copy-start.4 = (bf16[224,128]{1,0:T(8,128)(2,1)S(1)}, bf16[224,128]{1,0:T(8,128)(2,1)}, u32[]{:S(2)}) copy-start(bf16[224,128]{1,0:T(8,128)(2,1)} %get-tuple-element.35.own_ref) | copy-start | bytes 172036
  2.9 23.0 %copy-start.6 = (s32[128]{0:T(128)S(1)}, s32[128]{0:T(128)}, u32[]{:S(2)}) copy-start(s32[128]{0:T(128)} %param.11) | copy-start | bytes 1540
  2.9 23.9 %all-to-all-start = ((bf16[64,16,128]{2,1,0:T(8,128)(2,1)}), bf16[64,16,128]{2,1,0:T(8,128)(2,1)S(1)}, u32[]{:S(2)}, u32[]{:S(2)}) async-start(bf16[64,16,128]{2,1,0:T(8,128)(2,1)} %bitcast.23), calls=%async_computation | async-start | bytes 524288 | tf_op jit(solution)/shard_map/all_to_all | solution.py:31
  19.2 4.0 %collective-permute-start = (bf16[224,128]{1,0:T(8,128)(2,1)}, bf16[224,128]{1,0:T(8,128)(2,1)S(1)}, u32[]{:S(2)}, u32[]{:S(2)}) collective-permute-start(bf16[224,128]{1,0:T(8,128)(2,1)} %get-tuple-element.35.own_ref), channel_id=1, source_target_pairs={{0,2},{1,3},{2,0},{3,1},{4,6},{5,7},{6,4},{7,5},{8,10},{9,11},{10,... | collective-permute-start | bytes 172040 | tf_op jit(solution)/shard_map/ppermute | solution.py:26
  20.0 26.4 %copy-start.5 = (bf16[1,128,128]{2,1,0:T(8,128)(2,1)S(1)}, bf16[1,128,128]{2,1,0:T(8,128)(2,1)}, u32[]{:S(2)}) copy-start(bf16[1,128,128]{2,1,0:T(8,128)(2,1)} %last_ref.1) | copy-start | bytes 98308
  23.2 2.3 %collective-permute-start.1 = (bf16[224,128]{1,0:T(8,128)(2,1)S(1)}, bf16[224,128]{1,0:T(8,128)(2,1)S(1)}, u32[]{:S(2)}, u32[]{:S(2)}) collective-permute-start(bf16[224,128]{1,0:T(8,128)(2,1)S(1)} %copy-done.4), channel_id=1, source_target_pairs={{0,1},{1,0},{2,3},{3,2},{4,5},{5,4},{6,7},{7,6},{8,9},{9,8},{10,11... | collective-permute-start | bytes 172040 | tf_op jit(solution)/shard_map/ppermute | solution.py:26
  24.6 1.2 %collective-permute-start.2 = (bf16[224,128]{1,0:T(8,128)(2,1)S(1)}, bf16[224,128]{1,0:T(8,128)(2,1)S(1)}, u32[]{:S(2)}, u32[]{:S(2)}) collective-permute-start(bf16[224,128]{1,0:T(8,128)(2,1)S(1)} %collective-permute-done.far_ref), channel_id=1, source_target_pairs={{0,1},{1,0},{2,3},{3,2},{4,5},{5,4},{6,7},{7,6},{8,9},{9,8},{10,11... | collective-permute-start | bytes 172040 | tf_op jit(solution)/shard_map/ppermute | solution.py:26
  26.7 37.4 %copy-start.2 = (bf16[128,448]{1,0:T(8,128)(2,1)S(1)}, bf16[128,448]{1,0:T(8,128)(2,1)}, u32[]{:S(2)}) copy-start(bf16[128,448]{1,0:T(8,128)(2,1)} %get-tuple-element.43.up_t_ref) | copy-start | bytes 344068
  26.8 37.4 %copy-start.3 = (bf16[448,128]{1,0:T(8,128)(2,1)S(1)}, bf16[448,128]{1,0:T(8,128)(2,1)}, u32[]{:S(2)}) copy-start(bf16[448,128]{1,0:T(8,128)(2,1)} %get-tuple-element.42.down_ref) | copy-start | bytes 344068
  64.2 18.5 %copy-start.1 = (bf16[1024,128]{1,0:T(8,128)(2,1)S(1)}, bf16[1024,128]{1,0:T(8,128)(2,1)}, u32[]{:S(2)}) copy-start(bf16[1024,128]{1,0:T(8,128)(2,1)} %get-tuple-element.48.x_ref) | copy-start | bytes 786436
  65.5 17.1 %all-to-all-start.3 = ((bf16[64,16,128]{2,1,0:T(8,128)(2,1)}), bf16[64,16,128]{2,1,0:T(8,128)(2,1)S(1)}, u32[]{:S(2)}, u32[]{:S(2)}) async-start(bf16[64,16,128]{2,1,0:T(8,128)(2,1)} %bitcast.24), calls=%async_computation.3 | async-start | bytes 524288 | tf_op jit(solution)/shard_map/all_to_all | solution.py:31
  77.0 4.4 %collective-permute-start.6 = (f32[576,128]{1,0:T(8,128)S(1)}, f32[576,128]{1,0:T(8,128)S(1)}, u32[]{:S(2)}, u32[]{:S(2)}) collective-permute-start(f32[576,128]{1,0:T(8,128)S(1)} %get-tuple-element.50), channel_id=1, source_target_pairs={{0,1},{1,0},{2,3},{3,2},{4,5},{5,4},{6,7},{7,6},{8,9},{9,8},{10,11... | collective-permute-start | bytes 884744 | tf_op jit(solution)/shard_map/ppermute | solution.py:26
  81.4 6.7 %collective-permute-start.7 = (f32[352,128]{1,0:T(8,128)S(1)}, f32[352,128]{1,0:T(8,128)S(1)}, u32[]{:S(2)}, u32[]{:S(2)}) collective-permute-start(f32[352,128]{1,0:T(8,128)S(1)} %get-tuple-element.52), channel_id=1, source_target_pairs={{0,2},{1,3},{2,0},{3,1},{4,6},{5,7},{6,4},{7,5},{8,10},{9,11},{10,... | collective-permute-start | bytes 540680 | tf_op jit(solution)/shard_map/ppermute | solution.py:26
  83.0 6.0 %collective-permute-start.5 = (bf16[128,128]{1,0:T(8,128)(2,1)S(1)}, bf16[128,128]{1,0:T(8,128)(2,1)S(1)}, u32[]{:S(2)}, u32[]{:S(2)}) collective-permute-start(bf16[128,128]{1,0:T(8,128)(2,1)S(1)} %shard_map.117), channel_id=1, source_target_pairs={{0,3},{1,2},{2,1},{3,0},{4,7},{5,6},{6,5},{7,4},{8,11},{9,10},{10,... | collective-permute-start | bytes 98312 | tf_op jit(solution)/shard_map/ppermute | solution.py:26
  84.6 5.6 %collective-permute-start.4 = (bf16[128,128]{1,0:T(8,128)(2,1)S(1)}, bf16[128,128]{1,0:T(8,128)(2,1)S(1)}, u32[]{:S(2)}, u32[]{:S(2)}) collective-permute-start(bf16[128,128]{1,0:T(8,128)(2,1)S(1)} %shard_map.117), channel_id=1, source_target_pairs={{0,2},{1,3},{2,0},{3,1},{4,6},{5,7},{6,4},{7,5},{8,10},{9,11},{10,... | collective-permute-start | bytes 98312 | tf_op jit(solution)/shard_map/ppermute | solution.py:26
  88.2 2.0 %collective-permute-start.3 = (bf16[128,128]{1,0:T(8,128)(2,1)S(1)}, bf16[128,128]{1,0:T(8,128)(2,1)S(1)}, u32[]{:S(2)}, u32[]{:S(2)}) collective-permute-start(bf16[128,128]{1,0:T(8,128)(2,1)S(1)} %shard_map.117), channel_id=1, source_target_pairs={{0,1},{1,0},{2,3},{3,2},{4,5},{5,4},{6,7},{7,6},{8,9},{9,8},{10,11... | collective-permute-start | bytes 98312 | tf_op jit(solution)/shard_map/ppermute | solution.py:26

commit v8 on v6

--- a/solution.py
+++ b/solution.py
@@ -13,22 +13,23 @@
 N_HID = 4
 LANES = 128
 STEP = 1024
-
-
-def token_groups():
-    return [
-        [b * N_HID + (q ^ (2 * (b % 2))) for b in range(NB)] for q in range(N_HID)
-    ]
+LEADERS = (45, 53, 53, 53)
+
+
+def token_groups(leader):
+    order = list(range(NB))
+    order[0], order[leader] = leader, 0
+    return [[b * N_HID + (q ^ (2 * (b % 2))) for b in order] for q in range(N_HID)]
 
 
 def from_partner(value, m):
     return lax.ppermute(value, "hid", [(i, i ^ m) for i in range(N_HID)])
 
 
-def exchange(rows):
+def exchange(rows, step):
     pieces = rows.reshape(NB, rows.shape[0] // NB, LANES)
     pieces = lax.all_to_all(
-        pieces, ("blk", "hid"), 0, 0, tiled=True, axis_index_groups=token_groups()
+        pieces, ("blk", "hid"), 0, 0, tiled=True, axis_index_groups=token_groups(LEADERS[step])
     )
     return pieces.reshape(rows.shape)
 
@@ -62,7 +63,21 @@
     return jnp.concatenate(parts, axis=1).astype(jnp.bfloat16)
 
 
-def send_out(spread, buffer, hbm, sems, first_sem):
+def trade_leader(spread, step):
+    size = spread.shape[0] // NB
+    at = LEADERS[step] * size
+    leader = spread[at : at + size, :]
+    spread[at : at + size, :] = spread[0:size, :]
+    spread[0:size, :] = leader
+
+
+def take_in(spread, ref, step):
+    spread[...] = ref[...].astype(jnp.float32)
+    trade_leader(spread, step)
+
+
+def send_out(spread, buffer, hbm, sems, first_sem, step):
+    trade_leader(spread, step)
     half = spread.shape[0] // 2
     copies = []
     for i in range(2):
@@ -96,7 +111,7 @@
     first_t = first[0].T
     fetch[0].wait()
     put_pieces(spread, dot(first_t, x[...], ((1,), (1,))), 0)
-    copies = send_out(spread, buffer, out_hbm, sems, 5)
+    copies = send_out(spread, buffer, out_hbm, sems, 5, 0)
     for copy in fetch[2:]:
         copy.wait()
     for i, (source, target) in enumerate(((x, x_own_hbm), (packed, packed_hbm), (rows, rows_hbm))):
@@ -140,7 +155,7 @@
 def forward_kernel(
     in_ref, up_ref, down_t_ref, out_ref, slope_ref, hidden_ref, spread_in, spread
 ):
-    spread_in[...] = in_ref[...].astype(jnp.float32)
+    take_in(spread_in, in_ref, 0)
     up = up_ref[...]
     down_t = down_t_ref[...]
     for at in range(0, hidden_ref.shape[1], STEP):
@@ -151,11 +166,12 @@
         hidden_ref[:, at : at + STEP] = hidden
         slope_ref[:, at : at + STEP] = cdf + preact * dens
         put_pieces(spread, mm(down_t, hidden), at)
+    trade_leader(spread, 1)
     out_ref[...] = spread[...].astype(jnp.bfloat16)
 
 
 def error_kernel(scale, in_ref, last_ref, teacher_ref, out_ref, grad_ref, spread_in, spread):
-    spread_in[...] = in_ref[...].astype(jnp.float32)
+    take_in(spread_in, in_ref, 1)
     last = last_ref[0]
     last_t = last.T
     grad_last = None
@@ -166,6 +182,7 @@
         put_pieces(spread, mm(last, err), at)
         part = dot(returned, err, ((1,), (1,)))
         grad_last = part if grad_last is None else grad_last + part
+    trade_leader(spread, 2)
     out_ref[...] = spread[...].astype(jnp.bfloat16)
     grad_ref[...] = grad_last
 
@@ -176,18 +193,18 @@
 ):
     units, count = hidden_ref.shape
     half = units // 2
-    spread_in[...] = in_ref[...].astype(jnp.float32)
+    take_in(spread_in, in_ref, 2)
     grad_out = get_pieces(spread_in, 0, count)
     grad_hidden = mm(down_ref[...], grad_out)
     grad = (grad_hidden * slope_ref[...]).astype(jnp.bfloat16)
     put_pieces(spread, mm(up_t_ref[...], grad), 0)
-    copies = send_out(spread, buffer, out_hbm, sems, 0)
+    copies = send_out(spread, buffer, out_hbm, sems, 0, 3)
     mine_ref[units:, :] = last_ref[...]
     theirs_ref[units:, :] = last_ref[...]
     down = dot(hidden_ref[...], grad_out, ((1,), (1,)))
     mine_ref[half:units, :] = down[:half]
     theirs_ref[half:units, :] = down[half:]
-    spread_in[...] = arrived_ref[...].astype(jnp.float32)
+    take_in(spread_in, arrived_ref, 0)
     up = dot(grad, get_pieces(spread_in, 0, count), ((1,), (1,)))
     mine_ref[0:half, :] = up[:half]
     theirs_ref[0:half, :] = up[half:]
@@ -219,7 +236,7 @@
 
 
 def last_kernel(in_ref, x_ref, out_ref, spread_in):
-    spread_in[...] = in_ref[...].astype(jnp.float32)
+    take_in(spread_in, in_ref, 3)
     grad = get_pieces(spread_in, 0, x_ref.shape[0])
     out_ref[...] = mm(grad, x_ref[...]).T.astype(jnp.bfloat16)
 
@@ -295,7 +312,7 @@
         [HBM] * 4,
     )
     far = from_partner(weights, 2)
-    arrived = exchange(first_out)
+    arrived = exchange(first_out, 0)
 
     teacher = targets.at[rows.reshape(count)].get(mode="promise_in_bounds", wrap_negative_indices=False)
     weights, far, teacher = lax.optimization_barrier((weights, far, teacher))
@@ -323,7 +340,7 @@
         [spread, spread],
         2 * flops,
     )
-    returned = exchange(summed)
+    returned = exchange(summed, 1)
 
     grad_returned, grad_last = call(
         functools.partial(error_kernel, loss_scale),
@@ -332,7 +349,7 @@
         [spread, spread],
         3 * small,
     )
-    grad_arrived = exchange(grad_returned)
+    grad_arrived = exchange(grad_returned, 2)
 
     half_rows = shape((units + BS, BS), F32)
     grad_grouped, mine, theirs = call(
@@ -343,7 +360,7 @@
         4 * flops,
         out_specs=[HBM, VMEM, VMEM],
     )
-    grad_first_out = exchange(grad_grouped)
+    grad_first_out = exchange(grad_grouped, 3)
 
     quarter_rows = shape((units // 2 + BS, BS), F32)
     mine, theirs = call(

time: 97.9 us -> 90 us (0.919)
  waiting for transfers between devices: 16.2 us -> 3.53 us
  starting transfers between devices: 30.1 us -> 39.6 us
  blocking collectives: 38.1 us -> 33.4 us
    all_to_all x2, waiting for transfers between devices: 12.8 us -> 0.13 us  [exchange(): lax.all_to_all(pieces, ('blk', 'hid'), 0, 0, tiled=True, axis_index_group...]
    all_to_all x2, starting transfers between devices: 21.5 us -> 27.7 us  [exchange(): lax.all_to_all(pieces, ('blk', 'hid'), 0, 0, tiled=True, axis_index_group...]
    all_to_all x2, blocking collectives: 38.1 us -> 33.4 us  [exchange(): lax.all_to_all(pieces, ('blk', 'hid'), 0, 0, tiled=True, axis_index_group...]
    ppermute x8, starting transfers between devices: 8.58 us -> 11.9 us  [from_partner(): return lax.ppermute(value, 'hid', [(i, i ^ m) for i in range(N_HID)])]
  transfers between devices with their start and end apart: 10 -> 10, of which waited for: 6 -> 5; matrix products, arithmetic and copies ran while one was open for 4% -> 4% of each run, Pallas kernels for 2% -> 3%
where the time goes in v8:
time: 90 us; the launch traced here: 89.6 us
  starting transfers between devices  39.6 us (44%)
  blocking collectives  33.4 us (37%)
  Pallas kernels  7.68 us (9%)
  waiting for transfers between devices  3.53 us (4%)
  local copies, waits for them, and re-layouts  3.24 us (4%)
  other arithmetic  1.34 us (1%)
    all_to_all x2, blocking collectives, exchange(): lax.all_to_all(pieces, ('blk', 'hid'), 0, 0, tiled=True, axis_index_group...  33.4 us
    all_to_all x2, starting transfers between devices, exchange(): lax.all_to_all(pieces, ('blk', 'hid'), 0, 0, tiled=True, axis_index_group...  27.7 us
    ppermute x8, starting transfers between devices, from_partner(): return lax.ppermute(value, 'hid', [(i, i ^ m) for i in range(N_HID)])  11.9 us
    pallas_call x9, Pallas kernels, call(): pl.pallas_call(kernel, out_shape=outs, in_specs=in_specs or [VMEM] * len(...  7.68 us
    ppermute x8, waiting for transfers between devices, from_partner(): return lax.ppermute(value, 'hid', [(i, i ^ m) for i in range(N_HID)])  3.4 us
    gather x1, local copies, waits for them, and re-layouts, local(): targets.at[rows.reshape(count)]  3.2 us
  transfers between devices with their start and end apart: 10, of which 5 were waited for; matrix products, arithmetic and copies ran while one was open for 4% of the time, Pallas kernels for 3%

profile of v8, /device:TPU:1, one launch (start us, length us, event | category | flops | bytes accessed | tf_op | source)
XLA Modules:
  0.0 89.6 jit_solution(6885848318564330161)
XLA Ops:
  0.6 2.2 %shard_map.111 = (bf16[1024,128]{1,0:T(8,128)(2,1)}, bf16[224,128]{1,0:T(8,128)(2,1)}, bf16[1024,128]{1,0:T(8,128)(2,1)}, s32[8,128]{1,0:T(8,128)}) custom-call(bf16[4096,128]{1,0:T(8,128)(2,1)} %x_hbm.1, bf16[1,128,128]{2,1,0:T(8,128)(2,1)} %first_hbm.1, bf16[1,112,128]{2,1,0:T(8,128)(2,1)} %up_hbm.1, bf16[1,112,128]{2,1,0:T(8,128)(2,1)} %down_hbm.1, ...), custom_call_target="tpu_custom_call" | custom-call | flops 33554432 | bytes 1740800 | tf_op jit(solution)/shard_map/pallas_call | solution.py:264
  2.9 16.7 %all-to-all-start = ((bf16[64,16,128]{2,1,0:T(8,128)(2,1)}), bf16[64,16,128]{2,1,0:T(8,128)(2,1)S(1)}, u32[]{:S(2)}, u32[]{:S(2)}) async-start(bf16[64,16,128]{2,1,0:T(8,128)(2,1)} %bitcast.23), calls=%async_computation | async-start | bytes 524288 | tf_op jit(solution)/shard_map/all_to_all | solution.py:31
  19.7 0.7 bitcast_clamp_fusion
  20.4 3.2 %gather_fusion = bf16[1024,128]{1,0:T(8,128)(2,1)S(1)} fusion(bf16[4096,128]{1,0:T(8,128)(2,1)S(1)} %copy-done, s32[1024]{0:T(1024)S(1)} %bitcast_clamp_fusion), kind=kCustom, calls=%fused_computation | custom fusion | bytes 528384 | tf_op jit(solution)/shard_map/gather | solution.py:317
  23.6 1.4 %collective-permute-start.1 = (bf16[224,128]{1,0:T(8,128)(2,1)S(1)}, bf16[224,128]{1,0:T(8,128)(2,1)S(1)}, u32[]{:S(2)}, u32[]{:S(2)}) collective-permute-start(bf16[224,128]{1,0:T(8,128)(2,1)S(1)} %copy-done.4), channel_id=1, source_target_pairs={{0,1},{1,0},{2,3},{3,2},{4,5},{5,4},{6,7},{7,6},{8,9},{9,8},{10,11... | collective-permute-start | bytes 172040 | tf_op jit(solution)/shard_map/ppermute | solution.py:26
  25.0 0.2 shard_map.112.teacher_ref
  25.2 0.7 collective-permute-done.1.near_ref
  25.9 0.4 collective-permute-done.2.other_ref
  26.2 0.9 shard_map.113
  27.2 1.2 %shard_map.114 = (bf16[1024,128]{1,0:T(8,128)(2,1)S(1)}, f32[448,1024]{1,0:T(8,128)S(1)}, bf16[448,1024]{1,0:T(8,128)(2,1)S(1)}) custom-call(bf16[1024,128]{1,0:T(8,128)(2,1)S(1)} %bitcast.14, bf16[448,128]{1,0:T(8,128)(2,1)S(1)} %get-tuple-element.37.up_ref, bf16[128,448]{1,0:T(8,128)(2,1)S(1)} %get-tuple-element.38.down_t_ref), custom_call_target="tpu_custom_call" | custom-call | flops 234881024 | bytes 3506176 | tf_op jit(solution)/shard_map/pallas_call | solution.py:264
  28.4 16.4 %all_to_all.20 = bf16[64,16,128]{2,1,0:T(8,128)(2,1)S(1)} all-to-all(bf16[64,16,128]{2,1,0:T(8,128)(2,1)S(1)} %bitcast.19), channel_id=1, replica_groups={{214,6,8,14,16,22,24,30,32,38,40,46,48,54,56,62,64,70,72,78,80,86,88,94..., dimensions={0} | all-to-all | bytes 524288 | tf_op jit(solution)/shard_map/all_to_all | solution.py:31
  44.9 0.6 shard_map.115
  45.4 16.9 %all_to_all.21 = bf16[64,16,128]{2,1,0:T(8,128)(2,1)S(1)} all-to-all(bf16[64,16,128]{2,1,0:T(8,128)(2,1)S(1)} %bitcast.20), channel_id=1, replica_groups={{214,6,8,14,16,22,24,30,32,38,40,46,48,54,56,62,64,70,72,78,80,86,88,94..., dimensions={0} | all-to-all | bytes 524288 | tf_op jit(solution)/shard_map/all_to_all | solution.py:31
  62.3 1.4 %shard_map.116 = (bf16[1024,128]{1,0:T(8,128)(2,1)}, f32[576,128]{1,0:T(8,128)S(1)}, f32[576,128]{1,0:T(8,128)S(1)}) custom-call(bf16[1024,128]{1,0:T(8,128)(2,1)S(1)} %bitcast.16, bf16[448,128]{1,0:T(8,128)(2,1)S(1)} %copy-done.3, bf16[128,448]{1,0:T(8,128)(2,1)S(1)} %copy-done.2, f32[448,1024]{1,0:T(8,128)S(1)} %get-tuple-element.44.slope_ref, ...), custom_call_target="tpu_custom_call" | custom-call | flops 469762048 | bytes 4423680 | tf_op jit(solution)/shard_map/pallas_call | solution.py:264
  63.7 11.1 %all-to-all-start.3 = ((bf16[64,16,128]{2,1,0:T(8,128)(2,1)}), bf16[64,16,128]{2,1,0:T(8,128)(2,1)S(1)}, u32[]{:S(2)}, u32[]{:S(2)}) async-start(bf16[64,16,128]{2,1,0:T(8,128)(2,1)} %bitcast.24), calls=%async_computation.3 | async-start | bytes 524288 | tf_op jit(solution)/shard_map/all_to_all | solution.py:31
  74.8 4.2 %collective-permute-start.6 = (f32[576,128]{1,0:T(8,128)S(1)}, f32[576,128]{1,0:T(8,128)S(1)}, u32[]{:S(2)}, u32[]{:S(2)}) collective-permute-start(f32[576,128]{1,0:T(8,128)S(1)} %get-tuple-element.50), channel_id=1, source_target_pairs={{0,1},{1,0},{2,3},{3,2},{4,5},{5,4},{6,7},{7,6},{8,9},{9,8},{10,11... | collective-permute-start | bytes 884744 | tf_op jit(solution)/shard_map/ppermute | solution.py:26
  79.0 1.2 %collective-permute-done.6.got_ref = f32[576,128]{1,0:T(8,128)S(1)} collective-permute-done((f32[576,128]{1,0:T(8,128)S(1)}, f32[576,128]{1,0:T(8,128)S(1)}, u32[]{:S(2)}, u32[]{:S(2)}) %collective-permute-start.6) | collective-permute-done | bytes 294944 | tf_op jit(solution)/shard_map/ppermute | solution.py:26
  80.3 0.1 all-to-all-done.3
  80.4 0.3 shard_map.117
  80.8 3.3 %collective-permute-start.5 = (bf16[128,128]{1,0:T(8,128)(2,1)S(1)}, bf16[128,128]{1,0:T(8,128)(2,1)S(1)}, u32[]{:S(2)}, u32[]{:S(2)}) collective-permute-start(bf16[128,128]{1,0:T(8,128)(2,1)S(1)} %shard_map.117), channel_id=1, source_target_pairs={{0,3},{1,2},{2,1},{3,0},{4,7},{5,6},{6,5},{7,4},{8,11},{9,10},{10,... | collective-permute-start | bytes 98312 | tf_op jit(solution)/shard_map/ppermute | solution.py:26
  84.1 2.8 %collective-permute-start.4 = (bf16[128,128]{1,0:T(8,128)(2,1)S(1)}, bf16[128,128]{1,0:T(8,128)(2,1)S(1)}, u32[]{:S(2)}, u32[]{:S(2)}) collective-permute-start(bf16[128,128]{1,0:T(8,128)(2,1)S(1)} %shard_map.117), channel_id=1, source_target_pairs={{0,2},{1,3},{2,0},{3,1},{4,6},{5,7},{6,4},{7,5},{8,10},{9,11},{10,... | collective-permute-start | bytes 98312 | tf_op jit(solution)/shard_map/ppermute | solution.py:26
  86.9 0.8 shard_map.119
  87.7 1.2 %collective-permute-done.4 = bf16[128,128]{1,0:T(8,128)(2,1)S(1)} collective-permute-done((bf16[128,128]{1,0:T(8,128)(2,1)S(1)}, bf16[128,128]{1,0:T(8,128)(2,1)S(1)}, u32[]{:S(2)}, u32[]{:S(2)}) %collective-permute-start.4) | collective-permute-done | bytes 32800 | tf_op jit(solution)/shard_map/ppermute | solution.py:26
  88.9 0.6 add_bitcast_fusion
  (24 shorter events, 0.3 us)
Async XLA Ops:
  0.6 19.7 %copy-start = (bf16[4096,128]{1,0:T(8,128)(2,1)S(1)}, bf16[4096,128]{1,0:T(8,128)(2,1)}, u32[]{:S(2)}) copy-start(bf16[4096,128]{1,0:T(8,128)(2,1)} %param.9) | copy-start | bytes 3145732
  2.9 20.7 %copy-start.4 = (bf16[224,128]{1,0:T(8,128)(2,1)S(1)}, bf16[224,128]{1,0:T(8,128)(2,1)}, u32[]{:S(2)}) copy-start(bf16[224,128]{1,0:T(8,128)(2,1)} %get-tuple-element.35.own_ref) | copy-start | bytes 172036
  2.9 23.4 %copy-start.6 = (s32[128]{0:T(128)S(1)}, s32[128]{0:T(128)}, u32[]{:S(2)}) copy-start(s32[128]{0:T(128)} %param.11) | copy-start | bytes 1540
  2.9 24.3 %all-to-all-start = ((bf16[64,16,128]{2,1,0:T(8,128)(2,1)}), bf16[64,16,128]{2,1,0:T(8,128)(2,1)S(1)}, u32[]{:S(2)}, u32[]{:S(2)}) async-start(bf16[64,16,128]{2,1,0:T(8,128)(2,1)} %bitcast.23), calls=%async_computation | async-start | bytes 524288 | tf_op jit(solution)/shard_map/all_to_all | solution.py:31
  19.6 4.0 %collective-permute-start = (bf16[224,128]{1,0:T(8,128)(2,1)}, bf16[224,128]{1,0:T(8,128)(2,1)S(1)}, u32[]{:S(2)}, u32[]{:S(2)}) collective-permute-start(bf16[224,128]{1,0:T(8,128)(2,1)} %get-tuple-element.35.own_ref), channel_id=1, source_target_pairs={{0,2},{1,3},{2,0},{3,1},{4,6},{5,7},{6,4},{7,5},{8,10},{9,11},{10,... | collective-permute-start | bytes 172040 | tf_op jit(solution)/shard_map/ppermute | solution.py:26
  20.4 24.5 %copy-start.5 = (bf16[1,128,128]{2,1,0:T(8,128)(2,1)S(1)}, bf16[1,128,128]{2,1,0:T(8,128)(2,1)}, u32[]{:S(2)}) copy-start(bf16[1,128,128]{2,1,0:T(8,128)(2,1)} %last_ref.1) | copy-start | bytes 98308
  23.6 2.3 %collective-permute-start.1 = (bf16[224,128]{1,0:T(8,128)(2,1)S(1)}, bf16[224,128]{1,0:T(8,128)(2,1)S(1)}, u32[]{:S(2)}, u32[]{:S(2)}) collective-permute-start(bf16[224,128]{1,0:T(8,128)(2,1)S(1)} %copy-done.4), channel_id=1, source_target_pairs={{0,1},{1,0},{2,3},{3,2},{4,5},{5,4},{6,7},{7,6},{8,9},{9,8},{10,11... | collective-permute-start | bytes 172040 | tf_op jit(solution)/shard_map/ppermute | solution.py:26
  25.0 1.2 %collective-permute-start.2 = (bf16[224,128]{1,0:T(8,128)(2,1)S(1)}, bf16[224,128]{1,0:T(8,128)(2,1)S(1)}, u32[]{:S(2)}, u32[]{:S(2)}) collective-permute-start(bf16[224,128]{1,0:T(8,128)(2,1)S(1)} %collective-permute-done.far_ref), channel_id=1, source_target_pairs={{0,1},{1,0},{2,3},{3,2},{4,5},{5,4},{6,7},{7,6},{8,9},{9,8},{10,11... | collective-permute-start | bytes 172040 | tf_op jit(solution)/shard_map/ppermute | solution.py:26
  27.1 35.2 %copy-start.2 = (bf16[128,448]{1,0:T(8,128)(2,1)S(1)}, bf16[128,448]{1,0:T(8,128)(2,1)}, u32[]{:S(2)}) copy-start(bf16[128,448]{1,0:T(8,128)(2,1)} %get-tuple-element.43.up_t_ref) | copy-start | bytes 344068
  27.1 35.2 %copy-start.3 = (bf16[448,128]{1,0:T(8,128)(2,1)S(1)}, bf16[448,128]{1,0:T(8,128)(2,1)}, u32[]{:S(2)}) copy-start(bf16[448,128]{1,0:T(8,128)(2,1)} %get-tuple-element.42.down_ref) | copy-start | bytes 344068
  62.3 18.1 %copy-start.1 = (bf16[1024,128]{1,0:T(8,128)(2,1)S(1)}, bf16[1024,128]{1,0:T(8,128)(2,1)}, u32[]{:S(2)}) copy-start(bf16[1024,128]{1,0:T(8,128)(2,1)} %get-tuple-element.48.x_ref) | copy-start | bytes 786436
  63.7 16.7 %all-to-all-start.3 = ((bf16[64,16,128]{2,1,0:T(8,128)(2,1)}), bf16[64,16,128]{2,1,0:T(8,128)(2,1)S(1)}, u32[]{:S(2)}, u32[]{:S(2)}) async-start(bf16[64,16,128]{2,1,0:T(8,128)(2,1)} %bitcast.24), calls=%async_computation.3 | async-start | bytes 524288 | tf_op jit(solution)/shard_map/all_to_all | solution.py:31
  74.8 5.4 %collective-permute-start.6 = (f32[576,128]{1,0:T(8,128)S(1)}, f32[576,128]{1,0:T(8,128)S(1)}, u32[]{:S(2)}, u32[]{:S(2)}) collective-permute-start(f32[576,128]{1,0:T(8,128)S(1)} %get-tuple-element.50), channel_id=1, source_target_pairs={{0,1},{1,0},{2,3},{3,2},{4,5},{5,4},{6,7},{7,6},{8,9},{9,8},{10,11... | collective-permute-start | bytes 884744 | tf_op jit(solution)/shard_map/ppermute | solution.py:26
  80.2 6.7 %collective-permute-start.7 = (f32[352,128]{1,0:T(8,128)S(1)}, f32[352,128]{1,0:T(8,128)S(1)}, u32[]{:S(2)}, u32[]{:S(2)}) collective-permute-start(f32[352,128]{1,0:T(8,128)S(1)} %get-tuple-element.52), channel_id=1, source_target_pairs={{0,2},{1,3},{2,0},{3,1},{4,6},{5,7},{6,4},{7,5},{8,10},{9,11},{10,... | collective-permute-start | bytes 540680 | tf_op jit(solution)/shard_map/ppermute | solution.py:26
  80.8 7.0 %collective-permute-start.5 = (bf16[128,128]{1,0:T(8,128)(2,1)S(1)}, bf16[128,128]{1,0:T(8,128)(2,1)S(1)}, u32[]{:S(2)}, u32[]{:S(2)}) collective-permute-start(bf16[128,128]{1,0:T(8,128)(2,1)S(1)} %shard_map.117), channel_id=1, source_target_pairs={{0,3},{1,2},{2,1},{3,0},{4,7},{5,6},{6,5},{7,4},{8,11},{9,10},{10,... | collective-permute-start | bytes 98312 | tf_op jit(solution)/shard_map/ppermute | solution.py:26
  84.1 4.8 %collective-permute-start.4 = (bf16[128,128]{1,0:T(8,128)(2,1)S(1)}, bf16[128,128]{1,0:T(8,128)(2,1)S(1)}, u32[]{:S(2)}, u32[]{:S(2)}) collective-permute-start(bf16[128,128]{1,0:T(8,128)(2,1)S(1)} %shard_map.117), channel_id=1, source_target_pairs={{0,2},{1,3},{2,0},{3,1},{4,6},{5,7},{6,4},{7,5},{8,10},{9,11},{10,... | collective-permute-start | bytes 98312 | tf_op jit(solution)/shard_map/ppermute | solution.py:26
  86.9 2.0 %collective-permute-start.3 = (bf16[128,128]{1,0:T(8,128)(2,1)S(1)}, bf16[128,128]{1,0:T(8,128)(2,1)S(1)}, u32[]{:S(2)}, u32[]{:S(2)}) collective-permute-start(bf16[128,128]{1,0:T(8,128)(2,1)S(1)} %shard_map.117), channel_id=1, source_target_pairs={{0,1},{1,0},{2,3},{3,2},{4,5},{5,4},{6,7},{7,6},{8,9},{9,8},{10,11... | collective-permute-start | bytes 98312 | tf_op jit(solution)/shard_map/ppermute | solution.py:26

commit v9 on v8

--- a/solution.py
+++ b/solution.py
@@ -215,17 +215,18 @@
 def chip_sum_kernel(mine_ref, got_ref, mine_out, theirs_out):
     quarter = (mine_ref.shape[0] - BS) // 4
     total = mine_ref[...] + got_ref[...]
+    last = total[4 * quarter :].astype(jnp.bfloat16)
     mine_out[0:quarter, :] = total[0:quarter]
-    theirs_out[0:quarter, :] = total[quarter : 2 * quarter]
+    theirs_out[0:quarter, :] = total[quarter : 2 * quarter].astype(jnp.bfloat16)
     mine_out[quarter : 2 * quarter, :] = total[2 * quarter : 3 * quarter]
-    theirs_out[quarter : 2 * quarter, :] = total[3 * quarter : 4 * quarter]
-    mine_out[2 * quarter :, :] = total[4 * quarter :]
-    theirs_out[2 * quarter :, :] = total[4 * quarter :]
+    theirs_out[quarter : 2 * quarter, :] = total[3 * quarter : 4 * quarter].astype(jnp.bfloat16)
+    mine_out[2 * quarter :, :] = last.astype(jnp.float32)
+    theirs_out[2 * quarter :, :] = last
 
 
 def totals_kernel(mine_ref, got_ref, mix_ref, up_ref, down_ref, last_ref):
     quarter = up_ref.shape[1]
-    total = mine_ref[...] + got_ref[...]
+    total = mine_ref[...] + got_ref[...].astype(jnp.float32)
     ids = lax.broadcasted_iota(jnp.int32, (BS, BS), 0)
     one_hot = (mix_ref[...] == ids).astype(jnp.float32)
     up_ref[0] = jnp.dot(
@@ -363,8 +364,9 @@
     grad_first_out = exchange(grad_grouped, 3)
 
     quarter_rows = shape((units // 2 + BS, BS), F32)
+    sent_rows = shape((units // 2 + BS, BS), BF16)
     mine, theirs = call(
-        chip_sum_kernel, (mine, from_partner(theirs, 1)), (quarter_rows, quarter_rows), [], 0
+        chip_sum_kernel, (mine, from_partner(theirs, 1)), (quarter_rows, sent_rows), [], 0
     )
     factor_grad = shape((1, quarter_units, BS), F32)
     grad_up, grad_down, grad_last = call(

time: 90 us -> 90 us (level)
  no operation moved by 1% of the time
where the time goes in v9:
time: 90 us; the launch traced here: 89.6 us
  starting transfers between devices  39.6 us (44%)
  blocking collectives  33.4 us (37%)
  Pallas kernels  7.68 us (9%)
  waiting for transfers between devices  3.53 us (4%)
  local copies, waits for them, and re-layouts  3.24 us (4%)
  other arithmetic  1.34 us (1%)
    all_to_all x2, blocking collectives, exchange(): lax.all_to_all(pieces, ('blk', 'hid'), 0, 0, tiled=True, axis_index_group...  33.4 us
    all_to_all x2, starting transfers between devices, exchange(): lax.all_to_all(pieces, ('blk', 'hid'), 0, 0, tiled=True, axis_index_group...  27.7 us
    ppermute x8, starting transfers between devices, from_partner(): return lax.ppermute(value, 'hid', [(i, i ^ m) for i in range(N_HID)])  11.9 us
    pallas_call x9, Pallas kernels, call(): pl.pallas_call(kernel, out_shape=outs, in_specs=in_specs or [VMEM] * len(...  7.68 us
    ppermute x8, waiting for transfers between devices, from_partner(): return lax.ppermute(value, 'hid', [(i, i ^ m) for i in range(N_HID)])  3.4 us
    gather x1, local copies, waits for them, and re-layouts, local(): targets.at[rows.reshape(count)]  3.2 us
  transfers between devices with their start and end apart: 10, of which 5 were waited for; matrix products, arithmetic and copies ran while one was open for 4% of the time, Pallas kernels for 3%

profile of v9, /device:TPU:1, one launch (start us, length us, event | category | flops | bytes accessed | tf_op | source)
XLA Modules:
  0.0 89.6 jit_solution(15387837088400932826)
XLA Ops:
  0.6 2.2 %shard_map.111 = (bf16[1024,128]{1,0:T(8,128)(2,1)}, bf16[224,128]{1,0:T(8,128)(2,1)}, bf16[1024,128]{1,0:T(8,128)(2,1)}, s32[8,128]{1,0:T(8,128)}) custom-call(bf16[4096,128]{1,0:T(8,128)(2,1)} %x_hbm.1, bf16[1,128,128]{2,1,0:T(8,128)(2,1)} %first_hbm.1, bf16[1,112,128]{2,1,0:T(8,128)(2,1)} %up_hbm.1, bf16[1,112,128]{2,1,0:T(8,128)(2,1)} %down_hbm.1, ...), custom_call_target="tpu_custom_call" | custom-call | flops 33554432 | bytes 1740800 | tf_op jit(solution)/shard_map/pallas_call | solution.py:265
  2.9 16.7 %all-to-all-start = ((bf16[64,16,128]{2,1,0:T(8,128)(2,1)}), bf16[64,16,128]{2,1,0:T(8,128)(2,1)S(1)}, u32[]{:S(2)}, u32[]{:S(2)}) async-start(bf16[64,16,128]{2,1,0:T(8,128)(2,1)} %bitcast.23), calls=%async_computation | async-start | bytes 524288 | tf_op jit(solution)/shard_map/all_to_all | solution.py:31
  19.7 0.7 bitcast_clamp_fusion
  20.4 3.2 %gather_fusion = bf16[1024,128]{1,0:T(8,128)(2,1)S(1)} fusion(bf16[4096,128]{1,0:T(8,128)(2,1)S(1)} %copy-done, s32[1024]{0:T(1024)S(1)} %bitcast_clamp_fusion), kind=kCustom, calls=%fused_computation | custom fusion | bytes 528384 | tf_op jit(solution)/shard_map/gather | solution.py:318
  23.6 1.4 %collective-permute-start.1 = (bf16[224,128]{1,0:T(8,128)(2,1)S(1)}, bf16[224,128]{1,0:T(8,128)(2,1)S(1)}, u32[]{:S(2)}, u32[]{:S(2)}) collective-permute-start(bf16[224,128]{1,0:T(8,128)(2,1)S(1)} %copy-done.4), channel_id=1, source_target_pairs={{0,1},{1,0},{2,3},{3,2},{4,5},{5,4},{6,7},{7,6},{8,9},{9,8},{10,11... | collective-permute-start | bytes 172040 | tf_op jit(solution)/shard_map/ppermute | solution.py:26
  25.0 0.2 shard_map.112.teacher_ref
  25.2 0.7 collective-permute-done.1.near_ref
  25.9 0.4 collective-permute-done.2.other_ref
  26.2 0.9 shard_map.113
  27.2 1.2 %shard_map.114 = (bf16[1024,128]{1,0:T(8,128)(2,1)S(1)}, f32[448,1024]{1,0:T(8,128)S(1)}, bf16[448,1024]{1,0:T(8,128)(2,1)S(1)}) custom-call(bf16[1024,128]{1,0:T(8,128)(2,1)S(1)} %bitcast.14, bf16[448,128]{1,0:T(8,128)(2,1)S(1)} %get-tuple-element.37.up_ref, bf16[128,448]{1,0:T(8,128)(2,1)S(1)} %get-tuple-element.38.down_t_ref), custom_call_target="tpu_custom_call" | custom-call | flops 234881024 | bytes 3506176 | tf_op jit(solution)/shard_map/pallas_call | solution.py:265
  28.4 16.4 %all_to_all.20 = bf16[64,16,128]{2,1,0:T(8,128)(2,1)S(1)} all-to-all(bf16[64,16,128]{2,1,0:T(8,128)(2,1)S(1)} %bitcast.19), channel_id=1, replica_groups={{214,6,8,14,16,22,24,30,32,38,40,46,48,54,56,62,64,70,72,78,80,86,88,94..., dimensions={0} | all-to-all | bytes 524288 | tf_op jit(solution)/shard_map/all_to_all | solution.py:31
  44.9 0.6 shard_map.115
  45.4 16.9 %all_to_all.21 = bf16[64,16,128]{2,1,0:T(8,128)(2,1)S(1)} all-to-all(bf16[64,16,128]{2,1,0:T(8,128)(2,1)S(1)} %bitcast.20), channel_id=1, replica_groups={{214,6,8,14,16,22,24,30,32,38,40,46,48,54,56,62,64,70,72,78,80,86,88,94..., dimensions={0} | all-to-all | bytes 524288 | tf_op jit(solution)/shard_map/all_to_all | solution.py:31
  62.3 1.4 %shard_map.116 = (bf16[1024,128]{1,0:T(8,128)(2,1)}, f32[576,128]{1,0:T(8,128)S(1)}, f32[576,128]{1,0:T(8,128)S(1)}) custom-call(bf16[1024,128]{1,0:T(8,128)(2,1)S(1)} %bitcast.16, bf16[448,128]{1,0:T(8,128)(2,1)S(1)} %copy-done.3, bf16[128,448]{1,0:T(8,128)(2,1)S(1)} %copy-done.2, f32[448,1024]{1,0:T(8,128)S(1)} %get-tuple-element.44.slope_ref, ...), custom_call_target="tpu_custom_call" | custom-call | flops 469762048 | bytes 4423680 | tf_op jit(solution)/shard_map/pallas_call | solution.py:265
  63.7 11.1 %all-to-all-start.3 = ((bf16[64,16,128]{2,1,0:T(8,128)(2,1)}), bf16[64,16,128]{2,1,0:T(8,128)(2,1)S(1)}, u32[]{:S(2)}, u32[]{:S(2)}) async-start(bf16[64,16,128]{2,1,0:T(8,128)(2,1)} %bitcast.24), calls=%async_computation.3 | async-start | bytes 524288 | tf_op jit(solution)/shard_map/all_to_all | solution.py:31
  74.8 4.2 %collective-permute-start.6 = (f32[576,128]{1,0:T(8,128)S(1)}, f32[576,128]{1,0:T(8,128)S(1)}, u32[]{:S(2)}, u32[]{:S(2)}) collective-permute-start(f32[576,128]{1,0:T(8,128)S(1)} %get-tuple-element.50), channel_id=1, source_target_pairs={{0,1},{1,0},{2,3},{3,2},{4,5},{5,4},{6,7},{7,6},{8,9},{9,8},{10,11... | collective-permute-start | bytes 884744 | tf_op jit(solution)/shard_map/ppermute | solution.py:26
  79.0 1.2 %collective-permute-done.6.got_ref = f32[576,128]{1,0:T(8,128)S(1)} collective-permute-done((f32[576,128]{1,0:T(8,128)S(1)}, f32[576,128]{1,0:T(8,128)S(1)}, u32[]{:S(2)}, u32[]{:S(2)}) %collective-permute-start.6) | collective-permute-done | bytes 294944 | tf_op jit(solution)/shard_map/ppermute | solution.py:26
  80.3 0.1 all-to-all-done.3
  80.4 0.3 shard_map.117
  80.8 3.3 %collective-permute-start.5 = (bf16[128,128]{1,0:T(8,128)(2,1)S(1)}, bf16[128,128]{1,0:T(8,128)(2,1)S(1)}, u32[]{:S(2)}, u32[]{:S(2)}) collective-permute-start(bf16[128,128]{1,0:T(8,128)(2,1)S(1)} %shard_map.117), channel_id=1, source_target_pairs={{0,3},{1,2},{2,1},{3,0},{4,7},{5,6},{6,5},{7,4},{8,11},{9,10},{10,... | collective-permute-start | bytes 98312 | tf_op jit(solution)/shard_map/ppermute | solution.py:26
  84.1 2.8 %collective-permute-start.4 = (bf16[128,128]{1,0:T(8,128)(2,1)S(1)}, bf16[128,128]{1,0:T(8,128)(2,1)S(1)}, u32[]{:S(2)}, u32[]{:S(2)}) collective-permute-start(bf16[128,128]{1,0:T(8,128)(2,1)S(1)} %shard_map.117), channel_id=1, source_target_pairs={{0,2},{1,3},{2,0},{3,1},{4,6},{5,7},{6,4},{7,5},{8,10},{9,11},{10,... | collective-permute-start | bytes 98312 | tf_op jit(solution)/shard_map/ppermute | solution.py:26
  86.9 0.8 shard_map.119
  87.7 1.2 %collective-permute-done.4 = bf16[128,128]{1,0:T(8,128)(2,1)S(1)} collective-permute-done((bf16[128,128]{1,0:T(8,128)(2,1)S(1)}, bf16[128,128]{1,0:T(8,128)(2,1)S(1)}, u32[]{:S(2)}, u32[]{:S(2)}) %collective-permute-start.4) | collective-permute-done | bytes 32800 | tf_op jit(solution)/shard_map/ppermute | solution.py:26
  88.9 0.6 add_bitcast_fusion
  (24 shorter events, 0.3 us)
Async XLA Ops:
  0.6 19.7 %copy-start = (bf16[4096,128]{1,0:T(8,128)(2,1)S(1)}, bf16[4096,128]{1,0:T(8,128)(2,1)}, u32[]{:S(2)}) copy-start(bf16[4096,128]{1,0:T(8,128)(2,1)} %param.9) | copy-start | bytes 3145732
  2.9 20.7 %copy-start.4 = (bf16[224,128]{1,0:T(8,128)(2,1)S(1)}, bf16[224,128]{1,0:T(8,128)(2,1)}, u32[]{:S(2)}) copy-start(bf16[224,128]{1,0:T(8,128)(2,1)} %get-tuple-element.35.own_ref) | copy-start | bytes 172036
  2.9 23.4 %copy-start.6 = (s32[128]{0:T(128)S(1)}, s32[128]{0:T(128)}, u32[]{:S(2)}) copy-start(s32[128]{0:T(128)} %param.11) | copy-start | bytes 1540
  2.9 24.3 %all-to-all-start = ((bf16[64,16,128]{2,1,0:T(8,128)(2,1)}), bf16[64,16,128]{2,1,0:T(8,128)(2,1)S(1)}, u32[]{:S(2)}, u32[]{:S(2)}) async-start(bf16[64,16,128]{2,1,0:T(8,128)(2,1)} %bitcast.23), calls=%async_computation | async-start | bytes 524288 | tf_op jit(solution)/shard_map/all_to_all | solution.py:31
  19.6 4.0 %collective-permute-start = (bf16[224,128]{1,0:T(8,128)(2,1)}, bf16[224,128]{1,0:T(8,128)(2,1)S(1)}, u32[]{:S(2)}, u32[]{:S(2)}) collective-permute-start(bf16[224,128]{1,0:T(8,128)(2,1)} %get-tuple-element.35.own_ref), channel_id=1, source_target_pairs={{0,2},{1,3},{2,0},{3,1},{4,6},{5,7},{6,4},{7,5},{8,10},{9,11},{10,... | collective-permute-start | bytes 172040 | tf_op jit(solution)/shard_map/ppermute | solution.py:26
  20.4 24.5 %copy-start.5 = (bf16[1,128,128]{2,1,0:T(8,128)(2,1)S(1)}, bf16[1,128,128]{2,1,0:T(8,128)(2,1)}, u32[]{:S(2)}) copy-start(bf16[1,128,128]{2,1,0:T(8,128)(2,1)} %last_ref.1) | copy-start | bytes 98308
  23.6 2.3 %collective-permute-start.1 = (bf16[224,128]{1,0:T(8,128)(2,1)S(1)}, bf16[224,128]{1,0:T(8,128)(2,1)S(1)}, u32[]{:S(2)}, u32[]{:S(2)}) collective-permute-start(bf16[224,128]{1,0:T(8,128)(2,1)S(1)} %copy-done.4), channel_id=1, source_target_pairs={{0,1},{1,0},{2,3},{3,2},{4,5},{5,4},{6,7},{7,6},{8,9},{9,8},{10,11... | collective-permute-start | bytes 172040 | tf_op jit(solution)/shard_map/ppermute | solution.py:26
  25.0 1.2 %collective-permute-start.2 = (bf16[224,128]{1,0:T(8,128)(2,1)S(1)}, bf16[224,128]{1,0:T(8,128)(2,1)S(1)}, u32[]{:S(2)}, u32[]{:S(2)}) collective-permute-start(bf16[224,128]{1,0:T(8,128)(2,1)S(1)} %collective-permute-done.far_ref), channel_id=1, source_target_pairs={{0,1},{1,0},{2,3},{3,2},{4,5},{5,4},{6,7},{7,6},{8,9},{9,8},{10,11... | collective-permute-start | bytes 172040 | tf_op jit(solution)/shard_map/ppermute | solution.py:26
  27.1 35.2 %copy-start.2 = (bf16[128,448]{1,0:T(8,128)(2,1)S(1)}, bf16[128,448]{1,0:T(8,128)(2,1)}, u32[]{:S(2)}) copy-start(bf16[128,448]{1,0:T(8,128)(2,1)} %get-tuple-element.43.up_t_ref) | copy-start | bytes 344068
  27.1 35.2 %copy-start.3 = (bf16[448,128]{1,0:T(8,128)(2,1)S(1)}, bf16[448,128]{1,0:T(8,128)(2,1)}, u32[]{:S(2)}) copy-start(bf16[448,128]{1,0:T(8,128)(2,1)} %get-tuple-element.42.down_ref) | copy-start | bytes 344068
  62.3 18.1 %copy-start.1 = (bf16[1024,128]{1,0:T(8,128)(2,1)S(1)}, bf16[1024,128]{1,0:T(8,128)(2,1)}, u32[]{:S(2)}) copy-start(bf16[1024,128]{1,0:T(8,128)(2,1)} %get-tuple-element.48.x_ref) | copy-start | bytes 786436
  63.7 16.7 %all-to-all-start.3 = ((bf16[64,16,128]{2,1,0:T(8,128)(2,1)}), bf16[64,16,128]{2,1,0:T(8,128)(2,1)S(1)}, u32[]{:S(2)}, u32[]{:S(2)}) async-start(bf16[64,16,128]{2,1,0:T(8,128)(2,1)} %bitcast.24), calls=%async_computation.3 | async-start | bytes 524288 | tf_op jit(solution)/shard_map/all_to_all | solution.py:31
  74.8 5.4 %collective-permute-start.6 = (f32[576,128]{1,0:T(8,128)S(1)}, f32[576,128]{1,0:T(8,128)S(1)}, u32[]{:S(2)}, u32[]{:S(2)}) collective-permute-start(f32[576,128]{1,0:T(8,128)S(1)} %get-tuple-element.50), channel_id=1, source_target_pairs={{0,1},{1,0},{2,3},{3,2},{4,5},{5,4},{6,7},{7,6},{8,9},{9,8},{10,11... | collective-permute-start | bytes 884744 | tf_op jit(solution)/shard_map/ppermute | solution.py:26
  80.2 6.7 %collective-permute-start.7 = (bf16[352,128]{1,0:T(8,128)(2,1)S(1)}, bf16[352,128]{1,0:T(8,128)(2,1)S(1)}, u32[]{:S(2)}, u32[]{:S(2)}) collective-permute-start(bf16[352,128]{1,0:T(8,128)(2,1)S(1)} %get-tuple-element.52), channel_id=1, source_target_pairs={{0,2},{1,3},{2,0},{3,1},{4,6},{5,7},{6,4},{7,5},{8,10},{9,11},{10,... | collective-permute-start | bytes 270344 | tf_op jit(solution)/shard_map/ppermute | solution.py:26
  80.8 7.0 %collective-permute-start.5 = (bf16[128,128]{1,0:T(8,128)(2,1)S(1)}, bf16[128,128]{1,0:T(8,128)(2,1)S(1)}, u32[]{:S(2)}, u32[]{:S(2)}) collective-permute-start(bf16[128,128]{1,0:T(8,128)(2,1)S(1)} %shard_map.117), channel_id=1, source_target_pairs={{0,3},{1,2},{2,1},{3,0},{4,7},{5,6},{6,5},{7,4},{8,11},{9,10},{10,... | collective-permute-start | bytes 98312 | tf_op jit(solution)/shard_map/ppermute | solution.py:26
  84.1 4.8 %collective-permute-start.4 = (bf16[128,128]{1,0:T(8,128)(2,1)S(1)}, bf16[128,128]{1,0:T(8,128)(2,1)S(1)}, u32[]{:S(2)}, u32[]{:S(2)}) collective-permute-start(bf16[128,128]{1,0:T(8,128)(2,1)S(1)} %shard_map.117), channel_id=1, source_target_pairs={{0,2},{1,3},{2,0},{3,1},{4,6},{5,7},{6,4},{7,5},{8,10},{9,11},{10,... | collective-permute-start | bytes 98312 | tf_op jit(solution)/shard_map/ppermute | solution.py:26
  86.9 2.0 %collective-permute-start.3 = (bf16[128,128]{1,0:T(8,128)(2,1)S(1)}, bf16[128,128]{1,0:T(8,128)(2,1)S(1)}, u32[]{:S(2)}, u32[]{:S(2)}) collective-permute-start(bf16[128,128]{1,0:T(8,128)(2,1)S(1)} %shard_map.117), channel_id=1, source_target_pairs={{0,1},{1,0},{2,3},{3,2},{4,5},{5,4},{6,7},{7,6},{8,9},{9,8},{10,11... | collective-permute-start | bytes 98312 | tf_op jit(solution)/shard_map/ppermute | solution.py:26

commit v10 on v9

--- a/solution.py
+++ b/solution.py
@@ -89,7 +89,7 @@
 
 
 def first_kernel(
-    x_hbm, first_hbm, up_hbm, down_hbm, order_hbm, out_hbm, packed_hbm, x_own_hbm, rows_hbm,
+    x_hbm, first_hbm, up_hbm, down_hbm, order_hbm, out_hbm, packed_hbm, rows_hbm,
     x, first, packed, rows, spread, buffer, sems,
 ):
     count = x.shape[0]
@@ -114,11 +114,19 @@
     copies = send_out(spread, buffer, out_hbm, sems, 5, 0)
     for copy in fetch[2:]:
         copy.wait()
-    for i, (source, target) in enumerate(((x, x_own_hbm), (packed, packed_hbm), (rows, rows_hbm))):
+    for i, (source, target) in enumerate(((packed, packed_hbm), (rows, rows_hbm))):
         copies.append(pltpu.make_async_copy(source, target, sems.at[7 + i]))
         copies[-1].start()
     for copy in copies:
         copy.wait()
+
+
+def own_rows_kernel(x_hbm, out_ref, sem):
+    count = out_ref.shape[0]
+    start = pl.multiple_of(own_quarter() * count, count)
+    copy = pltpu.make_async_copy(x_hbm.at[pl.ds(start, count)], out_ref, sem)
+    copy.start()
+    copy.wait()
 
 
 def unit_matrix():
@@ -290,13 +298,12 @@
     small = 2 * BS * BS * count
     two_sems = pltpu.SemaphoreType.DMA((2,))
 
-    first_out, weights, x_own, rows = call(
+    first_out, weights, rows = call(
         first_kernel,
         (inputs, first_factor, up_factor, down_factor, row_order.reshape(-1, LANES)),
         (
             pieces,
             shape((2 * quarter_units, BS), BF16),
-            shape((count, BS), BF16),
             shape((count // LANES, LANES), jnp.int32),
         ),
         [
@@ -306,11 +313,11 @@
             pltpu.VMEM((count // LANES, LANES), jnp.int32),
             spread,
             buffer,
-            pltpu.SemaphoreType.DMA((10,)),
+            pltpu.SemaphoreType.DMA((9,)),
         ],
         small,
         [HBM] * 5,
-        [HBM] * 4,
+        [HBM] * 3,
     )
     far = from_partner(weights, 2)
     arrived = exchange(first_out, 0)
@@ -365,9 +372,12 @@
 
     quarter_rows = shape((units // 2 + BS, BS), F32)
     sent_rows = shape((units // 2 + BS, BS), BF16)
-    mine, theirs = call(
-        chip_sum_kernel, (mine, from_partner(theirs, 1)), (quarter_rows, sent_rows), [], 0
-    )
+    got = from_partner(theirs, 1)
+    inputs, got = lax.optimization_barrier((inputs, got))
+    (x_own,) = call(
+        own_rows_kernel, (inputs,), (shape((count, BS), BF16),), [pltpu.SemaphoreType.DMA], 0, [HBM]
+    )
+    mine, theirs = call(chip_sum_kernel, (mine, got), (quarter_rows, sent_rows), [], 0)
     factor_grad = shape((1, quarter_units, BS), F32)
     grad_up, grad_down, grad_last = call(
         totals_kernel,

time: 90 us -> 89.9 us (level)
  Pallas kernels: 7.68 us -> 8.58 us
    pallas_call x9 -> x10, Pallas kernels: 7.68 us -> 8.58 us  [call(): pl.pallas_call(kernel, out_shape=outs, in_specs=in_specs or [VMEM] * len(...]
  transfers between devices with their start and end apart: 10 -> 10, of which waited for: 5 -> 4; matrix products, arithmetic and copies ran while one was open for 4% -> 4% of each run, Pallas kernels for 3% -> 4%
where the time goes in v10:
time: 89.9 us; the launch traced here: 89.5 us
  starting transfers between devices  38.8 us (43%)
  blocking collectives  33.4 us (37%)
  Pallas kernels  8.58 us (10%)
  waiting for transfers between devices  3.4 us (4%)
  local copies, waits for them, and re-layouts  3.24 us (4%)
  other arithmetic  1.34 us (1%)
    all_to_all x2, blocking collectives, exchange(): lax.all_to_all(pieces, ('blk', 'hid'), 0, 0, tiled=True, axis_index_group...  33.4 us
    all_to_all x2, starting transfers between devices, exchange(): lax.all_to_all(pieces, ('blk', 'hid'), 0, 0, tiled=True, axis_index_group...  27.7 us
    ppermute x8, starting transfers between devices, from_partner(): return lax.ppermute(value, 'hid', [(i, i ^ m) for i in range(N_HID)])  11 us
    pallas_call x10, Pallas kernels, call(): pl.pallas_call(kernel, out_shape=outs, in_specs=in_specs or [VMEM] * len(...  8.58 us
    ppermute x8, waiting for transfers between devices, from_partner(): return lax.ppermute(value, 'hid', [(i, i ^ m) for i in range(N_HID)])  3.4 us
    gather x1, local copies, waits for them, and re-layouts, local(): targets.at[rows.reshape(count)]  3.2 us
  transfers between devices with their start and end apart: 10, of which 4 were waited for; matrix products, arithmetic and copies ran while one was open for 4% of the time, Pallas kernels for 4%

profile of v10, /device:TPU:1, one launch (start us, length us, event | category | flops | bytes accessed | tf_op | source)
XLA Modules:
  0.0 89.5 jit_solution(6133865711081624323)
XLA Ops:
  0.6 2.1 %shard_map.111 = (bf16[1024,128]{1,0:T(8,128)(2,1)}, bf16[224,128]{1,0:T(8,128)(2,1)}, s32[8,128]{1,0:T(8,128)}) custom-call(bf16[4096,128]{1,0:T(8,128)(2,1)} %x_hbm.2, bf16[1,128,128]{2,1,0:T(8,128)(2,1)} %first_hbm.1, bf16[1,112,128]{2,1,0:T(8,128)(2,1)} %up_hbm.1, bf16[1,112,128]{2,1,0:T(8,128)(2,1)} %down_hbm.1, s32[32,128]{1,0:T(8,128)} %bitcast.25), custom_call_target="tpu_custom_call" | custom-call | flops 33554432 | bytes 1478656 | tf_op jit(solution)/shard_map/pallas_call | solution.py:273
  2.8 16.7 %all-to-all-start = ((bf16[64,16,128]{2,1,0:T(8,128)(2,1)}), bf16[64,16,128]{2,1,0:T(8,128)(2,1)S(1)}, u32[]{:S(2)}, u32[]{:S(2)}) async-start(bf16[64,16,128]{2,1,0:T(8,128)(2,1)} %bitcast.23), calls=%async_computation | async-start | bytes 524288 | tf_op jit(solution)/shard_map/all_to_all | solution.py:31
  19.6 0.7 bitcast_clamp_fusion
  20.3 3.2 %gather_fusion = bf16[1024,128]{1,0:T(8,128)(2,1)S(1)} fusion(bf16[4096,128]{1,0:T(8,128)(2,1)S(1)} %copy-done, s32[1024]{0:T(1024)S(1)} %bitcast_clamp_fusion), kind=kCustom, calls=%fused_computation | custom fusion | bytes 528384 | tf_op jit(solution)/shard_map/gather | solution.py:325
  23.5 1.4 %collective-permute-start.1 = (bf16[224,128]{1,0:T(8,128)(2,1)S(1)}, bf16[224,128]{1,0:T(8,128)(2,1)S(1)}, u32[]{:S(2)}, u32[]{:S(2)}) collective-permute-start(bf16[224,128]{1,0:T(8,128)(2,1)S(1)} %copy-done.3), channel_id=1, source_target_pairs={{0,1},{1,0},{2,3},{3,2},{4,5},{5,4},{6,7},{7,6},{8,9},{9,8},{10,11... | collective-permute-start | bytes 172040 | tf_op jit(solution)/shard_map/ppermute | solution.py:26
  24.9 0.2 shard_map.112.teacher_ref
  25.2 0.7 collective-permute-done.1.near_ref
  25.8 0.4 collective-permute-done.2.other_ref
  26.2 0.9 shard_map.113
  27.1 1.2 %shard_map.114 = (bf16[1024,128]{1,0:T(8,128)(2,1)S(1)}, f32[448,1024]{1,0:T(8,128)S(1)}, bf16[448,1024]{1,0:T(8,128)(2,1)S(1)}) custom-call(bf16[1024,128]{1,0:T(8,128)(2,1)S(1)} %bitcast.14, bf16[448,128]{1,0:T(8,128)(2,1)S(1)} %get-tuple-element.38.up_ref, bf16[128,448]{1,0:T(8,128)(2,1)S(1)} %get-tuple-element.39.down_t_ref), custom_call_target="tpu_custom_call" | custom-call | flops 234881024 | bytes 3506176 | tf_op jit(solution)/shard_map/pallas_call | solution.py:273
  28.3 16.4 %all_to_all.20 = bf16[64,16,128]{2,1,0:T(8,128)(2,1)S(1)} all-to-all(bf16[64,16,128]{2,1,0:T(8,128)(2,1)S(1)} %bitcast.19), channel_id=1, replica_groups={{214,6,8,14,16,22,24,30,32,38,40,46,48,54,56,62,64,70,72,78,80,86,88,94..., dimensions={0} | all-to-all | bytes 524288 | tf_op jit(solution)/shard_map/all_to_all | solution.py:31
  44.8 0.6 shard_map.115
  45.3 16.9 %all_to_all.21 = bf16[64,16,128]{2,1,0:T(8,128)(2,1)S(1)} all-to-all(bf16[64,16,128]{2,1,0:T(8,128)(2,1)S(1)} %bitcast.20), channel_id=1, replica_groups={{214,6,8,14,16,22,24,30,32,38,40,46,48,54,56,62,64,70,72,78,80,86,88,94..., dimensions={0} | all-to-all | bytes 524288 | tf_op jit(solution)/shard_map/all_to_all | solution.py:31
  62.3 1.4 %shard_map.116 = (bf16[1024,128]{1,0:T(8,128)(2,1)}, f32[576,128]{1,0:T(8,128)S(1)}, f32[576,128]{1,0:T(8,128)S(1)}) custom-call(bf16[1024,128]{1,0:T(8,128)(2,1)S(1)} %bitcast.16, bf16[448,128]{1,0:T(8,128)(2,1)S(1)} %copy-done.2, bf16[128,448]{1,0:T(8,128)(2,1)S(1)} %copy-done.1, f32[448,1024]{1,0:T(8,128)S(1)} %get-tuple-element.45.slope_ref, ...), custom_call_target="tpu_custom_call" | custom-call | flops 469762048 | bytes 4423680 | tf_op jit(solution)/shard_map/pallas_call | solution.py:273
  63.6 11.0 %all-to-all-start.3 = ((bf16[64,16,128]{2,1,0:T(8,128)(2,1)}), bf16[64,16,128]{2,1,0:T(8,128)(2,1)S(1)}, u32[]{:S(2)}, u32[]{:S(2)}) async-start(bf16[64,16,128]{2,1,0:T(8,128)(2,1)} %bitcast.24), calls=%async_computation.3 | async-start | bytes 524288 | tf_op jit(solution)/shard_map/all_to_all | solution.py:31
  74.7 4.2 %collective-permute-start.3 = (f32[576,128]{1,0:T(8,128)S(1)}, f32[576,128]{1,0:T(8,128)S(1)}, u32[]{:S(2)}, u32[]{:S(2)}) collective-permute-start(f32[576,128]{1,0:T(8,128)S(1)} %get-tuple-element.49), channel_id=1, source_target_pairs={{0,1},{1,0},{2,3},{3,2},{4,5},{5,4},{6,7},{7,6},{8,9},{9,8},{10,11... | collective-permute-start | bytes 884744 | tf_op jit(solution)/shard_map/ppermute | solution.py:26
  78.9 1.2 %collective-permute-done.3.got_ref = f32[576,128]{1,0:T(8,128)S(1)} collective-permute-done((f32[576,128]{1,0:T(8,128)S(1)}, f32[576,128]{1,0:T(8,128)S(1)}, u32[]{:S(2)}, u32[]{:S(2)}) %collective-permute-start.3) | collective-permute-done | bytes 294944 | tf_op jit(solution)/shard_map/ppermute | solution.py:26
  80.2 1.0 %shard_map.117.x_ref = bf16[1024,128]{1,0:T(8,128)(2,1)S(1)} custom-call(bf16[4096,128]{1,0:T(8,128)(2,1)} %x_hbm.2), custom_call_target="tpu_custom_call" | custom-call | bytes 1310720 | tf_op jit(solution)/shard_map/pallas_call | solution.py:273
  81.2 0.3 shard_map.118
  81.6 2.5 %collective-permute-start.6 = (bf16[128,128]{1,0:T(8,128)(2,1)S(1)}, bf16[128,128]{1,0:T(8,128)(2,1)S(1)}, u32[]{:S(2)}, u32[]{:S(2)}) collective-permute-start(bf16[128,128]{1,0:T(8,128)(2,1)S(1)} %shard_map.118), channel_id=1, source_target_pairs={{0,3},{1,2},{2,1},{3,0},{4,7},{5,6},{6,5},{7,4},{8,11},{9,10},{10,... | collective-permute-start | bytes 98312 | tf_op jit(solution)/shard_map/ppermute | solution.py:26
  84.0 2.8 %collective-permute-start.5 = (bf16[128,128]{1,0:T(8,128)(2,1)S(1)}, bf16[128,128]{1,0:T(8,128)(2,1)S(1)}, u32[]{:S(2)}, u32[]{:S(2)}) collective-permute-start(bf16[128,128]{1,0:T(8,128)(2,1)S(1)} %shard_map.118), channel_id=1, source_target_pairs={{0,2},{1,3},{2,0},{3,1},{4,6},{5,7},{6,4},{7,5},{8,10},{9,11},{10,... | collective-permute-start | bytes 98312 | tf_op jit(solution)/shard_map/ppermute | solution.py:26
  86.8 0.8 shard_map.120
  87.7 1.2 %collective-permute-done.5 = bf16[128,128]{1,0:T(8,128)(2,1)S(1)} collective-permute-done((bf16[128,128]{1,0:T(8,128)(2,1)S(1)}, bf16[128,128]{1,0:T(8,128)(2,1)S(1)}, u32[]{:S(2)}, u32[]{:S(2)}) %collective-permute-start.5) | collective-permute-done | bytes 32800 | tf_op jit(solution)/shard_map/ppermute | solution.py:26
  88.8 0.6 add_bitcast_fusion
  (23 shorter events, 0.3 us)
Async XLA Ops:
  0.6 19.6 %copy-start = (bf16[4096,128]{1,0:T(8,128)(2,1)S(1)}, bf16[4096,128]{1,0:T(8,128)(2,1)}, u32[]{:S(2)}) copy-start(bf16[4096,128]{1,0:T(8,128)(2,1)} %param.9) | copy-start | bytes 3145732
  2.8 20.7 %copy-start.3 = (bf16[224,128]{1,0:T(8,128)(2,1)S(1)}, bf16[224,128]{1,0:T(8,128)(2,1)}, u32[]{:S(2)}) copy-start(bf16[224,128]{1,0:T(8,128)(2,1)} %get-tuple-element.36.own_ref) | copy-start | bytes 172036
  2.8 23.4 %copy-start.5 = (s32[128]{0:T(128)S(1)}, s32[128]{0:T(128)}, u32[]{:S(2)}) copy-start(s32[128]{0:T(128)} %param.11) | copy-start | bytes 1540
  2.8 24.3 %all-to-all-start = ((bf16[64,16,128]{2,1,0:T(8,128)(2,1)}), bf16[64,16,128]{2,1,0:T(8,128)(2,1)S(1)}, u32[]{:S(2)}, u32[]{:S(2)}) async-start(bf16[64,16,128]{2,1,0:T(8,128)(2,1)} %bitcast.23), calls=%async_computation | async-start | bytes 524288 | tf_op jit(solution)/shard_map/all_to_all | solution.py:31
  19.5 4.0 %collective-permute-start = (bf16[224,128]{1,0:T(8,128)(2,1)}, bf16[224,128]{1,0:T(8,128)(2,1)S(1)}, u32[]{:S(2)}, u32[]{:S(2)}) collective-permute-start(bf16[224,128]{1,0:T(8,128)(2,1)} %get-tuple-element.36.own_ref), channel_id=1, source_target_pairs={{0,2},{1,3},{2,0},{3,1},{4,6},{5,7},{6,4},{7,5},{8,10},{9,11},{10,... | collective-permute-start | bytes 172040 | tf_op jit(solution)/shard_map/ppermute | solution.py:26
  20.3 24.5 %copy-start.4 = (bf16[1,128,128]{2,1,0:T(8,128)(2,1)S(1)}, bf16[1,128,128]{2,1,0:T(8,128)(2,1)}, u32[]{:S(2)}) copy-start(bf16[1,128,128]{2,1,0:T(8,128)(2,1)} %last_ref.1) | copy-start | bytes 98308
  23.5 2.3 %collective-permute-start.1 = (bf16[224,128]{1,0:T(8,128)(2,1)S(1)}, bf16[224,128]{1,0:T(8,128)(2,1)S(1)}, u32[]{:S(2)}, u32[]{:S(2)}) collective-permute-start(bf16[224,128]{1,0:T(8,128)(2,1)S(1)} %copy-done.3), channel_id=1, source_target_pairs={{0,1},{1,0},{2,3},{3,2},{4,5},{5,4},{6,7},{7,6},{8,9},{9,8},{10,11... | collective-permute-start | bytes 172040 | tf_op jit(solution)/shard_map/ppermute | solution.py:26
  24.9 1.2 %collective-permute-start.2 = (bf16[224,128]{1,0:T(8,128)(2,1)S(1)}, bf16[224,128]{1,0:T(8,128)(2,1)S(1)}, u32[]{:S(2)}, u32[]{:S(2)}) collective-permute-start(bf16[224,128]{1,0:T(8,128)(2,1)S(1)} %collective-permute-done.far_ref), channel_id=1, source_target_pairs={{0,1},{1,0},{2,3},{3,2},{4,5},{5,4},{6,7},{7,6},{8,9},{9,8},{10,11... | collective-permute-start | bytes 172040 | tf_op jit(solution)/shard_map/ppermute | solution.py:26
  27.0 35.2 %copy-start.1 = (bf16[128,448]{1,0:T(8,128)(2,1)S(1)}, bf16[128,448]{1,0:T(8,128)(2,1)}, u32[]{:S(2)}) copy-start(bf16[128,448]{1,0:T(8,128)(2,1)} %get-tuple-element.44.up_t_ref) | copy-start | bytes 344068
  27.1 35.2 %copy-start.2 = (bf16[448,128]{1,0:T(8,128)(2,1)S(1)}, bf16[448,128]{1,0:T(8,128)(2,1)}, u32[]{:S(2)}) copy-start(bf16[448,128]{1,0:T(8,128)(2,1)} %get-tuple-element.43.down_ref) | copy-start | bytes 344068
  63.6 17.6 %all-to-all-start.3 = ((bf16[64,16,128]{2,1,0:T(8,128)(2,1)}), bf16[64,16,128]{2,1,0:T(8,128)(2,1)S(1)}, u32[]{:S(2)}, u32[]{:S(2)}) async-start(bf16[64,16,128]{2,1,0:T(8,128)(2,1)} %bitcast.24), calls=%async_computation.3 | async-start | bytes 524288 | tf_op jit(solution)/shard_map/all_to_all | solution.py:31
  74.7 5.4 %collective-permute-start.3 = (f32[576,128]{1,0:T(8,128)S(1)}, f32[576,128]{1,0:T(8,128)S(1)}, u32[]{:S(2)}, u32[]{:S(2)}) collective-permute-start(f32[576,128]{1,0:T(8,128)S(1)} %get-tuple-element.49), channel_id=1, source_target_pairs={{0,1},{1,0},{2,3},{3,2},{4,5},{5,4},{6,7},{7,6},{8,9},{9,8},{10,11... | collective-permute-start | bytes 884744 | tf_op jit(solution)/shard_map/ppermute | solution.py:26
  80.1 6.7 %collective-permute-start.7 = (bf16[352,128]{1,0:T(8,128)(2,1)S(1)}, bf16[352,128]{1,0:T(8,128)(2,1)S(1)}, u32[]{:S(2)}, u32[]{:S(2)}) collective-permute-start(bf16[352,128]{1,0:T(8,128)(2,1)S(1)} %get-tuple-element.54), channel_id=1, source_target_pairs={{0,2},{1,3},{2,0},{3,1},{4,6},{5,7},{6,4},{7,5},{8,10},{9,11},{10,... | collective-permute-start | bytes 270344 | tf_op jit(solution)/shard_map/ppermute | solution.py:26
  81.6 6.1 %collective-permute-start.6 = (bf16[128,128]{1,0:T(8,128)(2,1)S(1)}, bf16[128,128]{1,0:T(8,128)(2,1)S(1)}, u32[]{:S(2)}, u32[]{:S(2)}) collective-permute-start(bf16[128,128]{1,0:T(8,128)(2,1)S(1)} %shard_map.118), channel_id=1, source_target_pairs={{0,3},{1,2},{2,1},{3,0},{4,7},{5,6},{6,5},{7,4},{8,11},{9,10},{10,... | collective-permute-start | bytes 98312 | tf_op jit(solution)/shard_map/ppermute | solution.py:26
  84.0 4.8 %collective-permute-start.5 = (bf16[128,128]{1,0:T(8,128)(2,1)S(1)}, bf16[128,128]{1,0:T(8,128)(2,1)S(1)}, u32[]{:S(2)}, u32[]{:S(2)}) collective-permute-start(bf16[128,128]{1,0:T(8,128)(2,1)S(1)} %shard_map.118), channel_id=1, source_target_pairs={{0,2},{1,3},{2,0},{3,1},{4,6},{5,7},{6,4},{7,5},{8,10},{9,11},{10,... | collective-permute-start | bytes 98312 | tf_op jit(solution)/shard_map/ppermute | solution.py:26
  86.8 2.0 %collective-permute-start.4 = (bf16[128,128]{1,0:T(8,128)(2,1)S(1)}, bf16[128,128]{1,0:T(8,128)(2,1)S(1)}, u32[]{:S(2)}, u32[]{:S(2)}) collective-permute-start(bf16[128,128]{1,0:T(8,128)(2,1)S(1)} %shard_map.118), channel_id=1, source_target_pairs={{0,1},{1,0},{2,3},{3,2},{4,5},{5,4},{6,7},{7,6},{8,9},{9,8},{10,11... | collective-permute-start | bytes 98312 | tf_op jit(solution)/shard_map/ppermute | solution.py:26
